TPU v7x, 32 devices: a whole 2x2x4 slice. The times are simulated.
32 devices in a mesh: rep: 2 (over y), dp: 4 (over z), tensor: 4 (over x, core).
Axes of the slice: x: 2, y: 2, z: 4, core: 2. Of those that a mesh axis runs over, the one named last changes fastest.
Arguments:
- tokens: bfloat16 [4096, 4096], P(('rep', 'dp', 'tensor')), parts along dimension 0, may hold values from -6 to 6
- grad_out: bfloat16 [4096, 14336], P(('rep', 'dp'), 'tensor'), parts along dimension 0, may hold values from -6 to 6
- frozen_weight: bfloat16 [4096, 14336], P('dp', 'tensor'), may hold values from -0.09375 to 0.09375
- adapter_down: bfloat16 [128, 16, 4096], P('rep', None, 'tensor'), parts along dimension 0, may hold values from -0.09375 to 0.09375
- adapter_up: bfloat16 [128, 16, 14336], P('rep', None, 'tensor'), parts along dimension 0, may hold values from -0.1875 to 0.1875
- tenant_ids: int32 [4096], P('rep'), parts along dimension 0, may hold values from 0 to 63, as said below
- tenant_token_counts: int32 [128], P('rep'), parts along dimension 0, may hold values from 0 to 512, as said below
- owner_map: int32 [64], replicated, may hold values from 0 to 3, as said below
Outputs:
- input_grad: bfloat16 [4096, 4096], P(('rep', 'dp', 'tensor')), parts along dimension 0
- grad_down: float32 [256, 16, 4096], P(('rep', 'dp'), None, 'tensor'), parts along dimension 0
- grad_up: float32 [256, 16, 14336], P(('rep', 'dp'), None, 'tensor'), parts along dimension 0
There are 2 independent parts, one for each index of `rep`. A program takes and returns all parts, laid end to end along the dimension named above; an argument that names none is the same for every part. Nothing has to cross between parts.
Inputs may be any that keep to these rules, and one draw needn't show every extreme that they name: `tenant_ids`: constant on aligned blocks of 128 rows; the 4 blocks of one data group name different tenants; some tenant has a block in every data group. `tenant_token_counts`: 128 times the number of blocks of tenant_ids that name the tenant. `owner_map`: no owner holds more than 32 adapters, and one holds exactly 32.
All inputs are finite; a program needn't handle non-finite values.
Results may differ from a plain program's by a relative error of at most 0.014.
Values may be sent and summed in bfloat16 or wider, within the bound.
No kernel may reach another device: no remote copies, remote signals or barrier semaphores. Data moves between devices by JAX's collectives and lax.ppermute only.
A program may use at most 192 MiB of HBM per device.

v0:
```python
import jax
import jax.numpy as jnp
from jax import lax
from jax.sharding import PartitionSpec as P

TILE = 128


adapter_scale = 2.0


def owner_slots(owner_map, slot_count):
    positions = jnp.arange(owner_map.shape[0])
    same_owner = owner_map[:, None] == owner_map[None, :]
    earlier = positions[:, None] > positions[None, :]
    owner_rank = jnp.sum((same_owner & earlier).astype(jnp.int32), axis=1)
    return owner_map * slot_count + owner_rank


def body(
    tokens,
    grad_out,
    frozen_weight,
    adapter_down,
    adapter_up,
    tenant_ids,
    tenant_token_counts,
    owner_map,
):
    dp_count = lax.axis_size("dp")
    group_index = lax.axis_index("dp")
    shard_index = lax.axis_index("tensor")
    rows_group, ff_shard = grad_out.shape
    width_shard = adapter_down.shape[2]
    adapter_count = adapter_down.shape[0]
    tile_count = rows_group // TILE
    slot_count = 2 * adapter_count // dp_count
    all_tenants = tenant_ids.reshape(-1, TILE)[:, 0]
    selected_slot = lax.dynamic_slice_in_dim(all_tenants, group_index * tile_count, tile_count)
    columns = lax.all_to_all(tokens, "tensor", split_axis=1, concat_axis=0, tiled=True)
    down_tile_list = adapter_down[selected_slot]
    up_tiles = adapter_up[selected_slot]
    x_tiles = columns.reshape(tile_count, TILE, width_shard)
    dy_tiles = grad_out.reshape(tile_count, TILE, ff_shard)
    middle_part = jnp.einsum(
        "krd,ktd->krt", down_tile_list, x_tiles, preferred_element_type=jnp.float32
    )
    backed_part = jnp.einsum("krf,ktf->krt", up_tiles, dy_tiles, preferred_element_type=jnp.float32)
    middle, backward_result = (
        lax.psum(middle_part.astype(jnp.bfloat16), "tensor").astype(jnp.float32),
        lax.psum(backed_part.astype(jnp.bfloat16), "tensor").astype(jnp.float32),
    )
    middle = middle.astype(jnp.bfloat16)
    backward_result = backward_result.astype(jnp.bfloat16)
    frozen_term = jnp.einsum(
        "tf,df->td",
        grad_out,
        lax.all_gather(frozen_weight, "dp", axis=0, tiled=True),
        preferred_element_type=jnp.float32,
    ).astype(jnp.bfloat16)
    adapter_input = adapter_scale * jnp.einsum(
        "gqx,gqj->gxj", backward_result, down_tile_list, preferred_element_type=jnp.float32
    ).reshape(rows_group, width_shard)
    gradient_terms = lax.optimization_barrier(frozen_term).astype(jnp.float32)
    start_column = shard_index * width_shard
    local_block = (
        lax.dynamic_slice_in_dim(gradient_terms, start_column, width_shard, 1) + adapter_input
    )
    gradient_terms = lax.dynamic_update_slice_in_dim(gradient_terms, local_block, start_column, 1)
    input_grad = lax.psum_scatter(
        gradient_terms.astype(jnp.bfloat16), "tensor", scatter_dimension=0, tiled=True
    )
    per_tile_scale = adapter_scale / tenant_token_counts[selected_slot].astype(jnp.float32)
    tile_up = (
        per_tile_scale[:, None, None]
        * jnp.einsum("krt,ktf->krf", middle, dy_tiles, preferred_element_type=jnp.float32)
    ).astype(jnp.bfloat16)
    tile_down = (
        per_tile_scale[:, None, None]
        * jnp.einsum("krt,ktd->krd", backward_result, x_tiles, preferred_element_type=jnp.float32)
    ).astype(jnp.bfloat16)
    slot_of = owner_slots(owner_map, slot_count)
    wanted = group_index * slot_count + jnp.arange(slot_count)
    onehot = (selected_slot[None, :] == jnp.arange(adapter_count)[:, None]).astype(jnp.bfloat16)
    dense_down = jnp.einsum("ak,krd->ard", onehot, tile_down, preferred_element_type=jnp.float32)
    dense_up = jnp.einsum("ak,krf->arf", onehot, tile_up, preferred_element_type=jnp.float32)
    summed_down, summed_up = (
        lax.psum(dense_down.astype(jnp.bfloat16), "dp").astype(jnp.float32),
        lax.psum(dense_up.astype(jnp.bfloat16), "dp").astype(jnp.float32),
    )
    pick_rows = (slot_of[None, :] == wanted[:, None]).astype(jnp.float32)
    grad_down = jnp.einsum("sa,ard->srd", pick_rows, summed_down, precision=lax.Precision.HIGHEST)
    grad_up = jnp.einsum("sa,arf->srf", pick_rows, summed_up, precision=lax.Precision.HIGHEST)
    return (input_grad, grad_down, grad_up)


def solution(mesh):
    placed = (
        P(("rep", "dp", "tensor"), None),
        P(("rep", "dp"), "tensor"),
        P("dp", "tensor"),
        P("rep", None, "tensor"),
        P("rep", None, "tensor"),
        P("rep"),
        P("rep"),
        P(),
    )
    return jax.shard_map(
        body,
        mesh=mesh,
        in_specs=placed,
        out_specs=(
            P(("rep", "dp", "tensor"), None),
            P(("rep", "dp"), None, "tensor"),
            P(("rep", "dp"), None, "tensor"),
        ),
        check_vma=False,
    )
```

profile of v0, /device:TPU:0, one launch (start us, length us, event | category | flops | bytes accessed | tf_op | source)
XLA Modules:
  0.0 885.4 jit_solution(1471680977733211768)
XLA Ops:
  7.2 0.0 all-gather.2.cloned.1.call-start
  7.2 0.7 all-gather.2.cloned.1.call-update
  7.9 1.6 copy.25
  9.6 1.3 copy.26
  10.9 4.2 all-to-all-start
  15.1 0.8 dynamic-slice_reduce_fusion
  15.9 4.6 gather_fusion
  20.6 0.6 gather_fusion.1
  21.1 0.6 gather_fusion.2
  21.8 4.5 convolution_convert_fusion.4
  26.3 3.2 all-to-all-done
  29.5 0.4 convolution_convert_fusion.3
  29.9 11.1 %all-reduce = (bf16[4,16,128]{2,1,0:T(8,128)(2,1)S(1)}, bf16[4,16,128]{2,1,0:T(8,128)(2,1)S(1)}) all-reduce(bf16[4,16,128]{2,1,0:T(8,128)(2,1)S(1)} %convolution_convert_fusion.4, bf16[4,16,128]{2,1,0:T(8,128)(2,1)S(1)} %convolution_convert_fusion.3), channel_id=1, replica_groups=mesh['rep'=2,'dp'=4,'tensor'=4] {'tensor'}, use_global_device_ids=true, to_apply=%region_0.0 | all-reduce | flops 16384 | bytes 65536 | tf_op jit(solution)/shard_map/psum | solution.py:51
  41.0 0.3 fusion.1
  41.3 2.2 convolution_convert_fusion.2
  43.4 2.6 fusion
  46.1 5.2 convolution_convert_fusion
  51.3 0.2 reduce-scatter.2.cloned.1.call-start
  51.6 0.5 convolution_multiply_fusion.1
  52.0 453.4 %all-gather.2.cloned.1.call-done = bf16[4096,3584]{1,0:T(8,128)(2,1)} async-done(((bf16[1024,3584]{1,0:T(8,128)(2,1)}), bf16[4096,3584]{1,0:T(8,128)(2,1)}) %all-gather.2.cloned.1.call-update) | async-done | bytes 29360144 | tf_op jit(solution)/shard_map/all_gather | solution.py:58
  505.5 20.1 %convolution_convert_fusion.1 = bf16[512,4096]{1,0:T(8,128)(2,1)S(1)} fusion(bf16[512,3584]{1,0:T(8,128)(2,1)} %param.9, bf16[4096,3584]{1,0:T(8,128)(2,1)} %all-gather.2.cloned.1.call-done), kind=kOutput, calls=%fused_computation.4 | convolution fusion | flops 15034482688 | bytes 37224448 | tf_op jit(solution)/shard_map/tf,df->td/dot_general | solution.py:55
  525.6 1.1 convert_element_type.46
  526.7 0.5 constant_dynamic-update-slice_fusion
  527.2 2.6 convert_element_type.48
  529.8 0.6 copy-done.4
  530.4 0.2 convert_reduce_fusion
  530.6 301.6 %all-reduce.4.cloned.1.call-done = (bf16[64,16,1024]{2,0,1:T(8,128)(2,1)}, bf16[64,16,3584]{2,0,1:T(8,128)(2,1)}) async-done(((bf16[64,16,1024]{2,0,1:T(8,128)(2,1)}, bf16[64,16,3584]{2,0,1:T(8,128)(2,1)}), (bf16[64,16,1024]{2,0,1:T(8,128)(2,1)}, bf16[64,16,3584]{2,0,1:T(8,128)(2,1)})) %all-reduce.4.cloned.1.call-update) | async-done | bytes 9437200 | tf_op jit(solution)/shard_map/psum | solution.py:88
  832.2 2.2 fusion.9
  834.4 2.5 copy.29
  837.0 1.2 fusion.7
  838.2 7.5 copy.30
  845.7 33.2 %reduce-scatter.2.cloned.1.call-done = bf16[128,4096]{1,0:T(8,128)(2,1)} async-done(((bf16[512,4096]{1,0:T(8,128)(2,1)}), bf16[128,4096]{1,0:T(8,128)(2,1)}) %reduce-scatter.2.cloned.1.call-update) | async-done | bytes 1048592 | tf_op jit(solution)/shard_map/reduce_scatter | solution.py:70
  (16 shorter events, 0.1 us)
Async XLA Ops:
  7.2 13.4 %copy-start = (bf16[64,16,1024]{2,1,0:T(8,128)(2,1)S(1)}, bf16[64,16,1024]{2,1,0:T(8,128)(2,1)}, u32[]{:S(2)}) copy-start(bf16[64,16,1024]{2,1,0:T(8,128)(2,1)} %param.11) | copy-start | bytes 6291460
  7.2 498.3 %all-gather.2.cloned.1.call-start = ((), (), s32[]{:S(2)}) async-start(), calls=%async_computation.2 | async-start | bytes 36700160 | tf_op jit(solution)/shard_map/all_gather | solution.py:58
  7.9 13.2 %copy-start.2 = (s32[64]{0:T(128)S(1)}, s32[64]{0:T(128)}, u32[]{:S(2)}) copy-start(s32[64]{0:T(128)} %param.14) | copy-start | bytes 772
  10.9 18.7 %all-to-all-start = ((bf16[128,4,1024]{2,0,1:T(8,128)(2,1)}), bf16[128,4,1024]{2,0,1:T(8,128)(2,1)S(1)}, u32[]{:S(2)}, u32[]{:S(2)}) async-start(bf16[128,4,1024]{2,0,1:T(8,128)(2,1)} %copy.26), calls=%async_computation.1 | async-start | bytes 2097152 | tf_op jit(solution)/shard_map/all_to_all | solution.py:40
  15.1 817.1 %all-reduce.4.cloned.1.call-start = ((), (), s32[]{:S(2)}) async-start(), calls=%async_computation.4 | async-start | bytes 18874368 | tf_op jit(solution)/shard_map/psum | solution.py:88
  51.3 827.5 %reduce-scatter.2.cloned.1.call-start = ((), (), s32[]{:S(2)}) async-start(), calls=%async_computation.3 | async-start | bytes 5242880 | tf_op jit(solution)/shard_map/reduce_scatter | solution.py:70
  529.8 0.7 copy-start.4
  832.2 4.8 copy-start.3
  838.2 40.7 %copy-start.1 = (bf16[64,16,1024]{2,1,0:T(8,128)(2,1)S(1)}, bf16[64,16,1024]{2,1,0:T(8,128)(2,1)}, u32[]{:S(2)}) copy-start(bf16[64,16,1024]{2,1,0:T(8,128)(2,1)} %param.11) | copy-start | bytes 6291460
Sparse Core Ops, SparseCore 0:
  9.6 495.8 all-gather.1
  508.6 323.5 all-reduce.3
  835.3 43.4 reduce-scatter.1
where the time goes:
time: 886 us; the launch traced here: 885 us
  waiting for transfers between devices  792 us (89%)
  matrix products  39.2 us (4%)
  local copies, waits for them, and re-layouts  19.4 us (2%)
  between operations  13.9 us (2%)
  blocking collectives  11.1 us (1%)
    all_gather x1, waiting for transfers between devices, body(): lax.all_gather(frozen_weight, 'dp', axis=0, tiled=True)  453 us
    psum x1, waiting for transfers between devices, body(): lax.psum(dense_down.astype(jnp.bfloat16), 'dp').astype(jnp.float32)  302 us
    reduce_scatter x1, waiting for transfers between devices, body(): lax.psum_scatter(gradient_terms.astype(jnp.bfloat16), 'tensor', scatter_d...  33.2 us
    dot_general x1, matrix products, body(): jnp.einsum('tf,df->td', grad_out, lax.all_gather(frozen_weight, 'dp', axi...  20.1 us
  transfers between devices with their start and end apart: 4, of which 4 were waited for; matrix products, arithmetic and copies ran while one was open for 7% of the time, Pallas kernels for 0%

commit v1 on v0

v1 whole, which is shorter than its diff:
```python
import jax
import jax.numpy as jnp
from jax import lax
from jax.experimental import pallas as pl
from jax.experimental.pallas import tpu as pltpu
from jax.sharding import PartitionSpec as P

TILE = 128


adapter_scale = 2.0


def owner_slots(owner_map, slot_count):
    positions = jnp.arange(owner_map.shape[0])
    same_owner = owner_map[:, None] == owner_map[None, :]
    earlier = positions[:, None] > positions[None, :]
    owner_rank = jnp.sum((same_owner & earlier).astype(jnp.int32), axis=1)
    return owner_map * slot_count + owner_rank


def dot_last(a, b):
    return lax.dot_general(a, b, (((1,), (1,)), ((), ())), preferred_element_type=jnp.float32)


def place_kernel(slots_ref, tiles_ref, up_ref, down_ref):
    per_step = up_ref.shape[0]
    ff_shard = up_ref.shape[2]
    first = pl.program_id(0) * per_step
    up_ref[...] = jnp.zeros_like(up_ref)
    down_ref[...] = jnp.zeros_like(down_ref)

    def add_tile(k, carry):
        local = slots_ref[k] - first

        @pl.when((local >= 0) & (local < per_step))
        def _():
            up_ref[local] += tiles_ref[k, :, :ff_shard].astype(jnp.float32)
            down_ref[local] += tiles_ref[k, :, ff_shard:].astype(jnp.float32)

        return carry

    lax.fori_loop(0, tiles_ref.shape[0], add_tile, 0)


def place_in_slots(tiles, slots, slot_count, ff_shard):
    tile_count, rank, columns = tiles.shape
    per_step = min(4, slot_count)
    return pl.pallas_call(
        place_kernel,
        grid_spec=pltpu.PrefetchScalarGridSpec(
            num_scalar_prefetch=1,
            grid=(slot_count // per_step,),
            in_specs=[pl.BlockSpec((tile_count, rank, columns), lambda i, s: (0, 0, 0))],
            out_specs=[
                pl.BlockSpec((per_step, rank, ff_shard), lambda i, s: (i, 0, 0)),
                pl.BlockSpec((per_step, rank, columns - ff_shard), lambda i, s: (i, 0, 0)),
            ],
        ),
        out_shape=[
            jax.ShapeDtypeStruct((slot_count, rank, ff_shard), jnp.float32),
            jax.ShapeDtypeStruct((slot_count, rank, columns - ff_shard), jnp.float32),
        ],
        compiler_params=pltpu.CompilerParams(vmem_limit_bytes=32 * 1024 * 1024),
    )(slots, tiles)


def adapter_parts(tokens, grad_out, adapter_down, adapter_up, tenants, counts):
    tile_count = tenants.shape[0]
    shard_index = lax.axis_index("tensor")
    down_sel = adapter_down[tenants]
    up_sel = adapter_up[tenants]
    dy_tiles = grad_out.reshape(tile_count, TILE, -1)
    own_down = lax.all_to_all(down_sel, "tensor", split_axis=0, concat_axis=2, tiled=True)[0]
    middle = dot_last(own_down, tokens).astype(jnp.bfloat16)
    backed_part = jnp.einsum(
        "krf,ktf->krt", up_sel, dy_tiles, preferred_element_type=jnp.float32
    ).astype(jnp.bfloat16)
    sent = jnp.concatenate([backed_part, jnp.broadcast_to(middle, backed_part.shape)], axis=1)
    got = lax.all_to_all(sent, "tensor", split_axis=0, concat_axis=0, tiled=True)
    rank = middle.shape[0]
    backed = jnp.sum(got[:, :rank].astype(jnp.float32), axis=0).astype(jnp.bfloat16)
    middle_all = got[:, rank:]
    scale = adapter_scale / counts[tenants].astype(jnp.float32)
    tile_up = (
        scale[:, None, None]
        * jnp.einsum("krt,ktf->krf", middle_all, dy_tiles, preferred_element_type=jnp.float32)
    ).astype(jnp.bfloat16)
    own_tile_down = (
        scale[shard_index] * jnp.dot(backed, tokens, preferred_element_type=jnp.float32)
    ).astype(jnp.bfloat16)
    tile_down = lax.all_to_all(own_tile_down, "tensor", split_axis=1, concat_axis=0, tiled=True)
    tile_down = tile_down.reshape(tile_count, rank, -1)
    return own_down, backed, jnp.concatenate([tile_up, tile_down], axis=2)


def sum_over_tensor(terms):
    index = lax.axis_index("tensor")
    chip, core = index // 2, index % 2
    rows = terms.shape[-2] // 4
    split = terms.reshape(terms.shape[:-2] + (2, 2, rows, terms.shape[-1]))
    axis = split.ndim - 3
    away = lax.dynamic_index_in_dim(split, 1 - core, axis, keepdims=False)
    home = lax.dynamic_index_in_dim(split, core, axis, keepdims=False)
    got = lax.ppermute(away, "tensor", [(0, 1), (1, 0), (2, 3), (3, 2)])
    pair = (home.astype(jnp.float32) + got.astype(jnp.float32)).astype(jnp.bfloat16)
    axis = pair.ndim - 3
    away = lax.dynamic_index_in_dim(pair, 1 - chip, axis, keepdims=False)
    home = lax.dynamic_index_in_dim(pair, chip, axis, keepdims=False)
    got = lax.ppermute(away, "tensor", [(0, 2), (2, 0), (1, 3), (3, 1)])
    return (home.astype(jnp.float32) + got.astype(jnp.float32)).astype(jnp.bfloat16)


def line_of_four(
    tokens,
    grad_out,
    frozen_weight,
    adapter_down,
    adapter_up,
    tenant_ids,
    tenant_token_counts,
    owner_map,
):
    z = lax.axis_index("dp")
    rep = lax.axis_index("rep")
    rows_group, ff_shard = grad_out.shape
    tile_count = rows_group // TILE
    adapter_count = adapter_down.shape[0]
    slot_count = 2 * adapter_count // 4
    partner = [(0, 1), (1, 0), (2, 3), (3, 2)]
    swap_rep = [(0, 1), (1, 0)]
    all_tenants = tenant_ids.reshape(-1, TILE)[:, 0]
    tenants = lax.dynamic_slice_in_dim(all_tenants, z * tile_count, tile_count)

    half = frozen_weight.shape[0] // 2
    n1, n2 = 2, 4

    def piece(k, n):
        return lax.dynamic_slice_in_dim(frozen_weight, rep * half + k * (half // n), half // n, 0)

    partner_dy = lax.ppermute(grad_out, "dp", partner)
    near = [lax.ppermute(piece(k, n1), "dp", [(1, 2), (2, 1)]) for k in range(n1)]
    far = []
    for k in range(n2):
        sent = piece(k, n2)
        if k < 2:
            sent, _ = lax.optimization_barrier((sent, partner_dy))
        else:
            sent, _ = lax.optimization_barrier((sent, far[k - 2]))
        far.append(lax.ppermute(sent, "dp", [(0, 2), (3, 1)]))

    own_down, backed, tile_grads = adapter_parts(
        tokens, grad_out, adapter_down, adapter_up, tenants, tenant_token_counts
    )

    own_block = sum_over_tensor(dot_last(grad_out, frozen_weight).astype(jnp.bfloat16))
    block_for_partner = sum_over_tensor(dot_last(partner_dy, frozen_weight).astype(jnp.bfloat16))
    partner_block = lax.ppermute(block_for_partner, "dp", partner)

    inner = (z == 1) | (z == 2)

    def across(pieces):
        low, high = [], []
        for mine in pieces:
            other = lax.ppermute(mine, "rep", swap_rep)
            terms = jnp.stack(
                [
                    jnp.concatenate(
                        [dot_last(dy, w).astype(jnp.bfloat16) for w in (mine, other)], axis=1
                    )
                    for dy in (grad_out, partner_dy)
                ]
            )
            summed = sum_over_tensor(terms)
            got = lax.ppermute(summed[1], "dp", [(1, 0), (2, 3)])
            block = jnp.where(inner, summed[0], got)
            n = mine.shape[0]
            low.append(jnp.where(rep == 0, block[:, :n], block[:, n:]))
            high.append(jnp.where(rep == 0, block[:, n:], block[:, :n]))
        return jnp.concatenate(low + high, axis=1)

    near_block = across(near)
    far_block = across(far)

    lora = adapter_scale * lax.dot_general(
        backed, own_down, (((0,), (0,)), ((), ())), preferred_element_type=jnp.float32
    )
    even = z % 2 == 0
    first = jnp.where(even, own_block, partner_block)
    second = jnp.where(even, partner_block, own_block)
    left = z < 2
    frozen = jnp.concatenate(
        [
            jnp.where(left, first, far_block),
            jnp.where(left, second, near_block),
            jnp.where(left, near_block, first),
            jnp.where(left, far_block, second),
        ],
        axis=1,
    )
    input_grad = (frozen.astype(jnp.float32) + lora).astype(jnp.bfloat16)

    all_grads = lax.all_gather(tile_grads, "dp", axis=0, tiled=True)
    slots = owner_slots(owner_map, slot_count)[all_tenants] - z * slot_count
    grad_up, grad_down = place_in_slots(all_grads, slots, slot_count, ff_shard)
    return input_grad, grad_down, grad_up


def any_line(
    tokens,
    grad_out,
    frozen_weight,
    adapter_down,
    adapter_up,
    tenant_ids,
    tenant_token_counts,
    owner_map,
):
    dp_count = lax.axis_size("dp")
    group_index = lax.axis_index("dp")
    shard_index = lax.axis_index("tensor")
    rows_group, ff_shard = grad_out.shape
    width_shard = adapter_down.shape[2]
    adapter_count = adapter_down.shape[0]
    tile_count = rows_group // TILE
    slot_count = 2 * adapter_count // dp_count
    all_tenants = tenant_ids.reshape(-1, TILE)[:, 0]
    tenants = lax.dynamic_slice_in_dim(all_tenants, group_index * tile_count, tile_count)
    columns = lax.all_to_all(tokens, "tensor", split_axis=1, concat_axis=0, tiled=True)
    down_sel = adapter_down[tenants]
    up_sel = adapter_up[tenants]
    x_tiles = columns.reshape(tile_count, TILE, width_shard)
    dy_tiles = grad_out.reshape(tile_count, TILE, ff_shard)
    middle_part = jnp.einsum("krd,ktd->krt", down_sel, x_tiles, preferred_element_type=jnp.float32)
    backed_part = jnp.einsum("krf,ktf->krt", up_sel, dy_tiles, preferred_element_type=jnp.float32)
    middle = lax.psum(middle_part.astype(jnp.bfloat16), "tensor")
    backed = lax.psum(backed_part.astype(jnp.bfloat16), "tensor")
    whole = lax.all_gather(frozen_weight, "dp", axis=0, tiled=True)
    frozen = dot_last(grad_out, whole).astype(jnp.bfloat16).astype(jnp.float32)
    lora = adapter_scale * jnp.einsum(
        "krt,krd->ktd", backed, down_sel, preferred_element_type=jnp.float32
    ).reshape(rows_group, width_shard)
    start = shard_index * width_shard
    block = lax.dynamic_slice_in_dim(frozen, start, width_shard, 1) + lora
    terms = lax.dynamic_update_slice_in_dim(frozen, block, start, 1).astype(jnp.bfloat16)
    input_grad = lax.psum_scatter(terms, "tensor", scatter_dimension=0, tiled=True)
    scale = (adapter_scale / tenant_token_counts[tenants].astype(jnp.float32))[:, None, None]
    tile_up = scale * jnp.einsum(
        "krt,ktf->krf", middle, dy_tiles, preferred_element_type=jnp.float32
    )
    tile_down = scale * jnp.einsum(
        "krt,ktd->krd", backed, x_tiles, preferred_element_type=jnp.float32
    )
    tile_grads = jnp.concatenate([tile_up, tile_down], axis=2).astype(jnp.bfloat16)
    all_grads = lax.all_gather(tile_grads, "dp", axis=0, tiled=True)
    slots = owner_slots(owner_map, slot_count)[all_tenants] - group_index * slot_count
    grad_up, grad_down = place_in_slots(all_grads, slots, slot_count, ff_shard)
    return input_grad, grad_down, grad_up


def solution(mesh):
    sizes = mesh.shape
    four = sizes["dp"] == 4 and sizes["tensor"] == 4 and sizes["rep"] == 2
    placed = (
        P(("rep", "dp", "tensor"), None),
        P(("rep", "dp"), "tensor"),
        P("dp", "tensor"),
        P("rep", None, "tensor"),
        P("rep", None, "tensor"),
        P("rep"),
        P("rep"),
        P(),
    )
    return jax.shard_map(
        line_of_four if four else any_line,
        mesh=mesh,
        in_specs=placed,
        out_specs=(
            P(("rep", "dp", "tensor"), None),
            P(("rep", "dp"), None, "tensor"),
            P(("rep", "dp"), None, "tensor"),
        ),
        check_vma=False,
    )
```

time: 886 us -> 392 us (0.44)
  waiting for transfers between devices: 792 us -> 131 us
  starting transfers between devices: 4.47 us -> 78.4 us
  matrix products: 39.2 us -> 113 us
  other arithmetic: 5.21 us -> 16.7 us
  blocking collectives: 11.1 us -> 0 us
  local copies, waits for them, and re-layouts: 19.4 us -> 28.8 us
    all_gather x1, waiting for transfers between devices: 453 us -> 0.01 us  [line_of_four(): all_grads = lax.all_gather(tile_grads, 'dp', axis=0, tiled=True)]
    psum x1 -> x0, waiting for transfers between devices: 302 us -> none  [body(): lax.psum(dense_down.astype(jnp.bfloat16), 'dp').astype(jnp.float32)]
    ppermute x0 -> x36, waiting for transfers between devices: none -> 128 us  [the longest x1 58.4 us: line_of_four(): partner_dy = lax.ppermute(grad_out, 'dp', partner)]
    dot_general x10 -> x31, matrix products: 39.2 us -> 113 us  [the longest x27 105 us: dot_last(): lax.dot_general(a, b, (((1,), (1,)), ((), ())), preferred_element_type=jn...]
    ppermute x0 -> x36, starting transfers between devices: none -> 68.3 us  [the longest x4 29.8 us: line_of_four(): far.append(lax.ppermute(sent, 'dp', [(0, 2), (3, 1)]))]
    reduce_scatter x1 -> x0, waiting for transfers between devices: 33.2 us -> none  [body(): lax.psum_scatter(gradient_terms.astype(jnp.bfloat16), 'tensor', scatter_d...]
    psum x1 -> x0, blocking collectives: 11.1 us -> none  [body(): lax.psum(backed_part.astype(jnp.bfloat16), 'tensor').astype(jnp.float32)]
  transfers between devices with their start and end apart: 4 -> 40, of which waited for: 4 -> 17; matrix products, arithmetic and copies ran while one was open for 7% -> 38% of each run, Pallas kernels for 0% -> 2%
where the time goes in v1:
time: 392 us; the launch traced here: 390 us
  waiting for transfers between devices  131 us (33%)
  matrix products  113 us (29%)
  starting transfers between devices  78.4 us (20%)
  local copies, waits for them, and re-layouts  28.8 us (7%)
  other arithmetic  16.7 us (4%)
  between operations  15.3 us (4%)
  Pallas kernels  6.27 us (2%)
    dot_general x27, matrix products, dot_last(): lax.dot_general(a, b, (((1,), (1,)), ((), ())), preferred_element_type=jn...  105 us
    ppermute x1, waiting for transfers between devices, line_of_four(): partner_dy = lax.ppermute(grad_out, 'dp', partner)  58.4 us
    ppermute x6, waiting for transfers between devices, across(): other = lax.ppermute(mine, 'rep', swap_rep)  31.4 us
    ppermute x4, starting transfers between devices, line_of_four(): far.append(lax.ppermute(sent, 'dp', [(0, 2), (3, 1)]))  29.8 us
    ppermute x8, waiting for transfers between devices, sum_over_tensor(): got = lax.ppermute(away, 'tensor', [(0, 2), (2, 0), (1, 3), (3, 1)])  23.7 us
    ppermute x6, waiting for transfers between devices, across(): got = lax.ppermute(summed[1], 'dp', [(1, 0), (2, 3)])  14.4 us
    ppermute x8, starting transfers between devices, sum_over_tensor(): got = lax.ppermute(away, 'tensor', [(0, 2), (2, 0), (1, 3), (3, 1)])  10.5 us
    dynamic_slice x2, local copies, waits for them, and re-layouts, piece(): lax.dynamic_slice_in_dim(frozen_weight, rep * half + k * (half // n), hal...  8.15 us
  transfers between devices with their start and end apart: 40, of which 17 were waited for; matrix products, arithmetic and copies ran while one was open for 38% of the time, Pallas kernels for 2%

profile of v1, /device:TPU:0, one launch (start us, length us, event | category | flops | bytes accessed | tf_op | source)
XLA Modules:
  0.0 390.1 jit_solution(3315985773372660376)
XLA Ops:
  7.2 4.3 %constant_dynamic-slice_fusion.2 = (bf16[256,3584]{1,0:T(8,128)(2,1)}, bf16[256,3584]{1,0:T(8,128)(2,1)}) fusion(bf16[1024,3584]{1,0:T(8,128)(2,1)} %param.10, s32[]{:T(128)S(6)} %select_n.240, s32[]{:T(128)S(6)} %select_n.246), kind=kLoop, calls=%fused_computation.212 | loop fusion | bytes 7340040 | tf_op jit(solution)/shard_map/dynamic_slice | solution.py:139
  13.4 4.6 %collective-permute-start.2 = (bf16[512,3584]{1,0:T(8,128)(2,1)}, bf16[512,3584]{1,0:T(8,128)(2,1)}, u32[]{:S(2)}, u32[]{:S(2)}) collective-permute-start(bf16[512,3584]{1,0:T(8,128)(2,1)} %param.9), channel_id=1, source_target_pairs={{0,4},{4,0},{8,12},{12,8},{1,5},{5,1},{9,13},{13,9},{2,6},{6,2},{1... | collective-permute-start | bytes 11010056 | tf_op jit(solution)/shard_map/ppermute | solution.py:141
  20.0 8.2 %convolution_convert_fusion.1 = bf16[512,1024]{1,0:T(8,128)(2,1)S(1)} fusion(bf16[512,3584]{1,0:T(8,128)(2,1)} %param.9, bf16[1024,3584]{1,0:T(8,128)(2,1)} %param.10), kind=kOutput, calls=%fused_computation.11 | convolution fusion | flops 3758620672 | bytes 12058624 | tf_op jit(solution)/shard_map/dot_general | solution.py:23
  34.7 3.9 constant_dynamic-slice_fusion.3
  38.6 3.7 gather_fusion
  69.1 4.1 %fusion.2 = bf16[512,256]{0,1:T(8,128)(2,1)S(1)} fusion(bf16[256,3584]{1,0:T(8,128)(2,1)} %collective-permute-done.26, bf16[512,3584]{1,0:T(8,128)(2,1)} %param.9), kind=kOutput, calls=%fused_computation.28 | convolution fusion | flops 939655168 | bytes 5767168 | tf_op jit(solution)/shard_map/dot_general | solution.py:23
  73.2 3.7 fusion.6
  77.0 58.4 %collective-permute-done.2 = bf16[512,3584]{1,0:T(8,128)(2,1)} collective-permute-done((bf16[512,3584]{1,0:T(8,128)(2,1)}, bf16[512,3584]{1,0:T(8,128)(2,1)}, u32[]{:S(2)}, u32[]{:S(2)}) %collective-permute-start.2) | collective-permute-done | bytes 3670048 | tf_op jit(solution)/shard_map/ppermute | solution.py:141
  135.3 3.7 fusion.4
  139.1 3.7 fusion.5
  143.7 3.7 fusion.3
  149.3 3.7 fusion.8
  153.1 3.7 fusion.9
  157.7 3.7 fusion.7
  165.2 25.6 %collective-permute-start.11 = (bf16[128,3584]{1,0:T(8,128)(2,1)}, bf16[128,3584]{1,0:T(8,128)(2,1)}, u32[]{:S(2)}, u32[]{:S(2)}) collective-permute-start(bf16[128,3584]{1,0:T(8,128)(2,1)} %get-tuple-element.10), channel_id=1, source_target_pairs={{0,8},{12,4},{1,9},{13,5},{2,10},{14,6},{3,11},{15,7},{16,24},{28,... | collective-permute-start | bytes 2752520 | tf_op jit(solution)/shard_map/ppermute | solution.py:150
  192.3 8.2 %convolution_convert_fusion = bf16[512,1024]{1,0:T(8,128)(2,1)S(1)} fusion(bf16[512,3584]{1,0:T(8,128)(2,1)} %collective-permute-done.2, bf16[1024,3584]{1,0:T(8,128)(2,1)} %param.10), kind=kOutput, calls=%fused_computation.10 | convolution fusion | flops 3758620672 | bytes 12058624 | tf_op jit(solution)/shard_map/dot_general | solution.py:23
  204.0 6.3 %shard_map.103 = (f32[32,16,3584]{2,1,0:T(8,128)}, f32[32,16,1024]{2,1,0:T(8,128)}) custom-call(s32[16]{0:T(128)S(1)} %broadcast_subtract_fusion.slots_ref, bf16[16,16,4608]{2,1,0:T(8,128)(2,1)S(1)} %copy-done.2), custom_call_target="tpu_custom_call" | custom-call | tf_op jit(solution)/shard_map/pallas_call | solution.py:49
  215.3 5.6 %collective-permute-done.29 = bf16[2,128,512]{2,1,0:T(8,128)(2,1)S(1)} collective-permute-done((bf16[2,128,512]{2,1,0:T(8,128)(2,1)S(1)}, bf16[2,128,512]{2,1,0:T(8,128)(2,1)S(1)}, u32[]{:S(2)}, u32[]{:S(2)}) %collective-permute-start.29) | collective-permute-done | bytes 262176 | tf_op jit(solution)/shard_map/ppermute | solution.py:110
  222.5 4.0 %collective-permute-done.34 = bf16[2,128,512]{2,1,0:T(8,128)(2,1)S(1)} collective-permute-done((bf16[2,128,512]{2,1,0:T(8,128)(2,1)S(1)}, bf16[2,128,512]{2,1,0:T(8,128)(2,1)S(1)}, u32[]{:S(2)}, u32[]{:S(2)}) %collective-permute-start.34) | collective-permute-done | bytes 262176 | tf_op jit(solution)/shard_map/ppermute | solution.py:110
  249.1 4.0 %fusion.12 = bf16[512,128]{0,1:T(8,128)(2,1)} fusion(bf16[128,3584]{1,0:T(8,128)(2,1)S(1)} %collective-permute-done.6, bf16[512,3584]{1,0:T(8,128)(2,1)} %collective-permute-done.2), kind=kOutput, calls=%fused_computation.54 | convolution fusion | flops 469827584 | bytes 4718592 | tf_op jit(solution)/shard_map/dot_general | solution.py:23
  253.1 4.0 %fusion.10 = bf16[512,128]{0,1:T(8,128)(2,1)} fusion(bf16[128,3584]{1,0:T(8,128)(2,1)S(1)} %collective-permute-done.6, bf16[512,3584]{1,0:T(8,128)(2,1)} %param.9), kind=kOutput, calls=%fused_computation.52 | convolution fusion | flops 469827584 | bytes 4718592 | tf_op jit(solution)/shard_map/dot_general | solution.py:23
  257.1 10.6 %collective-permute-done.12 = bf16[128,3584]{1,0:T(8,128)(2,1)S(1)} collective-permute-done((bf16[128,3584]{1,0:T(8,128)(2,1)}, bf16[128,3584]{1,0:T(8,128)(2,1)S(1)}, u32[]{:S(2)}, u32[]{:S(2)}) %collective-permute-start.12) | collective-permute-done | bytes 917536 | tf_op jit(solution)/shard_map/ppermute | solution.py:165
  272.8 3.6 fusion.15
  277.4 10.6 %collective-permute-done.7 = bf16[128,3584]{1,0:T(8,128)(2,1)} collective-permute-done((bf16[128,3584]{1,0:T(8,128)(2,1)S(1)}, bf16[128,3584]{1,0:T(8,128)(2,1)}, u32[]{:S(2)}, u32[]{:S(2)}) %collective-permute-start.7) | collective-permute-done | bytes 917536 | tf_op jit(solution)/shard_map/ppermute | solution.py:165
  296.5 4.0 %fusion.24 = bf16[512,128]{0,1:T(8,128)(2,1)} fusion(bf16[128,3584]{1,0:T(8,128)(2,1)S(1)} %collective-permute-done.21, bf16[512,3584]{1,0:T(8,128)(2,1)} %collective-permute-done.2), kind=kOutput, calls=%fused_computation.66 | convolution fusion | flops 469827584 | bytes 4718592 | tf_op jit(solution)/shard_map/dot_general | solution.py:23
  300.4 4.0 %fusion.22 = bf16[512,128]{0,1:T(8,128)(2,1)} fusion(bf16[128,3584]{1,0:T(8,128)(2,1)S(1)} %collective-permute-done.21, bf16[512,3584]{1,0:T(8,128)(2,1)} %param.9), kind=kOutput, calls=%fused_computation.64 | convolution fusion | flops 469827584 | bytes 4718592 | tf_op jit(solution)/shard_map/dot_general | solution.py:23
  309.3 4.0 %fusion.18 = bf16[512,128]{0,1:T(8,128)(2,1)} fusion(bf16[128,3584]{1,0:T(8,128)(2,1)S(1)} %collective-permute-done.16, bf16[512,3584]{1,0:T(8,128)(2,1)} %param.9), kind=kOutput, calls=%fused_computation.60 | convolution fusion | flops 469827584 | bytes 4718592 | tf_op jit(solution)/shard_map/dot_general | solution.py:23
  325.3 4.8 %collective-permute-done.10 = bf16[128,256]{1,0:T(8,128)(2,1)S(1)} collective-permute-done((bf16[128,256]{1,0:T(8,128)(2,1)S(1)}, bf16[128,256]{1,0:T(8,128)(2,1)S(1)}, u32[]{:S(2)}, u32[]{:S(2)}) %collective-permute-start.10) | collective-permute-done | bytes 65568 | tf_op jit(solution)/shard_map/ppermute | solution.py:175
  331.4 4.8 %collective-permute-done.15 = bf16[128,256]{1,0:T(8,128)(2,1)S(1)} collective-permute-done((bf16[128,256]{1,0:T(8,128)(2,1)S(1)}, bf16[128,256]{1,0:T(8,128)(2,1)S(1)}, u32[]{:S(2)}, u32[]{:S(2)}) %collective-permute-start.15) | collective-permute-done | bytes 65568 | tf_op jit(solution)/shard_map/ppermute | solution.py:175
  336.3 10.2 %collective-permute-done.17 = bf16[128,3584]{1,0:T(8,128)(2,1)S(1)} collective-permute-done((bf16[128,3584]{1,0:T(8,128)(2,1)S(1)}, bf16[128,3584]{1,0:T(8,128)(2,1)S(1)}, u32[]{:S(2)}, u32[]{:S(2)}) %collective-permute-start.17) | collective-permute-done | bytes 917536 | tf_op jit(solution)/shard_map/ppermute | solution.py:165
  351.0 3.6 fusion.19
  366.8 4.2 %collective-permute-done.19 = bf16[2,128,256]{2,1,0:T(8,128)(2,1)S(1)} collective-permute-done((bf16[2,128,256]{2,1,0:T(8,128)(2,1)S(1)}, bf16[2,128,256]{2,1,0:T(8,128)(2,1)S(1)}, u32[]{:S(2)}, u32[]{:S(2)}) %collective-permute-start.19) | collective-permute-done | bytes 131104 | tf_op jit(solution)/shard_map/ppermute | solution.py:110
  (246 shorter events, 139.6 us)
Async XLA Ops:
  11.5 50.8 %collective-permute-start.26 = (bf16[256,3584]{1,0:T(8,128)(2,1)}, bf16[256,3584]{1,0:T(8,128)(2,1)}, u32[]{:S(2)}, u32[]{:S(2)}) collective-permute-start(bf16[256,3584]{1,0:T(8,128)(2,1)} %get-tuple-element.17), channel_id=1, source_target_pairs={{4,8},{8,4},{5,9},{9,5},{6,10},{10,6},{7,11},{11,7},{20,24},{24,20... | collective-permute-start | bytes 5505032 | tf_op jit(solution)/shard_map/ppermute | solution.py:142
  13.4 121.9 %collective-permute-start.2 = (bf16[512,3584]{1,0:T(8,128)(2,1)}, bf16[512,3584]{1,0:T(8,128)(2,1)}, u32[]{:S(2)}, u32[]{:S(2)}) collective-permute-start(bf16[512,3584]{1,0:T(8,128)(2,1)} %param.9), channel_id=1, source_target_pairs={{0,4},{4,0},{8,12},{12,8},{1,5},{5,1},{9,13},{13,9},{2,6},{6,2},{1... | collective-permute-start | bytes 11010056 | tf_op jit(solution)/shard_map/ppermute | solution.py:141
  18.0 50.6 %collective-permute-start.31 = (bf16[256,3584]{1,0:T(8,128)(2,1)}, bf16[256,3584]{1,0:T(8,128)(2,1)}, u32[]{:S(2)}, u32[]{:S(2)}) collective-permute-start(bf16[256,3584]{1,0:T(8,128)(2,1)} %get-tuple-element.18), channel_id=1, source_target_pairs={{4,8},{8,4},{5,9},{9,5},{6,10},{10,6},{7,11},{11,7},{20,24},{24,20... | collective-permute-start | bytes 5505032 | tf_op jit(solution)/shard_map/ppermute | solution.py:142
  29.0 35.9 %collective-permute-start = (bf16[2,128,1024]{2,1,0:T(8,128)(2,1)}, bf16[2,128,1024]{2,1,0:T(8,128)(2,1)}, u32[]{:S(2)}, u32[]{:S(2)}) collective-permute-start(bf16[2,128,1024]{2,1,0:T(8,128)(2,1)} %dynamic-slice_bitcast_fusion.1), channel_id=1, source_target_pairs={{0,1},{1,0},{2,3},{3,2},{4,5},{5,4},{6,7},{7,6},{8,9},{9,8},{10,11... | collective-permute-start | bytes 1572872 | tf_op jit(solution)/shard_map/ppermute | solution.py:105
  30.5 15.6 %all-to-all-start = ((bf16[4,16,1024]{2,1,0:T(8,128)(2,1)}), bf16[4,16,1024]{2,1,0:T(8,128)(2,1)S(1)}, u32[]{:S(2)}, u32[]{:S(2)}) async-start(bf16[4,16,1024]{2,1,0:T(8,128)(2,1)} %gather_fusion.1), calls=%async_computation | async-start | bytes 262144 | tf_op jit(solution)/shard_map/all_to_all | solution.py:74
  47.3 7.2 %all-to-all-start.1 = ((bf16[4,32,128]{2,1,0:T(8,128)(2,1)}), bf16[4,32,128]{2,1,0:T(8,128)(2,1)S(1)}, u32[]{:S(2)}, u32[]{:S(2)}) async-start(bf16[4,32,128]{2,1,0:T(8,128)(2,1)} %pad_maximum_fusion.14), calls=%async_computation.1 | async-start | bytes 65536 | tf_op jit(solution)/shard_map/all_to_all | solution.py:80
  56.1 7.9 %all-to-all-start.2 = ((bf16[16,4,1024]{2,0,1:T(8,128)(2,1)}), bf16[16,4,1024]{2,0,1:T(8,128)(2,1)S(1)}, u32[]{:S(2)}, u32[]{:S(2)}) async-start(bf16[16,4,1024]{2,0,1:T(8,128)(2,1)} %bitcast.281), calls=%async_computation.2 | async-start | bytes 262144 | tf_op jit(solution)/shard_map/all_to_all | solution.py:92
  59.4 142.9 %all-gather.2.cloned.1.call-start = ((), (), s32[]{:S(2)}) async-start(), calls=%async_computation.3 | async-start | bytes 2949120 | tf_op jit(solution)/shard_map/all_gather | solution.py:203
  62.3 76.8 %collective-permute-start.27 = (bf16[256,3584]{1,0:T(8,128)(2,1)}, bf16[256,3584]{1,0:T(8,128)(2,1)}, u32[]{:S(2)}, u32[]{:S(2)}) collective-permute-start(bf16[256,3584]{1,0:T(8,128)(2,1)} %collective-permute-done.26), channel_id=1, source_target_pairs={{0,16},{16,0},{1,17},{17,1},{2,18},{18,2},{3,19},{19,3},{4,20},{20... | collective-permute-start | bytes 5505032 | tf_op jit(solution)/shard_map/ppermute | solution.py:165
  67.0 312.3 %collective-permute-start.1 = (bf16[128,1024]{1,0:T(8,128)(2,1)}, bf16[128,1024]{1,0:T(8,128)(2,1)}, u32[]{:S(2)}, u32[]{:S(2)}) collective-permute-start(bf16[128,1024]{1,0:T(8,128)(2,1)} %dynamic-slice_bitcast_fusion.5), channel_id=1, source_target_pairs={{0,2},{2,0},{1,3},{3,1},{4,6},{6,4},{5,7},{7,5},{8,10},{10,8},{9,1... | collective-permute-start | bytes 786440 | tf_op jit(solution)/shard_map/ppermute | solution.py:110
  68.6 84.4 %collective-permute-start.32 = (bf16[256,3584]{1,0:T(8,128)(2,1)}, bf16[256,3584]{1,0:T(8,128)(2,1)}, u32[]{:S(2)}, u32[]{:S(2)}) collective-permute-start(bf16[256,3584]{1,0:T(8,128)(2,1)} %collective-permute-done.31), channel_id=1, source_target_pairs={{0,16},{16,0},{1,17},{17,1},{2,18},{18,2},{3,19},{19,3},{4,20},{20... | collective-permute-start | bytes 5505032 | tf_op jit(solution)/shard_map/ppermute | solution.py:165
  149.3 60.9 %collective-permute-start.28 = (bf16[2,2,128,512]{3,2,0,1:T(8,128)(2,1)}, bf16[2,2,128,512]{3,2,0,1:T(8,128)(2,1)}, u32[]{:S(2)}, u32[]{:S(2)}) collective-permute-start(bf16[2,2,128,512]{3,2,0,1:T(8,128)(2,1)} %fusion.35), channel_id=1, source_target_pairs={{0,1},{1,0},{2,3},{3,2},{4,5},{5,4},{6,7},{7,6},{8,9},{9,8},{10,11... | collective-permute-start | bytes 1572872 | tf_op jit(solution)/shard_map/ppermute | solution.py:105
  164.7 47.0 %collective-permute-start.33 = (bf16[2,2,128,512]{3,2,0,1:T(8,128)(2,1)}, bf16[2,2,128,512]{3,2,0,1:T(8,128)(2,1)}, u32[]{:S(2)}, u32[]{:S(2)}) collective-permute-start(bf16[2,2,128,512]{3,2,0,1:T(8,128)(2,1)} %fusion.31), channel_id=1, source_target_pairs={{0,1},{1,0},{2,3},{3,2},{4,5},{5,4},{6,7},{7,6},{8,9},{9,8},{10,11... | collective-permute-start | bytes 1572872 | tf_op jit(solution)/shard_map/ppermute | solution.py:105
  165.2 68.4 %collective-permute-start.11 = (bf16[128,3584]{1,0:T(8,128)(2,1)}, bf16[128,3584]{1,0:T(8,128)(2,1)}, u32[]{:S(2)}, u32[]{:S(2)}) collective-permute-start(bf16[128,3584]{1,0:T(8,128)(2,1)} %get-tuple-element.10), channel_id=1, source_target_pairs={{0,8},{12,4},{1,9},{13,5},{2,10},{14,6},{3,11},{15,7},{16,24},{28,... | collective-permute-start | bytes 2752520 | tf_op jit(solution)/shard_map/ppermute | solution.py:150
  190.7 52.7 %collective-permute-start.6 = (bf16[128,3584]{1,0:T(8,128)(2,1)}, bf16[128,3584]{1,0:T(8,128)(2,1)S(1)}, u32[]{:S(2)}, u32[]{:S(2)}) collective-permute-start(bf16[128,3584]{1,0:T(8,128)(2,1)} %get-tuple-element.9), channel_id=1, source_target_pairs={{0,8},{12,4},{1,9},{13,5},{2,10},{14,6},{3,11},{15,7},{16,24},{28,... | collective-permute-start | bytes 2752520 | tf_op jit(solution)/shard_map/ppermute | solution.py:150
  211.7 9.2 %collective-permute-start.29 = (bf16[2,128,512]{2,1,0:T(8,128)(2,1)S(1)}, bf16[2,128,512]{2,1,0:T(8,128)(2,1)S(1)}, u32[]{:S(2)}, u32[]{:S(2)}) collective-permute-start(bf16[2,128,512]{2,1,0:T(8,128)(2,1)S(1)} %dynamic-slice_bitcast_fusion.3), channel_id=1, source_target_pairs={{0,2},{2,0},{1,3},{3,1},{4,6},{6,4},{5,7},{7,5},{8,10},{10,8},{9,1... | collective-permute-start | bytes 786440 | tf_op jit(solution)/shard_map/ppermute | solution.py:110
  214.5 12.0 %collective-permute-start.34 = (bf16[2,128,512]{2,1,0:T(8,128)(2,1)S(1)}, bf16[2,128,512]{2,1,0:T(8,128)(2,1)S(1)}, u32[]{:S(2)}, u32[]{:S(2)}) collective-permute-start(bf16[2,128,512]{2,1,0:T(8,128)(2,1)S(1)} %dynamic-slice_bitcast_fusion.2), channel_id=1, source_target_pairs={{0,2},{2,0},{1,3},{3,1},{4,6},{6,4},{5,7},{7,5},{8,10},{10,8},{9,1... | collective-permute-start | bytes 786440 | tf_op jit(solution)/shard_map/ppermute | solution.py:110
  220.9 10.6 %collective-permute-start.4 = (bf16[128,1024]{1,0:T(8,128)(2,1)S(1)}, bf16[128,1024]{1,0:T(8,128)(2,1)S(1)}, u32[]{:S(2)}, u32[]{:S(2)}) collective-permute-start(bf16[128,1024]{1,0:T(8,128)(2,1)S(1)} %dynamic-slice_bitcast_fusion.4), channel_id=1, source_target_pairs={{0,2},{2,0},{1,3},{3,1},{4,6},{6,4},{5,7},{7,5},{8,10},{10,8},{9,1... | collective-permute-start | bytes 786440 | tf_op jit(solution)/shard_map/ppermute | solution.py:110
  226.5 18.3 %collective-permute-start.30 = (bf16[128,512]{1,0:T(8,128)(2,1)S(1)}, bf16[128,512]{1,0:T(8,128)(2,1)S(1)}, u32[]{:S(2)}, u32[]{:S(2)}) collective-permute-start(bf16[128,512]{1,0:T(8,128)(2,1)S(1)} %slice_bitcast_fusion.2), channel_id=1, source_target_pairs={{4,0},{8,12},{5,1},{9,13},{6,2},{10,14},{7,3},{11,15},{20,16},{24,... | collective-permute-start | bytes 393224 | tf_op jit(solution)/shard_map/ppermute | solution.py:175
  231.5 14.7 %collective-permute-start.35 = (bf16[128,512]{1,0:T(8,128)(2,1)S(1)}, bf16[128,512]{1,0:T(8,128)(2,1)S(1)}, u32[]{:S(2)}, u32[]{:S(2)}) collective-permute-start(bf16[128,512]{1,0:T(8,128)(2,1)S(1)} %slice_bitcast_fusion), channel_id=1, source_target_pairs={{4,0},{8,12},{5,1},{9,13},{6,2},{10,14},{7,3},{11,15},{20,16},{24,... | collective-permute-start | bytes 393224 | tf_op jit(solution)/shard_map/ppermute | solution.py:175
  233.6 145.7 %collective-permute-start.5 = (bf16[128,1024]{1,0:T(8,128)(2,1)}, bf16[128,1024]{1,0:T(8,128)(2,1)}, u32[]{:S(2)}, u32[]{:S(2)}) collective-permute-start(bf16[128,1024]{1,0:T(8,128)(2,1)} %fusion.44), channel_id=1, source_target_pairs={{0,4},{4,0},{8,12},{12,8},{1,5},{5,1},{9,13},{13,9},{2,6},{6,2},{1... | collective-permute-start | bytes 786440 | tf_op jit(solution)/shard_map/ppermute | solution.py:158
  243.5 52.4 %collective-permute-start.21 = (bf16[128,3584]{1,0:T(8,128)(2,1)}, bf16[128,3584]{1,0:T(8,128)(2,1)S(1)}, u32[]{:S(2)}, u32[]{:S(2)}) collective-permute-start(bf16[128,3584]{1,0:T(8,128)(2,1)} %get-tuple-element.12), channel_id=1, source_target_pairs={{0,8},{12,4},{1,9},{13,5},{2,10},{14,6},{3,11},{15,7},{16,24},{28,... | collective-permute-start | bytes 2752520 | tf_op jit(solution)/shard_map/ppermute | solution.py:150
  244.8 59.6 %collective-permute-start.16 = (bf16[128,3584]{1,0:T(8,128)(2,1)}, bf16[128,3584]{1,0:T(8,128)(2,1)S(1)}, u32[]{:S(2)}, u32[]{:S(2)}) collective-permute-start(bf16[128,3584]{1,0:T(8,128)(2,1)} %get-tuple-element.11), channel_id=1, source_target_pairs={{0,8},{12,4},{1,9},{13,5},{2,10},{14,6},{3,11},{15,7},{16,24},{28,... | collective-permute-start | bytes 2752520 | tf_op jit(solution)/shard_map/ppermute | solution.py:150
  246.2 21.4 %collective-permute-start.12 = (bf16[128,3584]{1,0:T(8,128)(2,1)}, bf16[128,3584]{1,0:T(8,128)(2,1)S(1)}, u32[]{:S(2)}, u32[]{:S(2)}) collective-permute-start(bf16[128,3584]{1,0:T(8,128)(2,1)} %collective-permute-done.11), channel_id=1, source_target_pairs={{0,16},{16,0},{1,17},{17,1},{2,18},{18,2},{3,19},{19,3},{4,20},{20... | collective-permute-start | bytes 2752520 | tf_op jit(solution)/shard_map/ppermute | solution.py:165
  267.7 20.4 %collective-permute-start.7 = (bf16[128,3584]{1,0:T(8,128)(2,1)S(1)}, bf16[128,3584]{1,0:T(8,128)(2,1)}, u32[]{:S(2)}, u32[]{:S(2)}) collective-permute-start(bf16[128,3584]{1,0:T(8,128)(2,1)S(1)} %collective-permute-done.6), channel_id=1, source_target_pairs={{0,16},{16,0},{1,17},{17,1},{2,18},{18,2},{3,19},{19,3},{4,20},{20... | collective-permute-start | bytes 2752520 | tf_op jit(solution)/shard_map/ppermute | solution.py:165
  288.0 25.9 %collective-permute-start.13 = (bf16[2,2,128,256]{3,2,0,1:T(8,128)(2,1)}, bf16[2,2,128,256]{3,2,0,1:T(8,128)(2,1)}, u32[]{:S(2)}, u32[]{:S(2)}) collective-permute-start(bf16[2,2,128,256]{3,2,0,1:T(8,128)(2,1)} %fusion.55), channel_id=1, source_target_pairs={{0,1},{1,0},{2,3},{3,2},{4,5},{5,4},{6,7},{7,6},{8,9},{9,8},{10,11... | collective-permute-start | bytes 786440 | tf_op jit(solution)/shard_map/ppermute | solution.py:105
  295.9 17.4 %collective-permute-start.8 = (bf16[2,2,128,256]{3,2,0,1:T(8,128)(2,1)S(1)}, bf16[2,2,128,256]{3,2,0,1:T(8,128)(2,1)S(1)}, u32[]{:S(2)}, u32[]{:S(2)}) collective-permute-start(bf16[2,2,128,256]{3,2,0,1:T(8,128)(2,1)S(1)} %fusion.59), channel_id=1, source_target_pairs={{0,1},{1,0},{2,3},{3,2},{4,5},{5,4},{6,7},{7,6},{8,9},{9,8},{10,11... | collective-permute-start | bytes 786440 | tf_op jit(solution)/shard_map/ppermute | solution.py:105
  304.4 51.2 %collective-permute-start.22 = (bf16[128,3584]{1,0:T(8,128)(2,1)S(1)}, bf16[128,3584]{1,0:T(8,128)(2,1)S(1)}, u32[]{:S(2)}, u32[]{:S(2)}) collective-permute-start(bf16[128,3584]{1,0:T(8,128)(2,1)S(1)} %collective-permute-done.21), channel_id=1, source_target_pairs={{0,16},{16,0},{1,17},{17,1},{2,18},{18,2},{3,19},{19,3},{4,20},{20... | collective-permute-start | bytes 2752520 | tf_op jit(solution)/shard_map/ppermute | solution.py:165
  313.3 33.1 %collective-permute-start.17 = (bf16[128,3584]{1,0:T(8,128)(2,1)S(1)}, bf16[128,3584]{1,0:T(8,128)(2,1)S(1)}, u32[]{:S(2)}, u32[]{:S(2)}) collective-permute-start(bf16[128,3584]{1,0:T(8,128)(2,1)S(1)} %collective-permute-done.16), channel_id=1, source_target_pairs={{0,16},{16,0},{1,17},{17,1},{2,18},{18,2},{3,19},{19,3},{4,20},{20... | collective-permute-start | bytes 2752520 | tf_op jit(solution)/shard_map/ppermute | solution.py:165
  355.6 7.9 %collective-permute-start.18 = (bf16[2,2,128,256]{3,2,0,1:T(8,128)(2,1)}, bf16[2,2,128,256]{3,2,0,1:T(8,128)(2,1)}, u32[]{:S(2)}, u32[]{:S(2)}) collective-permute-start(bf16[2,2,128,256]{3,2,0,1:T(8,128)(2,1)} %fusion.51), channel_id=1, source_target_pairs={{0,1},{1,0},{2,3},{3,2},{4,5},{5,4},{6,7},{7,6},{8,9},{9,8},{10,11... | collective-permute-start | bytes 786440 | tf_op jit(solution)/shard_map/ppermute | solution.py:105
  366.2 6.7 %collective-permute-start.24 = (bf16[2,128,256]{2,1,0:T(8,128)(2,1)S(1)}, bf16[2,128,256]{2,1,0:T(8,128)(2,1)S(1)}, u32[]{:S(2)}, u32[]{:S(2)}) collective-permute-start(bf16[2,128,256]{2,1,0:T(8,128)(2,1)S(1)} %dynamic-slice_bitcast_fusion.6), channel_id=1, source_target_pairs={{0,2},{2,0},{1,3},{3,1},{4,6},{6,4},{5,7},{7,5},{8,10},{10,8},{9,1... | collective-permute-start | bytes 393224 | tf_op jit(solution)/shard_map/ppermute | solution.py:110
  371.1 6.8 %collective-permute-start.20 = (bf16[128,256]{1,0:T(8,128)(2,1)S(1)}, bf16[128,256]{1,0:T(8,128)(2,1)S(1)}, u32[]{:S(2)}, u32[]{:S(2)}) collective-permute-start(bf16[128,256]{1,0:T(8,128)(2,1)S(1)} %slice_bitcast_fusion.6), channel_id=1, source_target_pairs={{4,0},{8,12},{5,1},{9,13},{6,2},{10,14},{7,3},{11,15},{20,16},{24,... | collective-permute-start | bytes 196616 | tf_op jit(solution)/shard_map/ppermute | solution.py:175
  (34 other events, 315.9 us)
Sparse Core Ops, SparseCore 0:
  65.0 69.6 all-gather.1

commit v2 on v1

--- a/solution.py
+++ b/solution.py
@@ -23,35 +23,34 @@
     return lax.dot_general(a, b, (((1,), (1,)), ((), ())), preferred_element_type=jnp.float32)
 
 
-def place_kernel(slots_ref, tiles_ref, up_ref, down_ref):
+def place_kernel(slots_ref, *refs):
+    *tile_refs, up_ref, down_ref = refs
     per_step = up_ref.shape[0]
     ff_shard = up_ref.shape[2]
+    tiles_each = tile_refs[0].shape[0]
     first = pl.program_id(0) * per_step
     up_ref[...] = jnp.zeros_like(up_ref)
     down_ref[...] = jnp.zeros_like(down_ref)
-
-    def add_tile(k, carry):
-        local = slots_ref[k] - first
-
-        @pl.when((local >= 0) & (local < per_step))
-        def _():
-            up_ref[local] += tiles_ref[k, :, :ff_shard].astype(jnp.float32)
-            down_ref[local] += tiles_ref[k, :, ff_shard:].astype(jnp.float32)
-
-        return carry
-
-    lax.fori_loop(0, tiles_ref.shape[0], add_tile, 0)
-
-
-def place_in_slots(tiles, slots, slot_count, ff_shard):
-    tile_count, rank, columns = tiles.shape
+    for i, tiles_ref in enumerate(tile_refs):
+        for k in range(tiles_each):
+            local = slots_ref[i * tiles_each + k] - first
+
+            @pl.when((local >= 0) & (local < per_step))
+            def _(tiles_ref=tiles_ref, k=k, local=local):
+                up_ref[local] += tiles_ref[k, :, :ff_shard].astype(jnp.float32)
+                down_ref[local] += tiles_ref[k, :, ff_shard:].astype(jnp.float32)
+
+
+def place_in_slots(groups, slots, slot_count, ff_shard):
+    tile_count, rank, columns = groups[0].shape
     per_step = min(4, slot_count)
     return pl.pallas_call(
         place_kernel,
         grid_spec=pltpu.PrefetchScalarGridSpec(
             num_scalar_prefetch=1,
             grid=(slot_count // per_step,),
-            in_specs=[pl.BlockSpec((tile_count, rank, columns), lambda i, s: (0, 0, 0))],
+            in_specs=[pl.BlockSpec((tile_count, rank, columns), lambda i, s: (0, 0, 0))]
+            * len(groups),
             out_specs=[
                 pl.BlockSpec((per_step, rank, ff_shard), lambda i, s: (i, 0, 0)),
                 pl.BlockSpec((per_step, rank, columns - ff_shard), lambda i, s: (i, 0, 0)),
@@ -62,7 +61,67 @@
             jax.ShapeDtypeStruct((slot_count, rank, columns - ff_shard), jnp.float32),
         ],
         compiler_params=pltpu.CompilerParams(vmem_limit_bytes=32 * 1024 * 1024),
-    )(slots, tiles)
+    )(slots, *groups)
+
+
+def terms_kernel(place_ref, own_ref, partner_ref, *refs):
+    *weight_refs, away_ref, home_ref = refs
+    chip = place_ref[0]
+    depth = own_ref.shape[-1]
+
+    def products(dy_ref, out_ref):
+        dy = dy_ref[...].reshape(2 * TILE, depth)
+        column = 0
+        for weight_ref in weight_refs:
+            rows = weight_ref.shape[0]
+            step = min(rows, 512)
+            for start in range(0, rows, step):
+                part = dot_last(dy, weight_ref[start : start + step]).astype(jnp.bfloat16)
+                out_ref[1 - chip, 0, :, column : column + step] = part[:TILE]
+                out_ref[chip, 0, :, column : column + step] = part[TILE:]
+                column += step
+
+    for side, out_ref in ((0, away_ref), (1, home_ref)):
+        for group, dy_ref in ((0, own_ref), (1, partner_ref)):
+
+            @pl.when((pl.program_id(0) == side) & (pl.program_id(1) == group))
+            def _(dy_ref=dy_ref, out_ref=out_ref):
+                products(dy_ref, out_ref)
+
+
+def product_terms(dy, partner_dy, weights, place):
+    depth = dy.shape[1]
+    columns = sum(w.shape[0] for w in weights)
+    split = (2, 2, TILE, depth)
+    out = jax.ShapeDtypeStruct((2, 2, TILE, columns), jnp.bfloat16)
+
+    def rows_of(side, group, place):
+        return (0, jnp.where(side == 0, 1 - place[1], place[1]), 0, 0)
+
+    dy_spec = pl.BlockSpec((2, 1, TILE, depth), rows_of)
+    return pl.pallas_call(
+        terms_kernel,
+        grid_spec=pltpu.PrefetchScalarGridSpec(
+            num_scalar_prefetch=1,
+            grid=(2, 2),
+            in_specs=[dy_spec, dy_spec]
+            + [
+                pl.BlockSpec(w.shape, lambda s, g, p: (0, 0), pipeline_mode=pl.Buffered(1))
+                for w in weights
+            ],
+            out_specs=[
+                pl.BlockSpec(
+                    (2, 1, TILE, columns), lambda s, g, p: (0, jnp.where(s == 0, g, 1), 0, 0)
+                ),
+                pl.BlockSpec(
+                    (2, 1, TILE, columns), lambda s, g, p: (0, jnp.where(s == 0, 0, g), 0, 0)
+                ),
+            ],
+        ),
+        out_shape=[out, out],
+        compiler_params=pltpu.CompilerParams(vmem_limit_bytes=48 * 1024 * 1024),
+        cost_estimate=pl.CostEstimate(flops=1000, bytes_accessed=1000, transcendentals=0),
+    )(place, dy.reshape(split), partner_dy.reshape(split), *weights)
 
 
 def adapter_parts(tokens, grad_out, adapter_down, adapter_up, tenants, counts):
@@ -94,21 +153,17 @@
     return own_down, backed, jnp.concatenate([tile_up, tile_down], axis=2)
 
 
-def sum_over_tensor(terms):
-    index = lax.axis_index("tensor")
-    chip, core = index // 2, index % 2
-    rows = terms.shape[-2] // 4
-    split = terms.reshape(terms.shape[:-2] + (2, 2, rows, terms.shape[-1]))
-    axis = split.ndim - 3
-    away = lax.dynamic_index_in_dim(split, 1 - core, axis, keepdims=False)
-    home = lax.dynamic_index_in_dim(split, core, axis, keepdims=False)
+def sum_over_tensor(away, home):
     got = lax.ppermute(away, "tensor", [(0, 1), (1, 0), (2, 3), (3, 2)])
-    pair = (home.astype(jnp.float32) + got.astype(jnp.float32)).astype(jnp.bfloat16)
-    axis = pair.ndim - 3
-    away = lax.dynamic_index_in_dim(pair, 1 - chip, axis, keepdims=False)
-    home = lax.dynamic_index_in_dim(pair, chip, axis, keepdims=False)
-    got = lax.ppermute(away, "tensor", [(0, 2), (2, 0), (1, 3), (3, 1)])
-    return (home.astype(jnp.float32) + got.astype(jnp.float32)).astype(jnp.bfloat16)
+    pair = home.astype(jnp.float32) + got.astype(jnp.float32)
+    got = lax.ppermute(pair[0].astype(jnp.bfloat16), "tensor", [(0, 2), (2, 0), (1, 3), (3, 1)])
+    return pair[1] + got.astype(jnp.float32)
+
+
+PARTNER = [(0, 1), (1, 0), (2, 3), (3, 2)]
+MIDDLE = [(1, 2), (2, 1)]
+OUTER_TO_MIDDLE = [(0, 2), (3, 1)]
+OUTWARD = [(1, 0), (2, 3)]
 
 
 def line_of_four(
@@ -123,64 +178,63 @@
 ):
     z = lax.axis_index("dp")
     rep = lax.axis_index("rep")
+    shard = lax.axis_index("tensor")
+    place = jnp.stack([shard // 2, shard % 2]).astype(jnp.int32)
     rows_group, ff_shard = grad_out.shape
     tile_count = rows_group // TILE
     adapter_count = adapter_down.shape[0]
     slot_count = 2 * adapter_count // 4
-    partner = [(0, 1), (1, 0), (2, 3), (3, 2)]
-    swap_rep = [(0, 1), (1, 0)]
+    inner = (z == 1) | (z == 2)
     all_tenants = tenant_ids.reshape(-1, TILE)[:, 0]
     tenants = lax.dynamic_slice_in_dim(all_tenants, z * tile_count, tile_count)
 
-    half = frozen_weight.shape[0] // 2
-    n1, n2 = 2, 4
-
-    def piece(k, n):
-        return lax.dynamic_slice_in_dim(frozen_weight, rep * half + k * (half // n), half // n, 0)
-
-    partner_dy = lax.ppermute(grad_out, "dp", partner)
-    near = [lax.ppermute(piece(k, n1), "dp", [(1, 2), (2, 1)]) for k in range(n1)]
-    far = []
-    for k in range(n2):
-        sent = piece(k, n2)
-        if k < 2:
-            sent, _ = lax.optimization_barrier((sent, partner_dy))
-        else:
-            sent, _ = lax.optimization_barrier((sent, far[k - 2]))
-        far.append(lax.ppermute(sent, "dp", [(0, 2), (3, 1)]))
+    width = frozen_weight.shape[0]
+    half = width // 2
+    pieces = 4
+    rows = half // pieces
+
+    def piece(k):
+        return lax.dynamic_slice_in_dim(frozen_weight, rep * half + k * rows, rows, 0)
+
+    def swap_rep(w):
+        return lax.ppermute(w, "rep", [(0, 1), (1, 0)])
+
+    partner_dy = lax.ppermute(grad_out, "dp", PARTNER)
+    near = [lax.ppermute(piece(k), "dp", MIDDLE) for k in range(pieces)]
+    far = [lax.ppermute(piece(k), "dp", OUTER_TO_MIDDLE) for k in range(pieces)]
+    near_pairs = [(w, swap_rep(w)) for w in near]
+    far_pairs = [(w, swap_rep(w)) for w in far]
 
     own_down, backed, tile_grads = adapter_parts(
         tokens, grad_out, adapter_down, adapter_up, tenants, tenant_token_counts
     )
-
-    own_block = sum_over_tensor(dot_last(grad_out, frozen_weight).astype(jnp.bfloat16))
-    block_for_partner = sum_over_tensor(dot_last(partner_dy, frozen_weight).astype(jnp.bfloat16))
-    partner_block = lax.ppermute(block_for_partner, "dp", partner)
-
-    inner = (z == 1) | (z == 2)
-
-    def across(pieces):
-        low, high = [], []
-        for mine in pieces:
-            other = lax.ppermute(mine, "rep", swap_rep)
-            terms = jnp.stack(
-                [
-                    jnp.concatenate(
-                        [dot_last(dy, w).astype(jnp.bfloat16) for w in (mine, other)], axis=1
-                    )
-                    for dy in (grad_out, partner_dy)
-                ]
-            )
-            summed = sum_over_tensor(terms)
-            got = lax.ppermute(summed[1], "dp", [(1, 0), (2, 3)])
-            block = jnp.where(inner, summed[0], got)
-            n = mine.shape[0]
-            low.append(jnp.where(rep == 0, block[:, :n], block[:, n:]))
-            high.append(jnp.where(rep == 0, block[:, n:], block[:, :n]))
-        return jnp.concatenate(low + high, axis=1)
-
-    near_block = across(near)
-    far_block = across(far)
+    partner_grads = lax.ppermute(tile_grads, "dp", PARTNER)
+    near_grads = lax.ppermute(tile_grads, "dp", MIDDLE)
+    far_grads = lax.ppermute(partner_grads, "dp", MIDDLE)
+    near_grads_out = lax.ppermute(near_grads, "dp", OUTWARD)
+    far_grads_out = lax.ppermute(far_grads, "dp", OUTWARD)
+
+    first_weights = [frozen_weight] + [w for pair in near_pairs for w in pair]
+    summed = sum_over_tensor(*product_terms(grad_out, partner_dy, first_weights, place))
+    own_first = summed[0].astype(jnp.bfloat16)
+    got_first = lax.ppermute(summed[1].astype(jnp.bfloat16), "dp", PARTNER)
+    own_block, partner_block = own_first[:, :width], got_first[:, :width]
+
+    def in_order(columns):
+        pairs = columns.reshape(TILE, -1, 2, rows)
+        mine = pairs[:, :, 0].reshape(TILE, half)
+        other = pairs[:, :, 1].reshape(TILE, half)
+        return jnp.concatenate(
+            [jnp.where(rep == 0, mine, other), jnp.where(rep == 0, other, mine)], axis=1
+        )
+
+    near_block = in_order(jnp.where(inner, own_first[:, width:], got_first[:, width:]))
+    far_columns = []
+    for pair in far_pairs:
+        summed = sum_over_tensor(*product_terms(grad_out, partner_dy, pair, place))
+        got = lax.ppermute(summed[1].astype(jnp.bfloat16), "dp", OUTWARD)
+        far_columns.append(jnp.where(inner, summed[0].astype(jnp.bfloat16), got))
+    far_block = in_order(jnp.concatenate(far_columns, axis=1))
 
     lora = adapter_scale * lax.dot_general(
         backed, own_down, (((0,), (0,)), ((), ())), preferred_element_type=jnp.float32
@@ -200,9 +254,28 @@
     )
     input_grad = (frozen.astype(jnp.float32) + lora).astype(jnp.bfloat16)
 
-    all_grads = lax.all_gather(tile_grads, "dp", axis=0, tiled=True)
-    slots = owner_slots(owner_map, slot_count)[all_tenants] - z * slot_count
-    grad_up, grad_down = place_in_slots(all_grads, slots, slot_count, ff_shard)
+    partner_index = z + 1 - 2 * (z % 2)
+    near_index = jnp.where(z < 2, 2, 1)
+    far_index = jnp.where(z < 2, 3, 0)
+    tile_slots = owner_slots(owner_map, slot_count)[all_tenants].reshape(4, tile_count)
+    tile_slots = tile_slots - z * slot_count
+    nowhere = jnp.full((tile_count,), -1, jnp.int32)
+    slots = jnp.concatenate(
+        [
+            tile_slots[z],
+            tile_slots[partner_index],
+            jnp.where(inner, tile_slots[near_index], nowhere),
+            jnp.where(inner, tile_slots[far_index], nowhere),
+            jnp.where(inner, nowhere, tile_slots[near_index]),
+            jnp.where(inner, nowhere, tile_slots[far_index]),
+        ]
+    )
+    grad_up, grad_down = place_in_slots(
+        [tile_grads, partner_grads, near_grads, far_grads, near_grads_out, far_grads_out],
+        slots,
+        slot_count,
+        ff_shard,
+    )
     return input_grad, grad_down, grad_up
 
 
@@ -254,7 +327,7 @@
     tile_grads = jnp.concatenate([tile_up, tile_down], axis=2).astype(jnp.bfloat16)
     all_grads = lax.all_gather(tile_grads, "dp", axis=0, tiled=True)
     slots = owner_slots(owner_map, slot_count)[all_tenants] - group_index * slot_count
-    grad_up, grad_down = place_in_slots(all_grads, slots, slot_count, ff_shard)
+    grad_up, grad_down = place_in_slots([all_grads], slots, slot_count, ff_shard)
     return input_grad, grad_down, grad_up
 
 

time: 392 us -> 501 us (1.28); the launches traced: 390 us -> 491 us
  waiting for transfers between devices: 131 us -> 295 us
  matrix products: 113 us -> 8.5 us
  Pallas kernels: 6.27 us -> 70.1 us
  between operations: 15.3 us -> 1.76 us
  other arithmetic: 16.7 us -> 3.93 us
    ppermute x28 -> x32, waiting for transfers between devices: 128 us -> 289 us  [the longest x4 66.6 us: line_of_four(): far = [lax.ppermute(piece(k), 'dp', OUTER_TO_MIDDLE) for k in range(pieces)]]
    dot_general x27 -> x1, matrix products: 105 us -> 0.37 us  [dot_last(): lax.dot_general(a, b, (((1,), (1,)), ((), ())), preferred_element_type=jn...]
    pallas_call x0 -> x5, Pallas kernels: none -> 62.7 us  [product_terms(): pl.pallas_call(terms_kernel, grid_spec=pltpu.PrefetchScalarGridSpec(num_s...]
    unnamed x53 -> x63, local copies, waits for them, and re-layouts: 3.7 us -> 21.9 us
    convert_element_type x15 -> x0, other arithmetic: 7.09 us -> none  [sum_over_tensor(): (home.astype(jnp.float32) + got.astype(jnp.float32)).astype(jnp.bfloat16)]
    another operation x24 -> x0, local copies, waits for them, and re-layouts: 6.62 us -> none  [across(): jnp.stack([jnp.concatenate([dot_last(dy, w).astype(jnp.bfloat16) for w in...]
    dynamic_slice x2 -> x1, local copies, waits for them, and re-layouts: 8.15 us -> 2.26 us  [piece(): lax.dynamic_slice_in_dim(frozen_weight, rep * half + k * rows, rows, 0)]
    ppermute x28 -> x32, starting transfers between devices: 66.4 us -> 66.9 us  [the longest x1 19.7 us: line_of_four(): got_first = lax.ppermute(summed[1].astype(jnp.bfloat16), 'dp', PARTNER)]
  transfers between devices with their start and end apart: 40 -> 40, of which waited for: 17 -> 21; matrix products, arithmetic and copies ran while one was open for 38% -> 4% of each run, Pallas kernels for 2% -> 14%
where the time goes in v2:
time: 501 us; the launch traced here: 491 us
  waiting for transfers between devices  295 us (59%)
  starting transfers between devices  78.8 us (16%)
  Pallas kernels  70.1 us (14%)
  local copies, waits for them, and re-layouts  33.7 us (7%)
  matrix products  8.5 us (2%)
    ppermute x4, waiting for transfers between devices, line_of_four(): far = [lax.ppermute(piece(k), 'dp', OUTER_TO_MIDDLE) for k in range(pieces)]  66.6 us
    pallas_call x5, Pallas kernels, product_terms(): pl.pallas_call(terms_kernel, grid_spec=pltpu.PrefetchScalarGridSpec(num_s...  62.7 us
    ppermute x4, waiting for transfers between devices, line_of_four(): got = lax.ppermute(summed[1].astype(jnp.bfloat16), 'dp', OUTWARD)  61.1 us
    ppermute x1, waiting for transfers between devices, line_of_four(): partner_grads = lax.ppermute(tile_grads, 'dp', PARTNER)  56.2 us
    ppermute x1, waiting for transfers between devices, line_of_four(): near_grads_out = lax.ppermute(near_grads, 'dp', OUTWARD)  46.9 us
    ppermute x8, waiting for transfers between devices, swap_rep(): return lax.ppermute(w, 'rep', [(0, 1), (1, 0)])  30.8 us
    unnamed x63, local copies, waits for them, and re-layouts  21.9 us
    ppermute x1, starting transfers between devices, line_of_four(): got_first = lax.ppermute(summed[1].astype(jnp.bfloat16), 'dp', PARTNER)  19.7 us
  transfers between devices with their start and end apart: 40, of which 21 were waited for; matrix products, arithmetic and copies ran while one was open for 4% of the time, Pallas kernels for 14%

profile of v2, /device:TPU:0, one launch (start us, length us, event | category | flops | bytes accessed | tf_op | source)
XLA Modules:
  0.0 491.4 jit_solution(14253460887286033092)
XLA Ops:
  3.5 4.2 all-to-all-start
  7.7 2.2 collective-permute-start
  9.9 3.7 gather_fusion
  13.6 3.2 convolution_convert_fusion
  18.6 3.3 all-to-all-start.1
  22.5 3.3 all-to-all-done.1
  27.3 3.3 all-to-all-start.2
  30.7 2.6 fusion.2
  36.1 2.3 constant_dynamic-slice_fusion.8
  38.4 6.6 %collective-permute-start.27 = (bf16[128,3584]{1,0:T(8,128)(2,1)S(1)}, bf16[128,3584]{1,0:T(8,128)(2,1)S(1)}, u32[]{:S(2)}, u32[]{:S(2)}) collective-permute-start(bf16[128,3584]{1,0:T(8,128)(2,1)S(1)} %get-tuple-element.30), channel_id=1, source_target_pairs={{0,8},{12,4},{1,9},{13,5},{2,10},{14,6},{3,11},{15,7},{16,24},{28,... | collective-permute-start | bytes 2752520 | tf_op jit(solution)/shard_map/ppermute | solution.py:204
  46.4 56.2 %collective-permute-done.32.refs_1_ = bf16[4,16,4608]{2,1,0:T(8,128)(2,1)S(1)} collective-permute-done((bf16[4,16,4608]{2,1,0:T(8,128)(2,1)S(1)}, bf16[4,16,4608]{2,1,0:T(8,128)(2,1)S(1)}, u32[]{:S(2)}, u32[]{:S(2)}) %collective-permute-start.32) | collective-permute-done | bytes 589856 | tf_op jit(solution)/shard_map/ppermute | solution.py:211
  102.6 5.2 %collective-permute-start.17 = (bf16[128,3584]{1,0:T(8,128)(2,1)S(1)}, bf16[128,3584]{1,0:T(8,128)(2,1)S(1)}, u32[]{:S(2)}, u32[]{:S(2)}) collective-permute-start(bf16[128,3584]{1,0:T(8,128)(2,1)S(1)} %get-tuple-element.29), channel_id=1, source_target_pairs={{0,8},{12,4},{1,9},{13,5},{2,10},{14,6},{3,11},{15,7},{16,24},{28,... | collective-permute-start | bytes 2752520 | tf_op jit(solution)/shard_map/ppermute | solution.py:204
  109.2 12.8 %collective-permute-done.27.refs_0_ = bf16[128,3584]{1,0:T(8,128)(2,1)S(1)} collective-permute-done((bf16[128,3584]{1,0:T(8,128)(2,1)S(1)}, bf16[128,3584]{1,0:T(8,128)(2,1)S(1)}, u32[]{:S(2)}, u32[]{:S(2)}) %collective-permute-start.27) | collective-permute-done | bytes 917536 | tf_op jit(solution)/shard_map/ppermute | solution.py:204
  123.7 18.1 %collective-permute-done.22.refs_0_ = bf16[128,3584]{1,0:T(8,128)(2,1)S(1)} collective-permute-done((bf16[128,3584]{1,0:T(8,128)(2,1)S(1)}, bf16[128,3584]{1,0:T(8,128)(2,1)S(1)}, u32[]{:S(2)}, u32[]{:S(2)}) %collective-permute-start.22) | collective-permute-done | bytes 917536 | tf_op jit(solution)/shard_map/ppermute | solution.py:204
  143.3 18.1 %collective-permute-done.17.refs_0_ = bf16[128,3584]{1,0:T(8,128)(2,1)S(1)} collective-permute-done((bf16[128,3584]{1,0:T(8,128)(2,1)S(1)}, bf16[128,3584]{1,0:T(8,128)(2,1)S(1)}, u32[]{:S(2)}, u32[]{:S(2)}) %collective-permute-start.17) | collective-permute-done | bytes 917536 | tf_op jit(solution)/shard_map/ppermute | solution.py:204
  163.0 17.6 %collective-permute-done.12.refs_0_ = bf16[128,3584]{1,0:T(8,128)(2,1)S(1)} collective-permute-done((bf16[128,3584]{1,0:T(8,128)(2,1)S(1)}, bf16[128,3584]{1,0:T(8,128)(2,1)S(1)}, u32[]{:S(2)}, u32[]{:S(2)}) %collective-permute-start.12) | collective-permute-done | bytes 917536 | tf_op jit(solution)/shard_map/ppermute | solution.py:204
  191.3 46.9 %collective-permute-done.35.refs_4_ = bf16[4,16,4608]{2,1,0:T(8,128)(2,1)S(1)} collective-permute-done((bf16[4,16,4608]{2,1,0:T(8,128)(2,1)S(1)}, bf16[4,16,4608]{2,1,0:T(8,128)(2,1)S(1)}, u32[]{:S(2)}, u32[]{:S(2)}) %collective-permute-start.35) | collective-permute-done | bytes 589856 | tf_op jit(solution)/shard_map/ppermute | solution.py:214
  250.0 17.2 %collective-permute-done.13.refs_1_ = bf16[128,3584]{1,0:T(8,128)(2,1)S(1)} collective-permute-done((bf16[128,3584]{1,0:T(8,128)(2,1)S(1)}, bf16[128,3584]{1,0:T(8,128)(2,1)S(1)}, u32[]{:S(2)}, u32[]{:S(2)}) %collective-permute-start.13) | collective-permute-done | bytes 917536 | tf_op jit(solution)/shard_map/ppermute | solution.py:200
  275.5 8.0 %shard_map.107 = (bf16[2,2,128,256]{3,2,1,0:T(8,128)(2,1)}, bf16[2,2,128,256]{3,2,1,0:T(8,128)(2,1)S(1)}) custom-call(s32[2]{0:T(128)S(1)} %pad_add_fusion.place_ref, bf16[2,2,128,3584]{3,2,1,0:T(8,128)(2,1)S(1)} %bitcast.114, bf16[2,2,128,3584]{3,2,1,0:T(8,128)(2,1)} %bitcast.3.partner_ref, bf16[128,3584]{1,0:T(8,128)(2,1)S(1)} %copy-done.11, ...), custom_call_target="tpu_custom_call" | custom-call | flops 1000 | bytes 1000 | tf_op jit(solution)/shard_map/pallas_call | solution.py:102
  283.5 12.2 %collective-permute-done.36.refs_5_ = bf16[4,16,4608]{2,1,0:T(8,128)(2,1)} collective-permute-done((bf16[4,16,4608]{2,1,0:T(8,128)(2,1)}, bf16[4,16,4608]{2,1,0:T(8,128)(2,1)}, u32[]{:S(2)}, u32[]{:S(2)}) %collective-permute-start.36) | collective-permute-done | bytes 589856 | tf_op jit(solution)/shard_map/ppermute | solution.py:215
  298.0 7.3 %shard_map.108 = (f32[32,16,3584]{2,1,0:T(8,128)}, f32[32,16,1024]{2,1,0:T(8,128)}) custom-call(s32[24]{0:T(128)S(1)} %concatenate.26.slots_ref, bf16[4,16,4608]{2,1,0:T(8,128)(2,1)S(1)} %pad_maximum_fusion.refs_0_, bf16[4,16,4608]{2,1,0:T(8,128)(2,1)S(1)} %collective-permute-done.32.refs_1_, bf16[4,16,4608]{2,1,0:T(8,128)(2,1)S(1)} %copy-done.21, ...), custom_call_target="tpu_custom_call" | custom-call | tf_op jit(solution)/shard_map/pallas_call | solution.py:47
  309.8 7.4 %shard_map.106 = (bf16[2,2,128,256]{3,2,1,0:T(8,128)(2,1)S(1)}, bf16[2,2,128,256]{3,2,1,0:T(8,128)(2,1)S(1)}) custom-call(s32[2]{0:T(128)S(1)} %pad_add_fusion.place_ref, bf16[2,2,128,3584]{3,2,1,0:T(8,128)(2,1)S(1)} %bitcast.115, bf16[2,2,128,3584]{3,2,1,0:T(8,128)(2,1)} %bitcast.3.partner_ref, bf16[128,3584]{1,0:T(8,128)(2,1)S(1)} %copy-done.5, ...), custom_call_target="tpu_custom_call" | custom-call | flops 1000 | bytes 1000 | tf_op jit(solution)/shard_map/pallas_call | solution.py:102
  317.2 7.4 %shard_map.105 = (bf16[2,2,128,256]{3,2,1,0:T(8,128)(2,1)S(1)}, bf16[2,2,128,256]{3,2,1,0:T(8,128)(2,1)S(1)}) custom-call(s32[2]{0:T(128)S(1)} %pad_add_fusion.place_ref, bf16[2,2,128,3584]{3,2,1,0:T(8,128)(2,1)S(1)} %bitcast.116, bf16[2,2,128,3584]{3,2,1,0:T(8,128)(2,1)} %bitcast.3.partner_ref, bf16[128,3584]{1,0:T(8,128)(2,1)S(1)} %copy-done.7, ...), custom_call_target="tpu_custom_call" | custom-call | flops 1000 | bytes 1000 | tf_op jit(solution)/shard_map/pallas_call | solution.py:102
  324.6 7.4 %shard_map.104 = (bf16[2,2,128,256]{3,2,1,0:T(8,128)(2,1)S(1)}, bf16[2,2,128,256]{3,2,1,0:T(8,128)(2,1)S(1)}) custom-call(s32[2]{0:T(128)S(1)} %pad_add_fusion.place_ref, bf16[2,2,128,3584]{3,2,1,0:T(8,128)(2,1)S(1)} %bitcast.117, bf16[2,2,128,3584]{3,2,1,0:T(8,128)(2,1)} %bitcast.3.partner_ref, bf16[128,3584]{1,0:T(8,128)(2,1)S(1)} %copy-done.9, ...), custom_call_target="tpu_custom_call" | custom-call | flops 1000 | bytes 1000 | tf_op jit(solution)/shard_map/pallas_call | solution.py:102
  333.1 11.5 %collective-permute-done.8.refs_8_ = bf16[128,3584]{1,0:T(8,128)(2,1)} collective-permute-done((bf16[128,3584]{1,0:T(8,128)(2,1)S(1)}, bf16[128,3584]{1,0:T(8,128)(2,1)}, u32[]{:S(2)}, u32[]{:S(2)}) %collective-permute-start.8) | collective-permute-done | bytes 917536 | tf_op jit(solution)/shard_map/ppermute | solution.py:200
  344.6 32.6 %shard_map.103 = (bf16[2,2,128,2048]{3,2,1,0:T(8,128)(2,1)}, bf16[2,2,128,2048]{3,2,1,0:T(8,128)(2,1)}) custom-call(s32[2]{0:T(128)S(1)} %pad_add_fusion.place_ref, bf16[2,2,128,3584]{3,2,1,0:T(8,128)(2,1)} %bitcast.113, bf16[2,2,128,3584]{3,2,1,0:T(8,128)(2,1)} %bitcast.3.partner_ref, bf16[1024,3584]{1,0:T(8,128)(2,1)} %refs_0_.1, ...), custom_call_target="tpu_custom_call" | custom-call | flops 1000 | bytes 1000 | tf_op jit(solution)/shard_map/pallas_call | solution.py:102
  395.4 50.5 %collective-permute-done.31 = bf16[128,256]{1,0:T(8,128)(2,1)S(1)} collective-permute-done((bf16[128,256]{1,0:T(8,128)(2,1)S(1)}, bf16[128,256]{1,0:T(8,128)(2,1)S(1)}, u32[]{:S(2)}, u32[]{:S(2)}) %collective-permute-start.31) | collective-permute-done | bytes 65568 | tf_op jit(solution)/shard_map/ppermute | solution.py:235
  445.9 2.8 collective-permute-done.26
  448.7 2.8 collective-permute-done.21
  451.5 5.0 %collective-permute-done.16 = bf16[128,256]{1,0:T(8,128)(2,1)S(1)} collective-permute-done((bf16[128,256]{1,0:T(8,128)(2,1)S(1)}, bf16[128,256]{1,0:T(8,128)(2,1)S(1)}, u32[]{:S(2)}, u32[]{:S(2)}) %collective-permute-start.16) | collective-permute-done | bytes 65568 | tf_op jit(solution)/shard_map/ppermute | solution.py:235
  456.9 19.7 %collective-permute-start.11 = (bf16[128,2048]{1,0:T(8,128)(2,1)S(1)}, bf16[128,2048]{1,0:T(8,128)(2,1)S(1)}, u32[]{:S(2)}, u32[]{:S(2)}) collective-permute-start(bf16[128,2048]{1,0:T(8,128)(2,1)S(1)} %get-tuple-element.36), channel_id=1, source_target_pairs={{0,4},{4,0},{8,12},{12,8},{1,5},{5,1},{9,13},{13,9},{2,6},{6,2},{1... | collective-permute-start | bytes 1572872 | tf_op jit(solution)/shard_map/ppermute | solution.py:220
  477.7 9.7 %collective-permute-done.11 = bf16[128,2048]{1,0:T(8,128)(2,1)S(1)} collective-permute-done((bf16[128,2048]{1,0:T(8,128)(2,1)S(1)}, bf16[128,2048]{1,0:T(8,128)(2,1)S(1)}, u32[]{:S(2)}, u32[]{:S(2)}) %collective-permute-start.11) | collective-permute-done | bytes 524320 | tf_op jit(solution)/shard_map/ppermute | solution.py:220
  (183 shorter events, 78.6 us)
Async XLA Ops:
  3.5 13.9 %all-to-all-start = ((bf16[4,16,1024]{2,1,0:T(8,128)(2,1)}), bf16[4,16,1024]{2,1,0:T(8,128)(2,1)S(1)}, u32[]{:S(2)}, u32[]{:S(2)}) async-start(bf16[4,16,1024]{2,1,0:T(8,128)(2,1)} %gather_fusion.1), calls=%async_computation | async-start | bytes 262144 | tf_op jit(solution)/shard_map/all_to_all | solution.py:133
  7.7 262.0 %collective-permute-start = (bf16[512,3584]{1,0:T(8,128)(2,1)}, bf16[512,3584]{1,0:T(8,128)(2,1)}, u32[]{:S(2)}, u32[]{:S(2)}) collective-permute-start(bf16[512,3584]{1,0:T(8,128)(2,1)} %param.9), channel_id=1, source_target_pairs={{0,4},{4,0},{8,12},{12,8},{1,5},{5,1},{9,13},{13,9},{2,6},{6,2},{1... | collective-permute-start | bytes 11010056 | tf_op jit(solution)/shard_map/ppermute | solution.py:202
  35.3 67.3 %collective-permute-start.32 = (bf16[4,16,4608]{2,1,0:T(8,128)(2,1)S(1)}, bf16[4,16,4608]{2,1,0:T(8,128)(2,1)S(1)}, u32[]{:S(2)}, u32[]{:S(2)}) collective-permute-start(bf16[4,16,4608]{2,1,0:T(8,128)(2,1)S(1)} %pad_maximum_fusion.refs_0_), channel_id=1, source_target_pairs={{0,4},{4,0},{8,12},{12,8},{1,5},{5,1},{9,13},{13,9},{2,6},{6,2},{1... | collective-permute-start | bytes 1769480 | tf_op jit(solution)/shard_map/ppermute | solution.py:211
  35.4 72.4 %collective-permute-start.33 = (bf16[4,16,4608]{2,1,0:T(8,128)(2,1)S(1)}, bf16[4,16,4608]{2,1,0:T(8,128)(2,1)S(1)}, u32[]{:S(2)}, u32[]{:S(2)}) collective-permute-start(bf16[4,16,4608]{2,1,0:T(8,128)(2,1)S(1)} %pad_maximum_fusion.refs_0_), channel_id=1, source_target_pairs={{4,8},{8,4},{5,9},{9,5},{6,10},{10,6},{7,11},{11,7},{20,24},{24,20... | collective-permute-start | bytes 1769480 | tf_op jit(solution)/shard_map/ppermute | solution.py:212
  38.4 83.7 %collective-permute-start.27 = (bf16[128,3584]{1,0:T(8,128)(2,1)S(1)}, bf16[128,3584]{1,0:T(8,128)(2,1)S(1)}, u32[]{:S(2)}, u32[]{:S(2)}) collective-permute-start(bf16[128,3584]{1,0:T(8,128)(2,1)S(1)} %get-tuple-element.30), channel_id=1, source_target_pairs={{0,8},{12,4},{1,9},{13,5},{2,10},{14,6},{3,11},{15,7},{16,24},{28,... | collective-permute-start | bytes 2752520 | tf_op jit(solution)/shard_map/ppermute | solution.py:204
  45.0 96.7 %collective-permute-start.22 = (bf16[128,3584]{1,0:T(8,128)(2,1)S(1)}, bf16[128,3584]{1,0:T(8,128)(2,1)S(1)}, u32[]{:S(2)}, u32[]{:S(2)}) collective-permute-start(bf16[128,3584]{1,0:T(8,128)(2,1)S(1)} %get-tuple-element.28), channel_id=1, source_target_pairs={{0,8},{12,4},{1,9},{13,5},{2,10},{14,6},{3,11},{15,7},{16,24},{28,... | collective-permute-start | bytes 2752520 | tf_op jit(solution)/shard_map/ppermute | solution.py:204
  102.6 58.8 %collective-permute-start.17 = (bf16[128,3584]{1,0:T(8,128)(2,1)S(1)}, bf16[128,3584]{1,0:T(8,128)(2,1)S(1)}, u32[]{:S(2)}, u32[]{:S(2)}) collective-permute-start(bf16[128,3584]{1,0:T(8,128)(2,1)S(1)} %get-tuple-element.29), channel_id=1, source_target_pairs={{0,8},{12,4},{1,9},{13,5},{2,10},{14,6},{3,11},{15,7},{16,24},{28,... | collective-permute-start | bytes 2752520 | tf_op jit(solution)/shard_map/ppermute | solution.py:204
  107.8 72.8 %collective-permute-start.12 = (bf16[128,3584]{1,0:T(8,128)(2,1)S(1)}, bf16[128,3584]{1,0:T(8,128)(2,1)S(1)}, u32[]{:S(2)}, u32[]{:S(2)}) collective-permute-start(bf16[128,3584]{1,0:T(8,128)(2,1)S(1)} %get-tuple-element.27), channel_id=1, source_target_pairs={{0,8},{12,4},{1,9},{13,5},{2,10},{14,6},{3,11},{15,7},{16,24},{28,... | collective-permute-start | bytes 2752520 | tf_op jit(solution)/shard_map/ppermute | solution.py:204
  122.0 59.3 %collective-permute-start.1 = (bf16[128,3584]{1,0:T(8,128)(2,1)S(1)}, bf16[128,3584]{1,0:T(8,128)(2,1)}, u32[]{:S(2)}, u32[]{:S(2)}) collective-permute-start(bf16[128,3584]{1,0:T(8,128)(2,1)S(1)} %get-tuple-element.27), channel_id=1, source_target_pairs={{4,8},{8,4},{5,9},{9,5},{6,10},{10,6},{7,11},{11,7},{20,24},{24,20... | collective-permute-start | bytes 2752520 | tf_op jit(solution)/shard_map/ppermute | solution.py:203
  141.8 41.1 %collective-permute-start.3 = (bf16[128,3584]{1,0:T(8,128)(2,1)S(1)}, bf16[128,3584]{1,0:T(8,128)(2,1)}, u32[]{:S(2)}, u32[]{:S(2)}) collective-permute-start(bf16[128,3584]{1,0:T(8,128)(2,1)S(1)} %get-tuple-element.29), channel_id=1, source_target_pairs={{4,8},{8,4},{5,9},{9,5},{6,10},{10,6},{7,11},{11,7},{20,24},{24,20... | collective-permute-start | bytes 2752520 | tf_op jit(solution)/shard_map/ppermute | solution.py:203
  161.4 23.5 %collective-permute-start.5 = (bf16[128,3584]{1,0:T(8,128)(2,1)S(1)}, bf16[128,3584]{1,0:T(8,128)(2,1)}, u32[]{:S(2)}, u32[]{:S(2)}) collective-permute-start(bf16[128,3584]{1,0:T(8,128)(2,1)S(1)} %get-tuple-element.28), channel_id=1, source_target_pairs={{4,8},{8,4},{5,9},{9,5},{6,10},{10,6},{7,11},{11,7},{20,24},{24,20... | collective-permute-start | bytes 2752520 | tf_op jit(solution)/shard_map/ppermute | solution.py:203
  182.8 55.4 %collective-permute-start.35 = (bf16[4,16,4608]{2,1,0:T(8,128)(2,1)S(1)}, bf16[4,16,4608]{2,1,0:T(8,128)(2,1)S(1)}, u32[]{:S(2)}, u32[]{:S(2)}) collective-permute-start(bf16[4,16,4608]{2,1,0:T(8,128)(2,1)S(1)} %collective-permute-done.33.refs_2_), channel_id=1, source_target_pairs={{4,0},{8,12},{5,1},{9,13},{6,2},{10,14},{7,3},{11,15},{20,16},{24,... | collective-permute-start | bytes 1769480 | tf_op jit(solution)/shard_map/ppermute | solution.py:214
  184.9 56.6 %collective-permute-start.28 = (bf16[128,3584]{1,0:T(8,128)(2,1)S(1)}, bf16[128,3584]{1,0:T(8,128)(2,1)S(1)}, u32[]{:S(2)}, u32[]{:S(2)}) collective-permute-start(bf16[128,3584]{1,0:T(8,128)(2,1)S(1)} %collective-permute-done.27.refs_0_), channel_id=1, source_target_pairs={{0,16},{16,0},{1,17},{17,1},{2,18},{18,2},{3,19},{19,3},{4,20},{20... | collective-permute-start | bytes 2752520 | tf_op jit(solution)/shard_map/ppermute | solution.py:200
  187.4 56.6 %collective-permute-start.23 = (bf16[128,3584]{1,0:T(8,128)(2,1)S(1)}, bf16[128,3584]{1,0:T(8,128)(2,1)S(1)}, u32[]{:S(2)}, u32[]{:S(2)}) collective-permute-start(bf16[128,3584]{1,0:T(8,128)(2,1)S(1)} %collective-permute-done.22.refs_0_), channel_id=1, source_target_pairs={{0,16},{16,0},{1,17},{17,1},{2,18},{18,2},{3,19},{19,3},{4,20},{20... | collective-permute-start | bytes 2752520 | tf_op jit(solution)/shard_map/ppermute | solution.py:200
  188.8 58.7 %collective-permute-start.18 = (bf16[128,3584]{1,0:T(8,128)(2,1)S(1)}, bf16[128,3584]{1,0:T(8,128)(2,1)S(1)}, u32[]{:S(2)}, u32[]{:S(2)}) collective-permute-start(bf16[128,3584]{1,0:T(8,128)(2,1)S(1)} %collective-permute-done.17.refs_0_), channel_id=1, source_target_pairs={{0,16},{16,0},{1,17},{17,1},{2,18},{18,2},{3,19},{19,3},{4,20},{20... | collective-permute-start | bytes 2752520 | tf_op jit(solution)/shard_map/ppermute | solution.py:200
  239.1 28.1 %collective-permute-start.13 = (bf16[128,3584]{1,0:T(8,128)(2,1)S(1)}, bf16[128,3584]{1,0:T(8,128)(2,1)S(1)}, u32[]{:S(2)}, u32[]{:S(2)}) collective-permute-start(bf16[128,3584]{1,0:T(8,128)(2,1)S(1)} %collective-permute-done.12.refs_0_), channel_id=1, source_target_pairs={{0,16},{16,0},{1,17},{17,1},{2,18},{18,2},{3,19},{19,3},{4,20},{20... | collective-permute-start | bytes 2752520 | tf_op jit(solution)/shard_map/ppermute | solution.py:200
  242.5 53.2 %collective-permute-start.36 = (bf16[4,16,4608]{2,1,0:T(8,128)(2,1)}, bf16[4,16,4608]{2,1,0:T(8,128)(2,1)}, u32[]{:S(2)}, u32[]{:S(2)}) collective-permute-start(bf16[4,16,4608]{2,1,0:T(8,128)(2,1)} %collective-permute-done.34.refs_3_), channel_id=1, source_target_pairs={{4,0},{8,12},{5,1},{9,13},{6,2},{10,14},{7,3},{11,15},{20,16},{24,... | collective-permute-start | bytes 1769480 | tf_op jit(solution)/shard_map/ppermute | solution.py:215
  244.9 87.1 %collective-permute-start.2 = (bf16[128,3584]{1,0:T(8,128)(2,1)}, bf16[128,3584]{1,0:T(8,128)(2,1)}, u32[]{:S(2)}, u32[]{:S(2)}) collective-permute-start(bf16[128,3584]{1,0:T(8,128)(2,1)} %collective-permute-done.1.refs_1_), channel_id=1, source_target_pairs={{0,16},{16,0},{1,17},{17,1},{2,18},{18,2},{3,19},{19,3},{4,20},{20... | collective-permute-start | bytes 2752520 | tf_op jit(solution)/shard_map/ppermute | solution.py:200
  248.5 84.1 %collective-permute-start.4 = (bf16[128,3584]{1,0:T(8,128)(2,1)}, bf16[128,3584]{1,0:T(8,128)(2,1)}, u32[]{:S(2)}, u32[]{:S(2)}) collective-permute-start(bf16[128,3584]{1,0:T(8,128)(2,1)} %collective-permute-done.3.refs_3_), channel_id=1, source_target_pairs={{0,16},{16,0},{1,17},{17,1},{2,18},{18,2},{3,19},{19,3},{4,20},{20... | collective-permute-start | bytes 2752520 | tf_op jit(solution)/shard_map/ppermute | solution.py:200
  268.1 64.5 %collective-permute-start.6 = (bf16[128,3584]{1,0:T(8,128)(2,1)}, bf16[128,3584]{1,0:T(8,128)(2,1)}, u32[]{:S(2)}, u32[]{:S(2)}) collective-permute-start(bf16[128,3584]{1,0:T(8,128)(2,1)} %collective-permute-done.5.refs_5_), channel_id=1, source_target_pairs={{0,16},{16,0},{1,17},{17,1},{2,18},{18,2},{3,19},{19,3},{4,20},{20... | collective-permute-start | bytes 2752520 | tf_op jit(solution)/shard_map/ppermute | solution.py:200
  269.6 74.9 %collective-permute-start.8 = (bf16[128,3584]{1,0:T(8,128)(2,1)S(1)}, bf16[128,3584]{1,0:T(8,128)(2,1)}, u32[]{:S(2)}, u32[]{:S(2)}) collective-permute-start(bf16[128,3584]{1,0:T(8,128)(2,1)S(1)} %collective-permute-done.7.refs_7_), channel_id=1, source_target_pairs={{0,16},{16,0},{1,17},{17,1},{2,18},{18,2},{3,19},{19,3},{4,20},{20... | collective-permute-start | bytes 2752520 | tf_op jit(solution)/shard_map/ppermute | solution.py:200
  295.7 81.6 %collective-permute-start.29 = (bf16[2,2,128,256]{3,2,1,0:T(8,128)(2,1)}, bf16[2,2,128,256]{3,2,1,0:T(8,128)(2,1)S(1)}, u32[]{:S(2)}, u32[]{:S(2)}) collective-permute-start(bf16[2,2,128,256]{3,2,1,0:T(8,128)(2,1)} %get-tuple-element.24), channel_id=1, source_target_pairs={{0,1},{1,0},{2,3},{3,2},{4,5},{5,4},{6,7},{7,6},{8,9},{9,8},{10,11... | collective-permute-start | bytes 786440 | tf_op jit(solution)/shard_map/ppermute | solution.py:157
  332.0 46.8 %collective-permute-start.24 = (bf16[2,2,128,256]{3,2,1,0:T(8,128)(2,1)S(1)}, bf16[2,2,128,256]{3,2,1,0:T(8,128)(2,1)S(1)}, u32[]{:S(2)}, u32[]{:S(2)}) collective-permute-start(bf16[2,2,128,256]{3,2,1,0:T(8,128)(2,1)S(1)} %get-tuple-element.22), channel_id=1, source_target_pairs={{0,1},{1,0},{2,3},{3,2},{4,5},{5,4},{6,7},{7,6},{8,9},{9,8},{10,11... | collective-permute-start | bytes 786440 | tf_op jit(solution)/shard_map/ppermute | solution.py:157
  332.6 47.1 %collective-permute-start.19 = (bf16[2,2,128,256]{3,2,1,0:T(8,128)(2,1)S(1)}, bf16[2,2,128,256]{3,2,1,0:T(8,128)(2,1)S(1)}, u32[]{:S(2)}, u32[]{:S(2)}) collective-permute-start(bf16[2,2,128,256]{3,2,1,0:T(8,128)(2,1)S(1)} %get-tuple-element.20), channel_id=1, source_target_pairs={{0,1},{1,0},{2,3},{3,2},{4,5},{5,4},{6,7},{7,6},{8,9},{9,8},{10,11... | collective-permute-start | bytes 786440 | tf_op jit(solution)/shard_map/ppermute | solution.py:157
  332.7 48.5 %collective-permute-start.14 = (bf16[2,2,128,256]{3,2,1,0:T(8,128)(2,1)S(1)}, bf16[2,2,128,256]{3,2,1,0:T(8,128)(2,1)S(1)}, u32[]{:S(2)}, u32[]{:S(2)}) collective-permute-start(bf16[2,2,128,256]{3,2,1,0:T(8,128)(2,1)S(1)} %get-tuple-element.18), channel_id=1, source_target_pairs={{0,1},{1,0},{2,3},{3,2},{4,5},{5,4},{6,7},{7,6},{8,9},{9,8},{10,11... | collective-permute-start | bytes 786440 | tf_op jit(solution)/shard_map/ppermute | solution.py:157
  377.2 14.6 %collective-permute-start.9 = (bf16[2,2,128,2048]{3,2,1,0:T(8,128)(2,1)}, bf16[2,2,128,2048]{3,2,1,0:T(8,128)(2,1)S(1)}, u32[]{:S(2)}, u32[]{:S(2)}) collective-permute-start(bf16[2,2,128,2048]{3,2,1,0:T(8,128)(2,1)} %get-tuple-element.16), channel_id=1, source_target_pairs={{0,1},{1,0},{2,3},{3,2},{4,5},{5,4},{6,7},{7,6},{8,9},{9,8},{10,11... | collective-permute-start | bytes 6291464 | tf_op jit(solution)/shard_map/ppermute | solution.py:157
  383.8 62.1 %collective-permute-start.31 = (bf16[128,256]{1,0:T(8,128)(2,1)S(1)}, bf16[128,256]{1,0:T(8,128)(2,1)S(1)}, u32[]{:S(2)}, u32[]{:S(2)}) collective-permute-start(bf16[128,256]{1,0:T(8,128)(2,1)S(1)} %slice_bitcast_fusion.7), channel_id=1, source_target_pairs={{4,0},{8,12},{5,1},{9,13},{6,2},{10,14},{7,3},{11,15},{20,16},{24,... | collective-permute-start | bytes 196616 | tf_op jit(solution)/shard_map/ppermute | solution.py:235
  386.6 62.1 %collective-permute-start.26 = (bf16[128,256]{1,0:T(8,128)(2,1)S(1)}, bf16[128,256]{1,0:T(8,128)(2,1)S(1)}, u32[]{:S(2)}, u32[]{:S(2)}) collective-permute-start(bf16[128,256]{1,0:T(8,128)(2,1)S(1)} %slice_bitcast_fusion.9), channel_id=1, source_target_pairs={{4,0},{8,12},{5,1},{9,13},{6,2},{10,14},{7,3},{11,15},{20,16},{24,... | collective-permute-start | bytes 196616 | tf_op jit(solution)/shard_map/ppermute | solution.py:235
  389.4 62.1 %collective-permute-start.21 = (bf16[128,256]{1,0:T(8,128)(2,1)S(1)}, bf16[128,256]{1,0:T(8,128)(2,1)S(1)}, u32[]{:S(2)}, u32[]{:S(2)}) collective-permute-start(bf16[128,256]{1,0:T(8,128)(2,1)S(1)} %slice_bitcast_fusion.11), channel_id=1, source_target_pairs={{4,0},{8,12},{5,1},{9,13},{6,2},{10,14},{7,3},{11,15},{20,16},{24,... | collective-permute-start | bytes 196616 | tf_op jit(solution)/shard_map/ppermute | solution.py:235
  392.7 63.8 %collective-permute-start.10 = (bf16[2,128,2048]{2,1,0:T(8,128)(2,1)S(1)}, bf16[2,128,2048]{2,1,0:T(8,128)(2,1)S(1)}, u32[]{:S(2)}, u32[]{:S(2)}) collective-permute-start(bf16[2,128,2048]{2,1,0:T(8,128)(2,1)S(1)} %fusion.6), channel_id=1, source_target_pairs={{0,2},{2,0},{1,3},{3,1},{4,6},{6,4},{5,7},{7,5},{8,10},{10,8},{9,1... | collective-permute-start | bytes 3145736 | tf_op jit(solution)/shard_map/ppermute | solution.py:159
  394.1 62.4 %collective-permute-start.16 = (bf16[128,256]{1,0:T(8,128)(2,1)S(1)}, bf16[128,256]{1,0:T(8,128)(2,1)S(1)}, u32[]{:S(2)}, u32[]{:S(2)}) collective-permute-start(bf16[128,256]{1,0:T(8,128)(2,1)S(1)} %slice_bitcast_fusion.13), channel_id=1, source_target_pairs={{4,0},{8,12},{5,1},{9,13},{6,2},{10,14},{7,3},{11,15},{20,16},{24,... | collective-permute-start | bytes 196616 | tf_op jit(solution)/shard_map/ppermute | solution.py:235
  456.9 30.6 %collective-permute-start.11 = (bf16[128,2048]{1,0:T(8,128)(2,1)S(1)}, bf16[128,2048]{1,0:T(8,128)(2,1)S(1)}, u32[]{:S(2)}, u32[]{:S(2)}) collective-permute-start(bf16[128,2048]{1,0:T(8,128)(2,1)S(1)} %get-tuple-element.36), channel_id=1, source_target_pairs={{0,4},{4,0},{8,12},{12,8},{1,5},{5,1},{9,13},{13,9},{2,6},{6,2},{1... | collective-permute-start | bytes 1572872 | tf_op jit(solution)/shard_map/ppermute | solution.py:220
  (37 other events, 489.1 us)

commit v3 on v2

--- a/solution.py
+++ b/solution.py
@@ -1,3 +1,5 @@
+import functools
+
 import jax
 import jax.numpy as jnp
 from jax import lax
@@ -64,106 +66,120 @@
     )(slots, *groups)
 
 
-def terms_kernel(place_ref, own_ref, partner_ref, *refs):
-    *weight_refs, away_ref, home_ref = refs
-    chip = place_ref[0]
-    depth = own_ref.shape[-1]
-
-    def products(dy_ref, out_ref):
-        dy = dy_ref[...].reshape(2 * TILE, depth)
-        column = 0
-        for weight_ref in weight_refs:
-            rows = weight_ref.shape[0]
-            step = min(rows, 512)
-            for start in range(0, rows, step):
-                part = dot_last(dy, weight_ref[start : start + step]).astype(jnp.bfloat16)
-                out_ref[1 - chip, 0, :, column : column + step] = part[:TILE]
-                out_ref[chip, 0, :, column : column + step] = part[TILE:]
-                column += step
-
-    for side, out_ref in ((0, away_ref), (1, home_ref)):
-        for group, dy_ref in ((0, own_ref), (1, partner_ref)):
-
-            @pl.when((pl.program_id(0) == side) & (pl.program_id(1) == group))
-            def _(dy_ref=dy_ref, out_ref=out_ref):
-                products(dy_ref, out_ref)
-
-
-def product_terms(dy, partner_dy, weights, place):
-    depth = dy.shape[1]
+def terms_kernel(group_count, out_count, place_ref, *refs):
+    dy_refs, refs = refs[:group_count], refs[group_count:]
+    *refs, dy_buffer, weight_buffer, dy_sems, weight_sems = refs
+    weight_refs, out_refs = refs[:-out_count], refs[-out_count:]
+    tiles_each = 4 // out_count
+    chip, core = place_ref[0], place_ref[1]
+    depth = dy_buffer.shape[-1]
+    starts = [0]
+    for ref in weight_refs:
+        starts.append(starts[-1] + ref.shape[0])
+
+    if out_count == 1:
+        owners = [(0, 0), (0, 1), (1, 0), (1, 1)]
+    else:
+        owners = [(1 - chip, 1 - core), (chip, 1 - core), (1 - chip, core), (chip, core)]
+
+    def start_dy(group, slot):
+        for k, dy_ref in enumerate(dy_refs):
+
+            @pl.when(group == k)
+            def _(dy_ref=dy_ref):
+                for i, (x, c) in enumerate(owners):
+                    pltpu.make_async_copy(
+                        dy_ref.at[x, c],
+                        dy_buffer.at[slot, pl.ds(i * TILE, TILE)],
+                        dy_sems.at[slot],
+                    ).start()
+
+    def wait_dy(slot):
+        whole = dy_buffer.at[slot]
+        pltpu.make_async_copy(whole, whole, dy_sems.at[slot]).wait()
+
+    start_dy(0, 0)
+    for i, (ref, start) in enumerate(zip(weight_refs, starts)):
+        for row in range(0, ref.shape[0], 256):
+            rows = min(256, ref.shape[0] - row)
+            pltpu.make_async_copy(
+                ref.at[pl.ds(row, rows)],
+                weight_buffer.at[pl.ds(start + row, rows)],
+                weight_sems.at[i],
+            ).start()
+
+    def one_group(group, carry):
+        slot = lax.rem(group, 2)
+
+        @pl.when(group + 1 < group_count)
+        def _():
+            start_dy(group + 1, 1 - slot)
+
+        wait_dy(slot)
+        dy = dy_buffer[slot]
+
+        @pl.when(group == 0)
+        def _():
+            for i, (start, end) in enumerate(zip(starts[:-1], starts[1:])):
+                whole = weight_buffer.at[pl.ds(start, end - start)]
+                pltpu.make_async_copy(whole, whole, weight_sems.at[i]).wait()
+
+        for column in range(0, starts[-1], 256):
+            stop = min(column + 256, starts[-1])
+            part = dot_last(dy, weight_buffer[column:stop]).astype(jnp.bfloat16)
+            for k in range(4):
+                out_ref = out_refs[k // tiles_each]
+                rows = part[k * TILE : (k + 1) * TILE]
+                out_ref[k % tiles_each, group, :, column:stop] = rows
+        return carry
+
+    lax.fori_loop(0, group_count, one_group, 0)
+
+
+def product_terms(groups, weights, place, out_count):
+    depth = groups[0].shape[1]
     columns = sum(w.shape[0] for w in weights)
-    split = (2, 2, TILE, depth)
-    out = jax.ShapeDtypeStruct((2, 2, TILE, columns), jnp.bfloat16)
-
-    def rows_of(side, group, place):
-        return (0, jnp.where(side == 0, 1 - place[1], place[1]), 0, 0)
-
-    dy_spec = pl.BlockSpec((2, 1, TILE, depth), rows_of)
+    out = jax.ShapeDtypeStruct((4 // out_count, len(groups), TILE, columns), jnp.bfloat16)
+    in_hbm = pl.BlockSpec(memory_space=pl.ANY)
     return pl.pallas_call(
-        terms_kernel,
+        functools.partial(terms_kernel, len(groups), out_count),
         grid_spec=pltpu.PrefetchScalarGridSpec(
             num_scalar_prefetch=1,
-            grid=(2, 2),
-            in_specs=[dy_spec, dy_spec]
-            + [
-                pl.BlockSpec(w.shape, lambda s, g, p: (0, 0), pipeline_mode=pl.Buffered(1))
-                for w in weights
-            ],
-            out_specs=[
-                pl.BlockSpec(
-                    (2, 1, TILE, columns), lambda s, g, p: (0, jnp.where(s == 0, g, 1), 0, 0)
-                ),
-                pl.BlockSpec(
-                    (2, 1, TILE, columns), lambda s, g, p: (0, jnp.where(s == 0, 0, g), 0, 0)
-                ),
+            grid=(1,),
+            in_specs=[in_hbm] * (len(groups) + len(weights)),
+            out_specs=[pl.BlockSpec(out.shape, lambda i, p: (0, 0, 0, 0))] * out_count,
+            scratch_shapes=[
+                pltpu.VMEM((2, 4 * TILE, depth), jnp.bfloat16),
+                pltpu.VMEM((columns, depth), jnp.bfloat16),
+                pltpu.SemaphoreType.DMA((2,)),
+                pltpu.SemaphoreType.DMA((len(weights),)),
             ],
         ),
-        out_shape=[out, out],
-        compiler_params=pltpu.CompilerParams(vmem_limit_bytes=48 * 1024 * 1024),
-        cost_estimate=pl.CostEstimate(flops=1000, bytes_accessed=1000, transcendentals=0),
-    )(place, dy.reshape(split), partner_dy.reshape(split), *weights)
-
-
-def adapter_parts(tokens, grad_out, adapter_down, adapter_up, tenants, counts):
-    tile_count = tenants.shape[0]
-    shard_index = lax.axis_index("tensor")
-    down_sel = adapter_down[tenants]
-    up_sel = adapter_up[tenants]
-    dy_tiles = grad_out.reshape(tile_count, TILE, -1)
-    own_down = lax.all_to_all(down_sel, "tensor", split_axis=0, concat_axis=2, tiled=True)[0]
-    middle = dot_last(own_down, tokens).astype(jnp.bfloat16)
-    backed_part = jnp.einsum(
-        "krf,ktf->krt", up_sel, dy_tiles, preferred_element_type=jnp.float32
-    ).astype(jnp.bfloat16)
-    sent = jnp.concatenate([backed_part, jnp.broadcast_to(middle, backed_part.shape)], axis=1)
-    got = lax.all_to_all(sent, "tensor", split_axis=0, concat_axis=0, tiled=True)
-    rank = middle.shape[0]
-    backed = jnp.sum(got[:, :rank].astype(jnp.float32), axis=0).astype(jnp.bfloat16)
-    middle_all = got[:, rank:]
-    scale = adapter_scale / counts[tenants].astype(jnp.float32)
-    tile_up = (
-        scale[:, None, None]
-        * jnp.einsum("krt,ktf->krf", middle_all, dy_tiles, preferred_element_type=jnp.float32)
-    ).astype(jnp.bfloat16)
-    own_tile_down = (
-        scale[shard_index] * jnp.dot(backed, tokens, preferred_element_type=jnp.float32)
-    ).astype(jnp.bfloat16)
-    tile_down = lax.all_to_all(own_tile_down, "tensor", split_axis=1, concat_axis=0, tiled=True)
-    tile_down = tile_down.reshape(tile_count, rank, -1)
-    return own_down, backed, jnp.concatenate([tile_up, tile_down], axis=2)
-
-
-def sum_over_tensor(away, home):
+        out_shape=[out] * out_count,
+        compiler_params=pltpu.CompilerParams(vmem_limit_bytes=60 * 1024 * 1024),
+        cost_estimate=pl.CostEstimate(flops=0, bytes_accessed=0, transcendentals=0),
+    )(place, *[dy.reshape(2, 2, TILE, depth) for dy in groups], *weights)
+
+
+def sum_over_tensor(terms):
+    away, home = terms
     got = lax.ppermute(away, "tensor", [(0, 1), (1, 0), (2, 3), (3, 2)])
     pair = home.astype(jnp.float32) + got.astype(jnp.float32)
     got = lax.ppermute(pair[0].astype(jnp.bfloat16), "tensor", [(0, 2), (2, 0), (1, 3), (3, 1)])
-    return pair[1] + got.astype(jnp.float32)
+    return (pair[1] + got.astype(jnp.float32)).astype(jnp.bfloat16)
+
+
+def sum_by_swap(terms):
+    got = lax.all_to_all(terms[0], "tensor", split_axis=0, concat_axis=0, tiled=True)
+    return jnp.sum(got.astype(jnp.float32), axis=0).astype(jnp.bfloat16)
 
 
 PARTNER = [(0, 1), (1, 0), (2, 3), (3, 2)]
 MIDDLE = [(1, 2), (2, 1)]
 OUTER_TO_MIDDLE = [(0, 2), (3, 1)]
 OUTWARD = [(1, 0), (2, 3)]
+OTHER_REP = [(0, 1), (1, 0)]
+OUTWARD_OTHER_REP = [(4 * r + a, 4 * (1 - r) + b) for r in (0, 1) for a, b in OUTWARD]
 
 
 def line_of_four(
@@ -182,59 +198,99 @@
     place = jnp.stack([shard // 2, shard % 2]).astype(jnp.int32)
     rows_group, ff_shard = grad_out.shape
     tile_count = rows_group // TILE
-    adapter_count = adapter_down.shape[0]
+    adapter_count, rank = adapter_down.shape[:2]
     slot_count = 2 * adapter_count // 4
     inner = (z == 1) | (z == 2)
     all_tenants = tenant_ids.reshape(-1, TILE)[:, 0]
     tenants = lax.dynamic_slice_in_dim(all_tenants, z * tile_count, tile_count)
-
-    width = frozen_weight.shape[0]
-    half = width // 2
-    pieces = 4
-    rows = half // pieces
-
-    def piece(k):
-        return lax.dynamic_slice_in_dim(frozen_weight, rep * half + k * rows, rows, 0)
-
-    def swap_rep(w):
-        return lax.ppermute(w, "rep", [(0, 1), (1, 0)])
-
-    partner_dy = lax.ppermute(grad_out, "dp", PARTNER)
-    near = [lax.ppermute(piece(k), "dp", MIDDLE) for k in range(pieces)]
-    far = [lax.ppermute(piece(k), "dp", OUTER_TO_MIDDLE) for k in range(pieces)]
-    near_pairs = [(w, swap_rep(w)) for w in near]
-    far_pairs = [(w, swap_rep(w)) for w in far]
-
-    own_down, backed, tile_grads = adapter_parts(
-        tokens, grad_out, adapter_down, adapter_up, tenants, tenant_token_counts
-    )
-    partner_grads = lax.ppermute(tile_grads, "dp", PARTNER)
-    near_grads = lax.ppermute(tile_grads, "dp", MIDDLE)
-    far_grads = lax.ppermute(partner_grads, "dp", MIDDLE)
+    half = frozen_weight.shape[0] // 2
+
+    def after(value, *events):
+        return lax.optimization_barrier((value,) + events)[0]
+
+    crossing = lax.dynamic_slice_in_dim(frozen_weight, rep * half, half, 0)
+    near = lax.ppermute(crossing, "dp", MIDDLE)
+    partner_dy = lax.ppermute(after(grad_out, crossing), "dp", PARTNER)
+    other_dy = lax.ppermute(grad_out, "rep", OTHER_REP)
+
+    dy_tiles = grad_out.reshape(tile_count, TILE, ff_shard)
+    down_sel = adapter_down[tenants]
+    up_sel = adapter_up[tenants]
+    own_down = lax.all_to_all(down_sel, "tensor", split_axis=0, concat_axis=2, tiled=True)[0]
+    middle = dot_last(own_down, tokens).astype(jnp.bfloat16)
+    backed_part = jnp.einsum(
+        "krf,ktf->krt", up_sel, dy_tiles, preferred_element_type=jnp.float32
+    ).astype(jnp.bfloat16)
+    sent = jnp.concatenate([backed_part, jnp.broadcast_to(middle, backed_part.shape)], axis=1)
+    got = lax.all_to_all(sent, "tensor", split_axis=0, concat_axis=0, tiled=True)
+    backed = jnp.sum(got[:, :rank].astype(jnp.float32), axis=0).astype(jnp.bfloat16)
+    middle = got[:, rank:]
+
+    def scale_of(tenants):
+        return adapter_scale / tenant_token_counts[tenants].astype(jnp.float32)
+
+    def up_gradients(scale, middle, dy):
+        dy = dy.reshape(tile_count, TILE, ff_shard)
+        product = jnp.einsum("krt,ktf->krf", middle, dy, preferred_element_type=jnp.float32)
+        return (scale[:, None, None] * product).astype(jnp.bfloat16)
+
+    scale = scale_of(tenants)
+    tile_up = up_gradients(scale, middle, grad_out)
+    own_tile_down = (
+        scale[shard] * jnp.dot(backed, tokens, preferred_element_type=jnp.float32)
+    ).astype(jnp.bfloat16)
+    tile_down = lax.all_to_all(
+        own_tile_down, "tensor", split_axis=1, concat_axis=0, tiled=True
+    ).reshape(tile_count, rank, -1)
+    tile_grads = jnp.concatenate([tile_up, tile_down], axis=2)
+    to_partner = jnp.concatenate([middle, tile_down], axis=2)
+
+    from_partner = lax.ppermute(to_partner, "dp", PARTNER)
+
+    partner_index = z + 1 - 2 * (z % 2)
+    partner_tenants = lax.dynamic_slice_in_dim(
+        all_tenants, partner_index * tile_count, tile_count
+    )
+    partner_up = up_gradients(
+        scale_of(partner_tenants), from_partner[:, :, :TILE], partner_dy
+    )
+    partner_grads = jnp.concatenate([partner_up, from_partner[:, :, TILE:]], axis=2)
+    far = lax.ppermute(after(crossing, partner_grads), "dp", OUTER_TO_MIDDLE)
+    partner_other_dy = lax.ppermute(after(partner_dy, other_dy), "rep", OTHER_REP)
+
+    events = (partner_dy, tile_grads, partner_grads)
+    own_terms = product_terms([after(grad_out, *events), partner_dy], [frozen_weight], place, 1)
+    own_sum = sum_by_swap(own_terms)
+
+    groups = [after(grad_out, near, own_terms[0]), partner_dy, other_dy]
+    near_terms = product_terms(groups, [near], place, 1)
+    near_sum = sum_by_swap(near_terms)
+
+    near_grads = lax.ppermute(after(tile_grads, own_sum, near_sum), "dp", MIDDLE)
+    far_grads = lax.ppermute(after(partner_grads, own_sum, near_sum), "dp", MIDDLE)
+
+    groups = [after(grad_out, own_sum, near_sum), partner_dy, other_dy]
+    far_terms = product_terms(groups, [far], place, 2)
+    far_sum = sum_over_tensor(far_terms)
+    outer_terms = product_terms(
+        [after(partner_other_dy, far_terms[0], near_grads)], [near, far], place, 2
+    )
+    outer_sum = sum_over_tensor(outer_terms)[0]
+    partner_block = lax.ppermute(own_sum[1], "dp", PARTNER)
+    both_sum = jnp.concatenate([near_sum, far_sum], axis=2)
+    both_out = lax.ppermute(both_sum[1], "dp", OUTWARD)
+    both_other = lax.ppermute(both_sum[2], "rep", OTHER_REP)
+    outer_other = lax.ppermute(outer_sum, ("rep", "dp"), OUTWARD_OTHER_REP)
     near_grads_out = lax.ppermute(near_grads, "dp", OUTWARD)
     far_grads_out = lax.ppermute(far_grads, "dp", OUTWARD)
 
-    first_weights = [frozen_weight] + [w for pair in near_pairs for w in pair]
-    summed = sum_over_tensor(*product_terms(grad_out, partner_dy, first_weights, place))
-    own_first = summed[0].astype(jnp.bfloat16)
-    got_first = lax.ppermute(summed[1].astype(jnp.bfloat16), "dp", PARTNER)
-    own_block, partner_block = own_first[:, :width], got_first[:, :width]
-
-    def in_order(columns):
-        pairs = columns.reshape(TILE, -1, 2, rows)
-        mine = pairs[:, :, 0].reshape(TILE, half)
-        other = pairs[:, :, 1].reshape(TILE, half)
-        return jnp.concatenate(
-            [jnp.where(rep == 0, mine, other), jnp.where(rep == 0, other, mine)], axis=1
-        )
-
-    near_block = in_order(jnp.where(inner, own_first[:, width:], got_first[:, width:]))
-    far_columns = []
-    for pair in far_pairs:
-        summed = sum_over_tensor(*product_terms(grad_out, partner_dy, pair, place))
-        got = lax.ppermute(summed[1].astype(jnp.bfloat16), "dp", OUTWARD)
-        far_columns.append(jnp.where(inner, summed[0].astype(jnp.bfloat16), got))
-    far_block = in_order(jnp.concatenate(far_columns, axis=1))
+    mine = jnp.where(inner, both_sum[0], both_out)
+    other = jnp.where(inner, both_other, outer_other)
+    low = jnp.where(rep == 0, mine, other)
+    high = jnp.where(rep == 0, other, mine)
+    near_block = jnp.concatenate([low[:, :half], high[:, :half]], axis=1)
+    far_block = jnp.concatenate([low[:, half:], high[:, half:]], axis=1)
+    own_block = own_sum[0]
 
     lora = adapter_scale * lax.dot_general(
         backed, own_down, (((0,), (0,)), ((), ())), preferred_element_type=jnp.float32
@@ -254,7 +310,6 @@
     )
     input_grad = (frozen.astype(jnp.float32) + lora).astype(jnp.bfloat16)
 
-    partner_index = z + 1 - 2 * (z % 2)
     near_index = jnp.where(z < 2, 2, 1)
     far_index = jnp.where(z < 2, 3, 0)
     tile_slots = owner_slots(owner_map, slot_count)[all_tenants].reshape(4, tile_count)

time: 501 us -> 268 us (0.53); the launches traced: 491 us -> 266 us
  waiting for transfers between devices: 295 us -> 94.6 us
  starting transfers between devices: 78.8 us -> 44.7 us
  blocking collectives: 0 us -> 24.5 us
  Pallas kernels: 70.1 us -> 53.9 us
  local copies, waits for them, and re-layouts: 33.7 us -> 20 us
  other arithmetic: 3.93 us -> 16.6 us
    ppermute x25 -> x12, waiting for transfers between devices: 224 us -> 49.8 us  [the longest x1 41.9 us: line_of_four(): from_partner = lax.ppermute(to_partner, 'dp', PARTNER)]
    ppermute x1, waiting for transfers between devices: 46.9 us -> 0.34 us  [line_of_four(): near_grads_out = lax.ppermute(near_grads, 'dp', OUTWARD)]
    ppermute x25 -> x12, starting transfers between devices: 58.5 us -> 26 us  [the longest x1 6.55 us: line_of_four(): far = lax.ppermute(after(crossing, partner_grads), 'dp', OUTER_TO_MIDDLE)]
    all_to_all x3 -> x4, waiting for transfers between devices: 5.27 us -> 30.4 us  [the longest x1 23.2 us: sum_by_swap(): lax.all_to_all(terms[0], 'tensor', split_axis=0, concat_axis=0, tiled=True)]
    all_to_all x0 -> x1, blocking collectives: none -> 24.5 us  [sum_by_swap(): lax.all_to_all(terms[0], 'tensor', split_axis=0, concat_axis=0, tiled=True)]
    unnamed x63 -> x29, local copies, waits for them, and re-layouts: 21.9 us -> 2.93 us
    pallas_call x5 -> x4, Pallas kernels: 62.7 us -> 47.8 us  [product_terms(): pl.pallas_call(functools.partial(terms_kernel, len(groups), out_count), g...]
    all_to_all x3 -> x4, starting transfers between devices: 10.8 us -> 13.5 us  [the longest x1 3.61 us: sum_by_swap(): lax.all_to_all(terms[0], 'tensor', split_axis=0, concat_axis=0, tiled=True)]
  transfers between devices with their start and end apart: 40 -> 22, of which waited for: 21 -> 11; matrix products, arithmetic and copies ran while one was open for 4% -> 15% of each run, Pallas kernels for 14% -> 16%
where the time goes in v3:
time: 268 us; the launch traced here: 266 us
  waiting for transfers between devices  94.6 us (35%)
  Pallas kernels  53.9 us (20%)
  starting transfers between devices  44.7 us (17%)
  blocking collectives  24.5 us (9%)
  local copies, waits for them, and re-layouts  20 us (7%)
  other arithmetic  16.6 us (6%)
  matrix products  11.1 us (4%)
    pallas_call x4, Pallas kernels, product_terms(): pl.pallas_call(functools.partial(terms_kernel, len(groups), out_count), g...  47.8 us
    ppermute x1, waiting for transfers between devices, line_of_four(): from_partner = lax.ppermute(to_partner, 'dp', PARTNER)  41.9 us
    all_to_all x1, blocking collectives, sum_by_swap(): lax.all_to_all(terms[0], 'tensor', split_axis=0, concat_axis=0, tiled=True)  24.5 us
    all_to_all x1, waiting for transfers between devices, sum_by_swap(): lax.all_to_all(terms[0], 'tensor', split_axis=0, concat_axis=0, tiled=True)  23.2 us
    ppermute x1, waiting for transfers between devices, line_of_four(): far_grads_out = lax.ppermute(far_grads, 'dp', OUTWARD)  9.13 us
    ppermute x1, starting transfers between devices, line_of_four(): far = lax.ppermute(after(crossing, partner_grads), 'dp', OUTER_TO_MIDDLE)  6.55 us
    pallas_call x1, Pallas kernels, place_in_slots(): pl.pallas_call(place_kernel, grid_spec=pltpu.PrefetchScalarGridSpec(num_s...  6.09 us
  transfers between devices with their start and end apart: 22, of which 11 were waited for; matrix products, arithmetic and copies ran while one was open for 15% of the time, Pallas kernels for 16%

profile of v3, /device:TPU:0, one launch (start us, length us, event | category | flops | bytes accessed | tf_op | source)
XLA Modules:
  0.0 266.5 jit_solution(8595849287712513613)
XLA Ops:
  0.7 4.3 %constant_dynamic-slice_fusion.4 = bf16[512,3584]{1,0:T(8,128)(2,1)} fusion(bf16[1024,3584]{1,0:T(8,128)(2,1)} %refs_2_.1, s32[]{:T(128)S(6)} %select_n.147), kind=kLoop, calls=%fused_computation.75 | loop fusion | bytes 7340036 | tf_op jit(solution)/shard_map/dynamic_slice | solution.py:211
  4.9 3.0 %collective-permute-start = (bf16[512,3584]{1,0:T(8,128)(2,1)}, bf16[512,3584]{1,0:T(8,128)(2,1)}, u32[]{:S(2)}, u32[]{:S(2)}) collective-permute-start(bf16[512,3584]{1,0:T(8,128)(2,1)} %param.9), channel_id=1, source_target_pairs={{0,4},{4,0},{8,12},{12,8},{1,5},{5,1},{9,13},{13,9},{2,6},{6,2},{1... | collective-permute-start | bytes 11010056 | tf_op jit(solution)/shard_map/ppermute | solution.py:213
  9.5 2.5 collective-permute-start.3
  13.5 3.3 %all-to-all-start = ((bf16[4,16,1024]{2,1,0:T(8,128)(2,1)}), bf16[4,16,1024]{2,1,0:T(8,128)(2,1)S(1)}, u32[]{:S(2)}, u32[]{:S(2)}) async-start(bf16[4,16,1024]{2,1,0:T(8,128)(2,1)} %gather_fusion.2), calls=%async_computation | async-start | bytes 262144 | tf_op jit(solution)/shard_map/all_to_all | solution.py:219
  16.8 3.7 %gather_fusion.1 = bf16[4,16,3584]{2,1,0:T(8,128)(2,1)S(1)} fusion(bf16[64,16,3584]{2,1,0:T(8,128)(2,1)} %param.12, s32[1024]{0:T(1024)S(1)} %pad_clamp_fusion.2), kind=kCustom, calls=%fused_computation.1 | custom fusion | bytes 917520 | tf_op jit(solution)/shard_map/gather | solution.py:218
  21.1 3.2 %convolution_convert_fusion = bf16[4,16,128]{2,1,0:T(8,128)(2,1)S(1)} fusion(bf16[4,16,3584]{2,1,0:T(8,128)(2,1)S(1)} %gather_fusion.1, bf16[4,128,3584]{2,1,0:T(8,128)(2,1)} %bitcast.3), kind=kOutput, calls=%fused_computation.14 | convolution fusion | flops 58728448 | bytes 4145152 | tf_op jit(solution)/shard_map/krf,ktf->krt/dot_general | solution.py:221
  26.8 3.3 %all-to-all-start.1 = ((bf16[4,32,128]{2,1,0:T(8,128)(2,1)}), bf16[4,32,128]{2,1,0:T(8,128)(2,1)S(1)}, u32[]{:S(2)}, u32[]{:S(2)}) async-start(bf16[4,32,128]{2,1,0:T(8,128)(2,1)} %pad_maximum_fusion.6), calls=%async_computation.1 | async-start | bytes 65536 | tf_op jit(solution)/shard_map/all_to_all | solution.py:225
  30.7 3.3 %all-to-all-done.1 = bf16[4,32,128]{2,1,0:T(8,128)(2,1)S(1)} async-done(((bf16[4,32,128]{2,1,0:T(8,128)(2,1)}), bf16[4,32,128]{2,1,0:T(8,128)(2,1)S(1)}, u32[]{:S(2)}, u32[]{:S(2)}) %all-to-all-start.1) | async-done | bytes 32800 | tf_op jit(solution)/shard_map/all_to_all | solution.py:225
  35.5 3.3 %all-to-all-start.2 = ((bf16[16,4,1024]{2,0,1:T(8,128)(2,1)}), bf16[16,4,1024]{2,0,1:T(8,128)(2,1)S(1)}, u32[]{:S(2)}, u32[]{:S(2)}) async-start(bf16[16,4,1024]{2,0,1:T(8,128)(2,1)} %bitcast.92), calls=%async_computation.2 | async-start | bytes 262144 | tf_op jit(solution)/shard_map/all_to_all | solution.py:242
  39.5 4.0 %all-to-all-done.2 = bf16[16,4,1024]{2,0,1:T(8,128)(2,1)S(1)} async-done(((bf16[16,4,1024]{2,0,1:T(8,128)(2,1)}), bf16[16,4,1024]{2,0,1:T(8,128)(2,1)S(1)}, u32[]{:S(2)}, u32[]{:S(2)}) %all-to-all-start.2) | async-done | bytes 131104 | tf_op jit(solution)/shard_map/all_to_all | solution.py:242
  43.5 2.7 %collective-permute-start.1 = (bf16[4,16,1152]{2,1,0:T(8,128)(2,1)S(1)}, bf16[4,16,1152]{2,1,0:T(8,128)(2,1)S(1)}, u32[]{:S(2)}, u32[]{:S(2)}) collective-permute-start(bf16[4,16,1152]{2,1,0:T(8,128)(2,1)S(1)} %pad_maximum_fusion.5), channel_id=1, source_target_pairs={{0,4},{4,0},{8,12},{12,8},{1,5},{5,1},{9,13},{13,9},{2,6},{6,2},{1... | collective-permute-start | bytes 442376 | tf_op jit(solution)/shard_map/ppermute | solution.py:248
  46.2 2.6 fusion
  48.8 41.9 %collective-permute-done.1 = bf16[4,16,1152]{2,1,0:T(8,128)(2,1)S(1)} collective-permute-done((bf16[4,16,1152]{2,1,0:T(8,128)(2,1)S(1)}, bf16[4,16,1152]{2,1,0:T(8,128)(2,1)S(1)}, u32[]{:S(2)}, u32[]{:S(2)}) %collective-permute-start.1) | collective-permute-done | bytes 147488 | tf_op jit(solution)/shard_map/ppermute | solution.py:248
  90.7 2.6 fusion.1
  93.4 6.5 %collective-permute-start.5 = (bf16[512,3584]{1,0:T(8,128)(2,1)}, bf16[512,3584]{1,0:T(8,128)(2,1)}, u32[]{:S(2)}, u32[]{:S(2)}) collective-permute-start(bf16[512,3584]{1,0:T(8,128)(2,1)} %constant_dynamic-slice_fusion.4), channel_id=1, source_target_pairs={{0,8},{12,4},{1,9},{13,5},{2,10},{14,6},{3,11},{15,7},{16,24},{28,... | collective-permute-start | bytes 11010056 | tf_op jit(solution)/shard_map/ppermute | solution.py:258
  101.5 14.4 %shard_map.103 = bf16[4,2,128,1024]{3,2,1,0:T(8,128)(2,1)} custom-call(s32[2]{0:T(128)} %pad_add_fusion.place_ref, bf16[2,2,128,3584]{3,2,1,0:T(8,128)(2,1)} %bitcast.9.refs_0_, bf16[2,2,128,3584]{3,2,1,0:T(8,128)(2,1)} %bitcast.10.refs_1_, bf16[1024,3584]{1,0:T(8,128)(2,1)} %refs_2_.1), custom_call_target="tpu_custom_call" | custom-call | tf_op jit(solution)/shard_map/pallas_call | solution.py:144
  115.9 11.8 %shard_map.104 = bf16[4,3,128,512]{3,2,1,0:T(8,128)(2,1)} custom-call(s32[2]{0:T(128)} %pad_add_fusion.place_ref, bf16[2,2,128,3584]{3,2,1,0:T(8,128)(2,1)} %bitcast.13.refs_0_, bf16[2,2,128,3584]{3,2,1,0:T(8,128)(2,1)} %bitcast.10.refs_1_, bf16[2,2,128,3584]{3,2,1,0:T(8,128)(2,1)} %bitcast.14.refs_2_, bf16[512,3584]{1,0:T(8,128)(2,1)} %collective-permute-done.3.refs_3_.refs_1_), custom_call_target="tpu_custom_call" | custom-call | tf_op jit(solution)/shard_map/pallas_call | solution.py:144
  127.7 24.5 %all_to_all.46 = bf16[4,3,128,512]{3,2,1,0:T(8,128)(2,1)} all-to-all(bf16[4,3,128,512]{3,2,1,0:T(8,128)(2,1)} %shard_map.104), channel_id=1, replica_groups=mesh['rep'=2,'dp'=4,'tensor'=4] {'tensor'}, dimensions={0} | all-to-all | bytes 3145728 | tf_op jit(solution)/shard_map/all_to_all | solution.py:173
  152.2 3.6 %all-to-all-start.3 = ((bf16[4,2,128,1024]{3,2,1,0:T(8,128)(2,1)}), bf16[4,2,128,1024]{3,2,1,0:T(8,128)(2,1)S(1)}, u32[]{:S(2)}, u32[]{:S(2)}) async-start(bf16[4,2,128,1024]{3,2,1,0:T(8,128)(2,1)} %shard_map.103), calls=%async_computation.3 | async-start | bytes 4194304 | tf_op jit(solution)/shard_map/all_to_all | solution.py:173
  155.8 2.5 reduce_sum.47
  158.3 23.2 %all-to-all-done.3 = bf16[4,2,128,1024]{3,2,1,0:T(8,128)(2,1)S(1)} async-done(((bf16[4,2,128,1024]{3,2,1,0:T(8,128)(2,1)}), bf16[4,2,128,1024]{3,2,1,0:T(8,128)(2,1)S(1)}, u32[]{:S(2)}, u32[]{:S(2)}) %all-to-all-start.3) | async-done | bytes 2097184 | tf_op jit(solution)/shard_map/all_to_all | solution.py:173
  183.7 11.7 %shard_map.105 = (bf16[2,3,128,512]{3,2,1,0:T(8,128)(2,1)}, bf16[2,3,128,512]{3,2,1,0:T(8,128)(2,1)}) custom-call(s32[2]{0:T(128)} %pad_add_fusion.place_ref, bf16[2,2,128,3584]{3,2,1,0:T(8,128)(2,1)} %bitcast.15.refs_0_, bf16[2,2,128,3584]{3,2,1,0:T(8,128)(2,1)} %bitcast.10.refs_1_, bf16[2,2,128,3584]{3,2,1,0:T(8,128)(2,1)} %bitcast.14.refs_2_, ...), custom_call_target="tpu_custom_call" | custom-call | tf_op jit(solution)/shard_map/pallas_call | solution.py:144
  195.4 9.9 %shard_map.106 = (bf16[2,1,128,1024]{3,2,1,0:T(8,128)(2,1)}, bf16[2,1,128,1024]{3,2,1,0:T(8,128)(2,1)}) custom-call(s32[2]{0:T(128)} %pad_add_fusion.place_ref, bf16[2,2,128,3584]{3,2,1,0:T(8,128)(2,1)} %bitcast.21.refs_0_, bf16[512,3584]{1,0:T(8,128)(2,1)} %collective-permute-done.3.refs_3_.refs_1_, bf16[512,3584]{1,0:T(8,128)(2,1)} %collective-permute-done.5.refs_3_.refs_2_), custom_call_target="tpu_custom_call" | custom-call | tf_op jit(solution)/shard_map/pallas_call | solution.py:144
  211.1 2.5 convert_add_fusion
  213.6 1.9 fusion.7
  220.2 1.9 fusion.8
  223.4 4.5 %collective-permute-done.7 = bf16[3,128,512]{2,1,0:T(8,128)(2,1)} collective-permute-done((bf16[3,128,512]{2,1,0:T(8,128)(2,1)}, bf16[3,128,512]{2,1,0:T(8,128)(2,1)}, u32[]{:S(2)}, u32[]{:S(2)}) %collective-permute-start.7) | collective-permute-done | bytes 393248 | tf_op jit(solution)/shard_map/ppermute | solution.py:168
  236.3 3.5 %collective-permute-start.2 = (bf16[128,1024]{1,0:T(8,128)(2,1)S(1)}, bf16[128,1024]{1,0:T(8,128)(2,1)S(1)}, u32[]{:S(2)}, u32[]{:S(2)}) collective-permute-start(bf16[128,1024]{1,0:T(8,128)(2,1)S(1)} %slice_bitcast_fusion.2), channel_id=1, source_target_pairs={{0,4},{4,0},{8,12},{12,8},{1,5},{5,1},{9,13},{13,9},{2,6},{6,2},{1... | collective-permute-start | bytes 786440 | tf_op jit(solution)/shard_map/ppermute | solution.py:279
  239.8 9.1 %collective-permute-done.17.refs_5_ = bf16[4,16,4608]{2,1,0:T(8,128)(2,1)S(1)} collective-permute-done((bf16[4,16,4608]{2,1,0:T(8,128)(2,1)S(1)}, bf16[4,16,4608]{2,1,0:T(8,128)(2,1)S(1)}, u32[]{:S(2)}, u32[]{:S(2)}) %collective-permute-start.17) | collective-permute-done | bytes 589856 | tf_op jit(solution)/shard_map/ppermute | solution.py:285
  249.0 6.1 %shard_map.107 = (f32[32,16,3584]{2,1,0:T(8,128)}, f32[32,16,1024]{2,1,0:T(8,128)}) custom-call(s32[24]{0:T(128)S(1)} %concatenate.35.slots_ref, bf16[4,16,4608]{2,1,0:T(8,128)(2,1)S(1)} %pad_maximum_fusion.refs_0_, bf16[4,16,4608]{2,1,0:T(8,128)(2,1)S(1)} %pad_maximum_fusion.1.refs_1_, bf16[4,16,4608]{2,1,0:T(8,128)(2,1)S(1)} %collective-permute-done.11.refs_2_, ...), custom_call_target="tpu_custom_call" | custom-call | tf_op jit(solution)/shard_map/pallas_call | solution.py:49
  255.1 5.2 %collective-permute-done.8 = bf16[128,1024]{1,0:T(8,128)(2,1)} collective-permute-done((bf16[128,1024]{1,0:T(8,128)(2,1)}, bf16[128,1024]{1,0:T(8,128)(2,1)}, u32[]{:S(2)}, u32[]{:S(2)}) %collective-permute-start.8) | collective-permute-done | bytes 262176 | tf_op jit(solution)/shard_map/ppermute | solution.py:281
  261.6 2.7 %collective-permute-done.2 = bf16[128,1024]{1,0:T(8,128)(2,1)S(1)} collective-permute-done((bf16[128,1024]{1,0:T(8,128)(2,1)S(1)}, bf16[128,1024]{1,0:T(8,128)(2,1)S(1)}, u32[]{:S(2)}, u32[]{:S(2)}) %collective-permute-start.2) | collective-permute-done | bytes 262176 | tf_op jit(solution)/shard_map/ppermute | solution.py:279
  (96 shorter events, 36.3 us)
Async XLA Ops:
  0.6 11.6 %copy-start = (bf16[64,16,1024]{2,1,0:T(8,128)(2,1)S(1)}, bf16[64,16,1024]{2,1,0:T(8,128)(2,1)}, u32[]{:S(2)}) copy-start(bf16[64,16,1024]{2,1,0:T(8,128)(2,1)} %param.11) | copy-start | bytes 6291460
  0.7 11.3 %copy-start.12 = (s32[2048]{0:T(1024)S(1)}, s32[2048]{0:T(1024)}, u32[]{:S(2)}) copy-start(s32[2048]{0:T(1024)} %param.13) | copy-start | bytes 24580
  0.7 19.8 %copy-start.2 = (s32[64]{0:T(128)S(1)}, s32[64]{0:T(128)}, u32[]{:S(2)}) copy-start(s32[64]{0:T(128)} %param.14) | copy-start | bytes 772
  4.9 85.7 %collective-permute-start = (bf16[512,3584]{1,0:T(8,128)(2,1)}, bf16[512,3584]{1,0:T(8,128)(2,1)}, u32[]{:S(2)}, u32[]{:S(2)}) collective-permute-start(bf16[512,3584]{1,0:T(8,128)(2,1)} %param.9), channel_id=1, source_target_pairs={{0,4},{4,0},{8,12},{12,8},{1,5},{5,1},{9,13},{13,9},{2,6},{6,2},{1... | collective-permute-start | bytes 11010056 | tf_op jit(solution)/shard_map/ppermute | solution.py:213
  8.0 92.0 %collective-permute-start.4 = (bf16[512,3584]{1,0:T(8,128)(2,1)}, bf16[512,3584]{1,0:T(8,128)(2,1)}, u32[]{:S(2)}, u32[]{:S(2)}) collective-permute-start(bf16[512,3584]{1,0:T(8,128)(2,1)} %param.9), channel_id=1, source_target_pairs={{0,16},{16,0},{1,17},{17,1},{2,18},{18,2},{3,19},{19,3},{4,20},{20... | collective-permute-start | bytes 11010056 | tf_op jit(solution)/shard_map/ppermute | solution.py:214
  9.5 106.4 %collective-permute-start.3 = (bf16[512,3584]{1,0:T(8,128)(2,1)}, bf16[512,3584]{1,0:T(8,128)(2,1)}, u32[]{:S(2)}, u32[]{:S(2)}) collective-permute-start(bf16[512,3584]{1,0:T(8,128)(2,1)} %constant_dynamic-slice_fusion.4), channel_id=1, source_target_pairs={{4,8},{8,4},{5,9},{9,5},{6,10},{10,6},{7,11},{11,7},{20,24},{24,20... | collective-permute-start | bytes 11010056 | tf_op jit(solution)/shard_map/ppermute | solution.py:212
  13.5 11.5 %all-to-all-start = ((bf16[4,16,1024]{2,1,0:T(8,128)(2,1)}), bf16[4,16,1024]{2,1,0:T(8,128)(2,1)S(1)}, u32[]{:S(2)}, u32[]{:S(2)}) async-start(bf16[4,16,1024]{2,1,0:T(8,128)(2,1)} %gather_fusion.2), calls=%async_computation | async-start | bytes 262144 | tf_op jit(solution)/shard_map/all_to_all | solution.py:219
  21.1 4.7 %copy-start.3 = (bf16[128,4096]{1,0:T(8,128)(2,1)S(1)}, bf16[128,4096]{1,0:T(8,128)(2,1)}, u32[]{:S(2)}) copy-start(bf16[128,4096]{1,0:T(8,128)(2,1)} %param.8) | copy-start | bytes 3145732
  26.8 7.2 %all-to-all-start.1 = ((bf16[4,32,128]{2,1,0:T(8,128)(2,1)}), bf16[4,32,128]{2,1,0:T(8,128)(2,1)S(1)}, u32[]{:S(2)}, u32[]{:S(2)}) async-start(bf16[4,32,128]{2,1,0:T(8,128)(2,1)} %pad_maximum_fusion.6), calls=%async_computation.1 | async-start | bytes 65536 | tf_op jit(solution)/shard_map/all_to_all | solution.py:225
  35.5 7.9 %all-to-all-start.2 = ((bf16[16,4,1024]{2,0,1:T(8,128)(2,1)}), bf16[16,4,1024]{2,0,1:T(8,128)(2,1)S(1)}, u32[]{:S(2)}, u32[]{:S(2)}) async-start(bf16[16,4,1024]{2,0,1:T(8,128)(2,1)} %bitcast.92), calls=%async_computation.2 | async-start | bytes 262144 | tf_op jit(solution)/shard_map/all_to_all | solution.py:242
  43.5 47.2 %collective-permute-start.1 = (bf16[4,16,1152]{2,1,0:T(8,128)(2,1)S(1)}, bf16[4,16,1152]{2,1,0:T(8,128)(2,1)S(1)}, u32[]{:S(2)}, u32[]{:S(2)}) collective-permute-start(bf16[4,16,1152]{2,1,0:T(8,128)(2,1)S(1)} %pad_maximum_fusion.5), channel_id=1, source_target_pairs={{0,4},{4,0},{8,12},{12,8},{1,5},{5,1},{9,13},{13,9},{2,6},{6,2},{1... | collective-permute-start | bytes 442376 | tf_op jit(solution)/shard_map/ppermute | solution.py:248
  93.4 90.3 %collective-permute-start.5 = (bf16[512,3584]{1,0:T(8,128)(2,1)}, bf16[512,3584]{1,0:T(8,128)(2,1)}, u32[]{:S(2)}, u32[]{:S(2)}) collective-permute-start(bf16[512,3584]{1,0:T(8,128)(2,1)} %constant_dynamic-slice_fusion.4), channel_id=1, source_target_pairs={{0,8},{12,4},{1,9},{13,5},{2,10},{14,6},{3,11},{15,7},{16,24},{28,... | collective-permute-start | bytes 11010056 | tf_op jit(solution)/shard_map/ppermute | solution.py:258
  99.9 95.5 %collective-permute-start.10 = (bf16[512,3584]{1,0:T(8,128)(2,1)}, bf16[512,3584]{1,0:T(8,128)(2,1)}, u32[]{:S(2)}, u32[]{:S(2)}) collective-permute-start(bf16[512,3584]{1,0:T(8,128)(2,1)} %collective-permute-done), channel_id=1, source_target_pairs={{0,16},{16,0},{1,17},{17,1},{2,18},{18,2},{3,19},{19,3},{4,20},{20... | collective-permute-start | bytes 11010056 | tf_op jit(solution)/shard_map/ppermute | solution.py:259
  152.2 29.3 %all-to-all-start.3 = ((bf16[4,2,128,1024]{3,2,1,0:T(8,128)(2,1)}), bf16[4,2,128,1024]{3,2,1,0:T(8,128)(2,1)S(1)}, u32[]{:S(2)}, u32[]{:S(2)}) async-start(bf16[4,2,128,1024]{3,2,1,0:T(8,128)(2,1)} %shard_map.103), calls=%async_computation.3 | async-start | bytes 4194304 | tf_op jit(solution)/shard_map/all_to_all | solution.py:173
  182.8 12.6 %collective-permute-start.11 = (bf16[4,16,4608]{2,1,0:T(8,128)(2,1)S(1)}, bf16[4,16,4608]{2,1,0:T(8,128)(2,1)S(1)}, u32[]{:S(2)}, u32[]{:S(2)}) collective-permute-start(bf16[4,16,4608]{2,1,0:T(8,128)(2,1)S(1)} %pad_maximum_fusion.refs_0_), channel_id=1, source_target_pairs={{4,8},{8,4},{5,9},{9,5},{6,10},{10,6},{7,11},{11,7},{20,24},{24,20... | collective-permute-start | bytes 1769480 | tf_op jit(solution)/shard_map/ppermute | solution.py:269
  195.4 10.1 %copy-start.13 = (s32[64]{0:T(128)S(1)}, s32[64]{0:T(128)}, u32[]{:S(2)}) copy-start(s32[64]{0:T(128)} %param.15) | copy-start | bytes 772
  205.3 5.8 %copy-start.9 = (bf16[2,3,128,512]{3,2,1,0:T(8,128)(2,1)S(1)}, bf16[2,3,128,512]{3,2,1,0:T(8,128)(2,1)}, u32[]{:S(2)}) copy-start(bf16[2,3,128,512]{3,2,1,0:T(8,128)(2,1)} %get-tuple-element.23) | copy-start | bytes 2359300
  205.4 2.3 collective-permute-start.12
  205.6 5.5 %collective-permute-start.6 = (bf16[2,3,128,512]{3,2,1,0:T(8,128)(2,1)}, bf16[2,3,128,512]{3,2,1,0:T(8,128)(2,1)}, u32[]{:S(2)}, u32[]{:S(2)}) collective-permute-start(bf16[2,3,128,512]{3,2,1,0:T(8,128)(2,1)} %get-tuple-element.24), channel_id=1, source_target_pairs={{0,1},{1,0},{2,3},{3,2},{4,5},{5,4},{6,7},{7,6},{8,9},{9,8},{10,11... | collective-permute-start | bytes 2359304 | tf_op jit(solution)/shard_map/ppermute | solution.py:166
  206.8 11.8 %collective-permute-start.15 = (bf16[4,16,4608]{2,1,0:T(8,128)(2,1)S(1)}, bf16[4,16,4608]{2,1,0:T(8,128)(2,1)S(1)}, u32[]{:S(2)}, u32[]{:S(2)}) collective-permute-start(bf16[4,16,4608]{2,1,0:T(8,128)(2,1)S(1)} %pad_maximum_fusion.1.refs_1_), channel_id=1, source_target_pairs={{4,8},{8,4},{5,9},{9,5},{6,10},{10,6},{7,11},{11,7},{20,24},{24,20... | collective-permute-start | bytes 1769480 | tf_op jit(solution)/shard_map/ppermute | solution.py:270
  210.8 9.5 %collective-permute-start.13 = (bf16[1,128,1024]{2,1,0:T(8,128)(2,1)}, bf16[1,128,1024]{2,1,0:T(8,128)(2,1)}, u32[]{:S(2)}, u32[]{:S(2)}) collective-permute-start(bf16[1,128,1024]{2,1,0:T(8,128)(2,1)} %fusion.9), channel_id=1, source_target_pairs={{0,2},{2,0},{1,3},{3,1},{4,6},{6,4},{5,7},{7,5},{8,10},{10,8},{9,1... | collective-permute-start | bytes 786440 | tf_op jit(solution)/shard_map/ppermute | solution.py:168
  215.5 12.3 %collective-permute-start.7 = (bf16[3,128,512]{2,1,0:T(8,128)(2,1)}, bf16[3,128,512]{2,1,0:T(8,128)(2,1)}, u32[]{:S(2)}, u32[]{:S(2)}) collective-permute-start(bf16[3,128,512]{2,1,0:T(8,128)(2,1)} %fusion.7), channel_id=1, source_target_pairs={{0,2},{2,0},{1,3},{3,1},{4,6},{6,4},{5,7},{7,5},{8,10},{10,8},{9,1... | collective-permute-start | bytes 1179656 | tf_op jit(solution)/shard_map/ppermute | solution.py:168
  217.3 19.0 %collective-permute-start.16 = (bf16[4,16,4608]{2,1,0:T(8,128)(2,1)S(1)}, bf16[4,16,4608]{2,1,0:T(8,128)(2,1)S(1)}, u32[]{:S(2)}, u32[]{:S(2)}) collective-permute-start(bf16[4,16,4608]{2,1,0:T(8,128)(2,1)S(1)} %collective-permute-done.11.refs_2_), channel_id=1, source_target_pairs={{4,0},{8,12},{5,1},{9,13},{6,2},{10,14},{7,3},{11,15},{20,16},{24,... | collective-permute-start | bytes 1769480 | tf_op jit(solution)/shard_map/ppermute | solution.py:284
  218.6 30.4 %collective-permute-start.17 = (bf16[4,16,4608]{2,1,0:T(8,128)(2,1)S(1)}, bf16[4,16,4608]{2,1,0:T(8,128)(2,1)S(1)}, u32[]{:S(2)}, u32[]{:S(2)}) collective-permute-start(bf16[4,16,4608]{2,1,0:T(8,128)(2,1)S(1)} %collective-permute-done.15.refs_3_), channel_id=1, source_target_pairs={{4,0},{8,12},{5,1},{9,13},{6,2},{10,14},{7,3},{11,15},{20,16},{24,... | collective-permute-start | bytes 1769480 | tf_op jit(solution)/shard_map/ppermute | solution.py:285
  222.1 33.0 %collective-permute-start.14 = (bf16[128,1024]{1,0:T(8,128)(2,1)}, bf16[128,1024]{1,0:T(8,128)(2,1)}, u32[]{:S(2)}, u32[]{:S(2)}) collective-permute-start(bf16[128,1024]{1,0:T(8,128)(2,1)} %fusion.8), channel_id=1, source_target_pairs={{4,16},{8,28},{20,0},{24,12},{5,17},{9,29},{21,1},{25,13},{6,18},{... | collective-permute-start | bytes 786440 | tf_op jit(solution)/shard_map/ppermute | solution.py:283
  231.8 28.5 %collective-permute-start.8 = (bf16[128,1024]{1,0:T(8,128)(2,1)}, bf16[128,1024]{1,0:T(8,128)(2,1)}, u32[]{:S(2)}, u32[]{:S(2)}) collective-permute-start(bf16[128,1024]{1,0:T(8,128)(2,1)} %get-tuple-element.43), channel_id=1, source_target_pairs={{4,0},{8,12},{5,1},{9,13},{6,2},{10,14},{7,3},{11,15},{20,16},{24,... | collective-permute-start | bytes 786440 | tf_op jit(solution)/shard_map/ppermute | solution.py:281
  233.1 27.2 %collective-permute-start.9 = (bf16[128,1024]{1,0:T(8,128)(2,1)}, bf16[128,1024]{1,0:T(8,128)(2,1)}, u32[]{:S(2)}, u32[]{:S(2)}) collective-permute-start(bf16[128,1024]{1,0:T(8,128)(2,1)} %get-tuple-element.44), channel_id=1, source_target_pairs={{0,16},{16,0},{1,17},{17,1},{2,18},{18,2},{3,19},{19,3},{4,20},{20... | collective-permute-start | bytes 786440 | tf_op jit(solution)/shard_map/ppermute | solution.py:282
  234.9 25.4 %copy-start.4 = (bf16[3,128,512]{2,1,0:T(8,128)(2,1)S(1)}, bf16[3,128,512]{2,1,0:T(8,128)(2,1)}, u32[]{:S(2)}) copy-start(bf16[3,128,512]{2,1,0:T(8,128)(2,1)} %reduce_sum.47) | copy-start | bytes 1179652
  234.9 25.4 %copy-start.6 = (bf16[3,128,512]{2,1,0:T(8,128)(2,1)S(1)}, bf16[3,128,512]{2,1,0:T(8,128)(2,1)}, u32[]{:S(2)}) copy-start(bf16[3,128,512]{2,1,0:T(8,128)(2,1)} %copy-done.5) | copy-start | bytes 1179652
  236.3 28.0 %collective-permute-start.2 = (bf16[128,1024]{1,0:T(8,128)(2,1)S(1)}, bf16[128,1024]{1,0:T(8,128)(2,1)S(1)}, u32[]{:S(2)}, u32[]{:S(2)}) collective-permute-start(bf16[128,1024]{1,0:T(8,128)(2,1)S(1)} %slice_bitcast_fusion.2), channel_id=1, source_target_pairs={{0,4},{4,0},{8,12},{12,8},{1,5},{5,1},{9,13},{13,9},{2,6},{6,2},{1... | collective-permute-start | bytes 786440 | tf_op jit(solution)/shard_map/ppermute | solution.py:279
  255.0 9.2 %copy-start.8 = (bf16[2,128,1024]{2,1,0:T(8,128)(2,1)S(1)}, bf16[2,128,1024]{2,1,0:T(8,128)(2,1)}, u32[]{:S(2)}) copy-start(bf16[2,128,1024]{2,1,0:T(8,128)(2,1)} %reduce_sum.46) | copy-start | bytes 1572868
  261.5 3.0 %copy-start.11 = (bf16[2,8,4,1024]{3,1,2,0:T(8,128)(2,1)S(1)}, bf16[2,8,4,1024]{3,1,2,0:T(8,128)(2,1)}, u32[]{:S(2)}) copy-start(bf16[2,8,4,1024]{3,1,2,0:T(8,128)(2,1)} %copy-done.10) | copy-start | bytes 393220
  (4 other events, 4.3 us)

commit v4 on v3

--- a/solution.py
+++ b/solution.py
@@ -63,82 +63,82 @@
             jax.ShapeDtypeStruct((slot_count, rank, columns - ff_shard), jnp.float32),
         ],
         compiler_params=pltpu.CompilerParams(vmem_limit_bytes=32 * 1024 * 1024),
+        cost_estimate=pl.CostEstimate(
+            flops=0, bytes_accessed=8 * slot_count * rank * columns, transcendentals=0
+        ),
     )(slots, *groups)
 
 
 def terms_kernel(group_count, out_count, place_ref, *refs):
     dy_refs, refs = refs[:group_count], refs[group_count:]
-    *refs, dy_buffer, weight_buffer, dy_sems, weight_sems = refs
+    *refs, dy_buffer, weight_buffer, total, dy_sems, weight_sems = refs
     weight_refs, out_refs = refs[:-out_count], refs[-out_count:]
-    tiles_each = 4 // out_count
     chip, core = place_ref[0], place_ref[1]
-    depth = dy_buffer.shape[-1]
-    starts = [0]
-    for ref in weight_refs:
-        starts.append(starts[-1] + ref.shape[0])
-
-    if out_count == 1:
-        owners = [(0, 0), (0, 1), (1, 0), (1, 1)]
-    else:
-        owners = [(1 - chip, 1 - core), (chip, 1 - core), (1 - chip, core), (chip, core)]
-
-    def start_dy(group, slot):
-        for k, dy_ref in enumerate(dy_refs):
-
-            @pl.when(group == k)
-            def _(dy_ref=dy_ref):
-                for i, (x, c) in enumerate(owners):
-                    pltpu.make_async_copy(
-                        dy_ref.at[x, c],
-                        dy_buffer.at[slot, pl.ds(i * TILE, TILE)],
-                        dy_sems.at[slot],
-                    ).start()
-
-    def wait_dy(slot):
-        whole = dy_buffer.at[slot]
-        pltpu.make_async_copy(whole, whole, dy_sems.at[slot]).wait()
-
-    start_dy(0, 0)
-    for i, (ref, start) in enumerate(zip(weight_refs, starts)):
-        for row in range(0, ref.shape[0], 256):
-            rows = min(256, ref.shape[0] - row)
-            pltpu.make_async_copy(
-                ref.at[pl.ds(row, rows)],
-                weight_buffer.at[pl.ds(start + row, rows)],
-                weight_sems.at[i],
-            ).start()
-
-    def one_group(group, carry):
-        slot = lax.rem(group, 2)
-
-        @pl.when(group + 1 < group_count)
+    rows_group, depth = dy_refs[0].shape
+    step_depth = dy_buffer.shape[-1]
+    steps = depth // step_depth
+    columns = total.shape[1]
+
+    def start(step):
+        slot = lax.rem(step, 2)
+        part = pl.ds(pl.multiple_of(step * step_depth, step_depth), step_depth)
+        for refs, buffer, sems in (
+            (dy_refs, dy_buffer, dy_sems),
+            (weight_refs, weight_buffer, weight_sems),
+        ):
+            row = 0
+            for ref in refs:
+                rows = pl.ds(row, ref.shape[0])
+                pltpu.make_async_copy(
+                    ref.at[:, part], buffer.at[slot, rows], sems.at[slot]
+                ).start()
+                row += ref.shape[0]
+
+    def one_step(step, carry):
+        slot = lax.rem(step, 2)
+
+        @pl.when(step + 1 < steps)
         def _():
-            start_dy(group + 1, 1 - slot)
-
-        wait_dy(slot)
-        dy = dy_buffer[slot]
-
-        @pl.when(group == 0)
-        def _():
-            for i, (start, end) in enumerate(zip(starts[:-1], starts[1:])):
-                whole = weight_buffer.at[pl.ds(start, end - start)]
-                pltpu.make_async_copy(whole, whole, weight_sems.at[i]).wait()
-
-        for column in range(0, starts[-1], 256):
-            stop = min(column + 256, starts[-1])
-            part = dot_last(dy, weight_buffer[column:stop]).astype(jnp.bfloat16)
-            for k in range(4):
-                out_ref = out_refs[k // tiles_each]
-                rows = part[k * TILE : (k + 1) * TILE]
-                out_ref[k % tiles_each, group, :, column:stop] = rows
+            start(step + 1)
+
+        for buffer, sems in ((dy_buffer, dy_sems), (weight_buffer, weight_sems)):
+            whole = buffer.at[slot]
+            pltpu.make_async_copy(whole, whole, sems.at[slot]).wait()
+        for column in range(0, columns, 256):
+            part = dot_last(dy_buffer[slot], weight_buffer[slot, column : column + 256])
+            total[:, column : column + 256] += part
         return carry
 
-    lax.fori_loop(0, group_count, one_group, 0)
+    start(jnp.int32(0))
+    total[...] = jnp.zeros_like(total)
+    lax.fori_loop(0, steps, one_step, 0)
+    for group in range(group_count):
+        for k in range(4):
+            first = group * rows_group + k * TILE
+
+            def tile(first=first):
+                return total[first : first + TILE].astype(jnp.bfloat16)
+
+            if out_count == 1:
+                out_refs[0][k, group] = tile()
+                continue
+            x, c = k // 2, k % 2
+            slot = jnp.where(chip == x, 1, 0)
+
+            @pl.when(core != c)
+            def _(slot=slot, group=group, tile=tile):
+                out_refs[0][slot, group] = tile()
+
+            @pl.when(core == c)
+            def _(slot=slot, group=group, tile=tile):
+                out_refs[1][slot, group] = tile()
 
 
 def product_terms(groups, weights, place, out_count):
-    depth = groups[0].shape[1]
+    rows_group, depth = groups[0].shape
     columns = sum(w.shape[0] for w in weights)
+    rows = rows_group * len(groups)
+    step_depth = 512
     out = jax.ShapeDtypeStruct((4 // out_count, len(groups), TILE, columns), jnp.bfloat16)
     in_hbm = pl.BlockSpec(memory_space=pl.ANY)
     return pl.pallas_call(
@@ -149,23 +149,31 @@
             in_specs=[in_hbm] * (len(groups) + len(weights)),
             out_specs=[pl.BlockSpec(out.shape, lambda i, p: (0, 0, 0, 0))] * out_count,
             scratch_shapes=[
-                pltpu.VMEM((2, 4 * TILE, depth), jnp.bfloat16),
-                pltpu.VMEM((columns, depth), jnp.bfloat16),
+                pltpu.VMEM((2, rows, step_depth), jnp.bfloat16),
+                pltpu.VMEM((2, columns, step_depth), jnp.bfloat16),
+                pltpu.VMEM((rows, columns), jnp.float32),
                 pltpu.SemaphoreType.DMA((2,)),
-                pltpu.SemaphoreType.DMA((len(weights),)),
+                pltpu.SemaphoreType.DMA((2,)),
             ],
         ),
         out_shape=[out] * out_count,
-        compiler_params=pltpu.CompilerParams(vmem_limit_bytes=60 * 1024 * 1024),
+        compiler_params=pltpu.CompilerParams(vmem_limit_bytes=20 * 1024 * 1024),
         cost_estimate=pl.CostEstimate(flops=0, bytes_accessed=0, transcendentals=0),
-    )(place, *[dy.reshape(2, 2, TILE, depth) for dy in groups], *weights)
-
-
-def sum_over_tensor(terms):
-    away, home = terms
-    got = lax.ppermute(away, "tensor", [(0, 1), (1, 0), (2, 3), (3, 2)])
+    )(place, *groups, *weights)
+
+
+def after(value, *events):
+    return lax.optimization_barrier((value,) + events)[0]
+
+
+def from_other_core(away):
+    return lax.ppermute(away, "tensor", [(0, 1), (1, 0), (2, 3), (3, 2)])
+
+
+def sum_of_chips(home, got, *events):
     pair = home.astype(jnp.float32) + got.astype(jnp.float32)
-    got = lax.ppermute(pair[0].astype(jnp.bfloat16), "tensor", [(0, 2), (2, 0), (1, 3), (3, 1)])
+    sent = after(pair[0].astype(jnp.bfloat16), *events)
+    got = lax.ppermute(sent, "tensor", [(0, 2), (2, 0), (1, 3), (3, 1)])
     return (pair[1] + got.astype(jnp.float32)).astype(jnp.bfloat16)
 
 
@@ -205,9 +213,6 @@
     tenants = lax.dynamic_slice_in_dim(all_tenants, z * tile_count, tile_count)
     half = frozen_weight.shape[0] // 2
 
-    def after(value, *events):
-        return lax.optimization_barrier((value,) + events)[0]
-
     crossing = lax.dynamic_slice_in_dim(frozen_weight, rep * half, half, 0)
     near = lax.ppermute(crossing, "dp", MIDDLE)
     partner_dy = lax.ppermute(after(grad_out, crossing), "dp", PARTNER)
@@ -266,23 +271,27 @@
     near_terms = product_terms(groups, [near], place, 1)
     near_sum = sum_by_swap(near_terms)
 
-    near_grads = lax.ppermute(after(tile_grads, own_sum, near_sum), "dp", MIDDLE)
-    far_grads = lax.ppermute(after(partner_grads, own_sum, near_sum), "dp", MIDDLE)
+    near_grads = lax.ppermute(after(tile_grads, near_terms[0]), "dp", MIDDLE)
+    far_grads = lax.ppermute(after(partner_grads, near_terms[0]), "dp", MIDDLE)
+    partner_block = lax.ppermute(own_sum[1], "dp", PARTNER)
 
     groups = [after(grad_out, own_sum, near_sum), partner_dy, other_dy]
     far_terms = product_terms(groups, [far], place, 2)
-    far_sum = sum_over_tensor(far_terms)
     outer_terms = product_terms(
-        [after(partner_other_dy, far_terms[0], near_grads)], [near, far], place, 2
-    )
-    outer_sum = sum_over_tensor(outer_terms)[0]
-    partner_block = lax.ppermute(own_sum[1], "dp", PARTNER)
+        [after(partner_other_dy, far_terms[0], near_grads, partner_block)], [near, far], place, 2
+    )
+    near_grads_out = lax.ppermute(after(near_grads, far_terms[0]), "dp", OUTWARD)
+    outer_got = from_other_core(after(outer_terms[0], far_grads))
+    far_grads_out = lax.ppermute(far_grads, "dp", OUTWARD)
+    far_got = from_other_core(far_terms[0])
+    far_sum = sum_of_chips(far_terms[1], far_got)
+    outer_sum = sum_of_chips(after(outer_terms[1], near_grads_out), outer_got)[0]
     both_sum = jnp.concatenate([near_sum, far_sum], axis=2)
     both_out = lax.ppermute(both_sum[1], "dp", OUTWARD)
     both_other = lax.ppermute(both_sum[2], "rep", OTHER_REP)
-    outer_other = lax.ppermute(outer_sum, ("rep", "dp"), OUTWARD_OTHER_REP)
-    near_grads_out = lax.ppermute(near_grads, "dp", OUTWARD)
-    far_grads_out = lax.ppermute(far_grads, "dp", OUTWARD)
+    outer_other = lax.ppermute(
+        after(outer_sum, far_grads_out), ("rep", "dp"), OUTWARD_OTHER_REP
+    )
 
     mine = jnp.where(inner, both_sum[0], both_out)
     other = jnp.where(inner, both_other, outer_other)

time: 268 us -> 245 us (0.914)
  blocking collectives: 24.5 us -> 0 us
  other arithmetic: 16.6 us -> 12.6 us
  starting transfers between devices: 44.7 us -> 48.2 us
    all_to_all x1 -> x0, blocking collectives: 24.5 us -> none  [sum_by_swap(): lax.all_to_all(terms[0], 'tensor', split_axis=0, concat_axis=0, tiled=True)]
    ppermute x1, waiting for transfers between devices: 9.13 us -> 0.01 us  [line_of_four(): far_grads_out = lax.ppermute(far_grads, 'dp', OUTWARD)]
    ppermute x8, waiting for transfers between devices: 5.25 us -> 11.7 us  [the longest x2 7.22 us: sum_of_chips(): got = lax.ppermute(sent, 'tensor', [(0, 2), (2, 0), (1, 3), (3, 1)])]
    ppermute x1, waiting for transfers between devices: 5.25 us -> 0.01 us  [line_of_four(): both_out = lax.ppermute(both_sum[1], 'dp', OUTWARD)]
    all_to_all x1 -> x2, waiting for transfers between devices: 23.2 us -> 27.7 us  [sum_by_swap(): lax.all_to_all(terms[0], 'tensor', split_axis=0, concat_axis=0, tiled=True)]
    all_to_all x1 -> x2, starting transfers between devices: 3.61 us -> 8.02 us  [sum_by_swap(): lax.all_to_all(terms[0], 'tensor', split_axis=0, concat_axis=0, tiled=True)]
    ppermute x1, waiting for transfers between devices: 0.01 us -> 3.94 us  [line_of_four(): far = lax.ppermute(after(crossing, partner_grads), 'dp', OUTER_TO_MIDDLE)]
    ppermute x1, waiting for transfers between devices: 41.9 us -> 45.7 us  [line_of_four(): from_partner = lax.ppermute(to_partner, 'dp', PARTNER)]
  transfers between devices with their start and end apart: 22 -> 23, of which waited for: 11 -> 9; matrix products, arithmetic and copies ran while one was open for 15% -> 13% of each run, Pallas kernels for 16% -> 22%
where the time goes in v4:
time: 245 us; the launch traced here: 243 us
  waiting for transfers between devices  96.4 us (39%)
  Pallas kernels  52.6 us (21%)
  starting transfers between devices  48.2 us (20%)
  local copies, waits for them, and re-layouts  20.9 us (9%)
  other arithmetic  12.6 us (5%)
  matrix products  11.1 us (5%)
    ppermute x1, waiting for transfers between devices, line_of_four(): from_partner = lax.ppermute(to_partner, 'dp', PARTNER)  45.7 us
    pallas_call x4, Pallas kernels, product_terms(): pl.pallas_call(functools.partial(terms_kernel, len(groups), out_count), g...  45.1 us
    all_to_all x2, waiting for transfers between devices, sum_by_swap(): lax.all_to_all(terms[0], 'tensor', split_axis=0, concat_axis=0, tiled=True)  27.7 us
    all_to_all x2, starting transfers between devices, sum_by_swap(): lax.all_to_all(terms[0], 'tensor', split_axis=0, concat_axis=0, tiled=True)  8.02 us
    pallas_call x1, Pallas kernels, place_in_slots(): pl.pallas_call(place_kernel, grid_spec=pltpu.PrefetchScalarGridSpec(num_s...  7.51 us
    ppermute x2, waiting for transfers between devices, sum_of_chips(): got = lax.ppermute(sent, 'tensor', [(0, 2), (2, 0), (1, 3), (3, 1)])  7.22 us
    ppermute x1, starting transfers between devices, line_of_four(): far = lax.ppermute(after(crossing, partner_grads), 'dp', OUTER_TO_MIDDLE)  6.54 us
    dot_general x2, matrix products, up_gradients(): jnp.einsum('krt,ktf->krf', middle, dy, preferred_element_type=jnp.float32)  5.26 us
  transfers between devices with their start and end apart: 23, of which 9 were waited for; matrix products, arithmetic and copies ran while one was open for 13% of the time, Pallas kernels for 22%

profile of v4, /device:TPU:0, one launch (start us, length us, event | category | flops | bytes accessed | tf_op | source)
XLA Modules:
  0.0 243.0 jit_solution(12063453599228129997)
XLA Ops:
  0.7 4.3 %constant_dynamic-slice_fusion.4 = bf16[512,3584]{1,0:T(8,128)(2,1)} fusion(bf16[1024,3584]{1,0:T(8,128)(2,1)} %refs_2_.1, s32[]{:T(128)S(6)} %select_n.147), kind=kLoop, calls=%fused_computation.75 | loop fusion | bytes 7340036 | tf_op jit(solution)/shard_map/dynamic_slice | solution.py:216
  4.9 3.0 %collective-permute-start = (bf16[512,3584]{1,0:T(8,128)(2,1)}, bf16[512,3584]{1,0:T(8,128)(2,1)}, u32[]{:S(2)}, u32[]{:S(2)}) collective-permute-start(bf16[512,3584]{1,0:T(8,128)(2,1)} %refs_0_.2), channel_id=1, source_target_pairs={{0,4},{4,0},{8,12},{12,8},{1,5},{5,1},{9,13},{13,9},{2,6},{6,2},{1... | collective-permute-start | bytes 11010056 | tf_op jit(solution)/shard_map/ppermute | solution.py:218
  9.5 2.5 %collective-permute-start.3 = (bf16[512,3584]{1,0:T(8,128)(2,1)}, bf16[512,3584]{1,0:T(8,128)(2,1)}, u32[]{:S(2)}, u32[]{:S(2)}) collective-permute-start(bf16[512,3584]{1,0:T(8,128)(2,1)} %constant_dynamic-slice_fusion.4), channel_id=1, source_target_pairs={{4,8},{8,4},{5,9},{9,5},{6,10},{10,6},{7,11},{11,7},{20,24},{24,20... | collective-permute-start | bytes 11010056 | tf_op jit(solution)/shard_map/ppermute | solution.py:217
  13.5 3.3 %all-to-all-start = ((bf16[4,16,1024]{2,1,0:T(8,128)(2,1)}), bf16[4,16,1024]{2,1,0:T(8,128)(2,1)S(1)}, u32[]{:S(2)}, u32[]{:S(2)}) async-start(bf16[4,16,1024]{2,1,0:T(8,128)(2,1)} %gather_fusion.2), calls=%async_computation | async-start | bytes 262144 | tf_op jit(solution)/shard_map/all_to_all | solution.py:224
  16.8 3.7 %gather_fusion.1 = bf16[4,16,3584]{2,1,0:T(8,128)(2,1)S(1)} fusion(bf16[64,16,3584]{2,1,0:T(8,128)(2,1)} %param.12, s32[1024]{0:T(1024)S(1)} %pad_clamp_fusion.2), kind=kCustom, calls=%fused_computation.1 | custom fusion | bytes 917520 | tf_op jit(solution)/shard_map/gather | solution.py:223
  20.5 3.2 %convolution_convert_fusion = bf16[4,16,128]{2,1,0:T(8,128)(2,1)S(1)} fusion(bf16[4,16,3584]{2,1,0:T(8,128)(2,1)S(1)} %gather_fusion.1, bf16[4,128,3584]{2,1,0:T(8,128)(2,1)} %bitcast.3), kind=kOutput, calls=%fused_computation.14 | convolution fusion | flops 58728448 | bytes 4145152 | tf_op jit(solution)/shard_map/krf,ktf->krt/dot_general | solution.py:226
  25.5 3.3 %all-to-all-start.1 = ((bf16[4,32,128]{2,1,0:T(8,128)(2,1)}), bf16[4,32,128]{2,1,0:T(8,128)(2,1)S(1)}, u32[]{:S(2)}, u32[]{:S(2)}) async-start(bf16[4,32,128]{2,1,0:T(8,128)(2,1)} %pad_maximum_fusion.6), calls=%async_computation.1 | async-start | bytes 65536 | tf_op jit(solution)/shard_map/all_to_all | solution.py:230
  29.4 3.3 %all-to-all-done.1 = bf16[4,32,128]{2,1,0:T(8,128)(2,1)S(1)} async-done(((bf16[4,32,128]{2,1,0:T(8,128)(2,1)}), bf16[4,32,128]{2,1,0:T(8,128)(2,1)S(1)}, u32[]{:S(2)}, u32[]{:S(2)}) %all-to-all-start.1) | async-done | bytes 32800 | tf_op jit(solution)/shard_map/all_to_all | solution.py:230
  34.3 3.3 %all-to-all-start.2 = ((bf16[16,4,1024]{2,0,1:T(8,128)(2,1)}), bf16[16,4,1024]{2,0,1:T(8,128)(2,1)S(1)}, u32[]{:S(2)}, u32[]{:S(2)}) async-start(bf16[16,4,1024]{2,0,1:T(8,128)(2,1)} %bitcast.86), calls=%async_computation.2 | async-start | bytes 262144 | tf_op jit(solution)/shard_map/all_to_all | solution.py:247
  38.3 3.9 %all-to-all-done.2 = bf16[16,4,1024]{2,0,1:T(8,128)(2,1)S(1)} async-done(((bf16[16,4,1024]{2,0,1:T(8,128)(2,1)}), bf16[16,4,1024]{2,0,1:T(8,128)(2,1)S(1)}, u32[]{:S(2)}, u32[]{:S(2)}) %all-to-all-start.2) | async-done | bytes 131104 | tf_op jit(solution)/shard_map/all_to_all | solution.py:247
  42.2 2.7 %collective-permute-start.1 = (bf16[4,16,1152]{2,1,0:T(8,128)(2,1)S(1)}, bf16[4,16,1152]{2,1,0:T(8,128)(2,1)S(1)}, u32[]{:S(2)}, u32[]{:S(2)}) collective-permute-start(bf16[4,16,1152]{2,1,0:T(8,128)(2,1)S(1)} %pad_maximum_fusion.5), channel_id=1, source_target_pairs={{0,4},{4,0},{8,12},{12,8},{1,5},{5,1},{9,13},{13,9},{2,6},{6,2},{1... | collective-permute-start | bytes 442376 | tf_op jit(solution)/shard_map/ppermute | solution.py:253
  44.9 45.7 %collective-permute-done.1 = bf16[4,16,1152]{2,1,0:T(8,128)(2,1)S(1)} collective-permute-done((bf16[4,16,1152]{2,1,0:T(8,128)(2,1)S(1)}, bf16[4,16,1152]{2,1,0:T(8,128)(2,1)S(1)}, u32[]{:S(2)}, u32[]{:S(2)}) %collective-permute-start.1) | collective-permute-done | bytes 147488 | tf_op jit(solution)/shard_map/ppermute | solution.py:253
  90.7 2.6 %fusion.1 = bf16[4,16,3584]{2,1,0:T(8,128)(2,1)S(1)} fusion(bf16[4,128,3584]{2,1,0:T(8,128)(2,1)} %bitcast.8, f32[4]{0:T(128)S(1)} %convert_divide_fusion, bf16[4,16,1152]{2,1,0:T(8,128)(2,1)S(1)} %collective-permute-done.1), kind=kOutput, calls=%fused_computation.9 | convolution fusion | flops 59179008 | bytes 4145664 | tf_op jit(solution)/shard_map/krt,ktf->krf/dot_general | solution.py:239
  93.4 6.5 %collective-permute-start.5 = (bf16[512,3584]{1,0:T(8,128)(2,1)}, bf16[512,3584]{1,0:T(8,128)(2,1)}, u32[]{:S(2)}, u32[]{:S(2)}) collective-permute-start(bf16[512,3584]{1,0:T(8,128)(2,1)} %constant_dynamic-slice_fusion.4), channel_id=1, source_target_pairs={{0,8},{12,4},{1,9},{13,5},{2,10},{14,6},{3,11},{15,7},{16,24},{28,... | collective-permute-start | bytes 11010056 | tf_op jit(solution)/shard_map/ppermute | solution.py:263
  101.5 2.6 %fusion = bf16[4,16,3584]{2,1,0:T(8,128)(2,1)S(1)} fusion(bf16[4,128,3584]{2,1,0:T(8,128)(2,1)} %bitcast.3, f32[4]{0:T(128)S(1)} %convert_divide_fusion.1, bf16[4,32,128]{2,1,0:T(8,128)(2,1)S(1)} %all-to-all-done.1), kind=kOutput, calls=%fused_computation.8 | convolution fusion | flops 59179008 | bytes 4145664 | tf_op jit(solution)/shard_map/krt,ktf->krf/dot_general | solution.py:239
  104.2 3.1 %copy-done.2 = bf16[1024,3584]{1,0:T(8,128)(2,1)S(1)} copy-done((bf16[1024,3584]{1,0:T(8,128)(2,1)S(1)}, bf16[1024,3584]{1,0:T(8,128)(2,1)}, u32[]{:S(2)}) %copy-start.2) | copy-done | bytes 7340056
  107.3 12.7 %shard_map.103 = bf16[4,2,128,1024]{3,2,1,0:T(8,128)(2,1)} custom-call(s32[2]{0:T(128)S(1)} %pad_add_fusion.place_ref, bf16[512,3584]{1,0:T(8,128)(2,1)} %refs_0_.2, bf16[512,3584]{1,0:T(8,128)(2,1)} %collective-permute-done.refs_1_, bf16[1024,3584]{1,0:T(8,128)(2,1)S(1)} %copy-done.2), custom_call_target="tpu_custom_call" | custom-call | tf_op jit(solution)/shard_map/pallas_call | solution.py:144
  119.9 4.5 %all-to-all-start.3 = ((bf16[4,2,128,1024]{3,2,1,0:T(8,128)(2,1)}), bf16[4,2,128,1024]{3,2,1,0:T(8,128)(2,1)}, u32[]{:S(2)}, u32[]{:S(2)}) async-start(bf16[4,2,128,1024]{3,2,1,0:T(8,128)(2,1)} %shard_map.103), calls=%async_computation.3 | async-start | bytes 4194304 | tf_op jit(solution)/shard_map/all_to_all | solution.py:181
  124.4 12.2 %shard_map.104 = bf16[4,3,128,512]{3,2,1,0:T(8,128)(2,1)} custom-call(s32[2]{0:T(128)S(1)} %pad_add_fusion.place_ref, bf16[512,3584]{1,0:T(8,128)(2,1)} %refs_0_.2, bf16[512,3584]{1,0:T(8,128)(2,1)} %collective-permute-done.refs_1_, bf16[512,3584]{1,0:T(8,128)(2,1)} %collective-permute-done.4.refs_2_, bf16[512,3584]{1,0:T(8,128)(2,1)} %collective-permute-done.3.refs_3_.refs_1_), custom_call_target="tpu_custom_call" | custom-call | tf_op jit(solution)/shard_map/pallas_call | solution.py:144
  136.6 13.6 %all-to-all-done.3 = bf16[4,2,128,1024]{3,2,1,0:T(8,128)(2,1)} async-done(((bf16[4,2,128,1024]{3,2,1,0:T(8,128)(2,1)}), bf16[4,2,128,1024]{3,2,1,0:T(8,128)(2,1)}, u32[]{:S(2)}, u32[]{:S(2)}) %all-to-all-start.3) | async-done | bytes 2097184 | tf_op jit(solution)/shard_map/all_to_all | solution.py:181
  150.2 3.6 %all-to-all-start.4 = ((bf16[4,3,128,512]{3,2,1,0:T(8,128)(2,1)}), bf16[4,3,128,512]{3,2,1,0:T(8,128)(2,1)S(1)}, u32[]{:S(2)}, u32[]{:S(2)}) async-start(bf16[4,3,128,512]{3,2,1,0:T(8,128)(2,1)} %shard_map.104), calls=%async_computation.4 | async-start | bytes 3145728 | tf_op jit(solution)/shard_map/all_to_all | solution.py:181
  156.7 2.0 reduce_sum.46
  159.6 14.2 %all-to-all-done.4 = bf16[4,3,128,512]{3,2,1,0:T(8,128)(2,1)S(1)} async-done(((bf16[4,3,128,512]{3,2,1,0:T(8,128)(2,1)}), bf16[4,3,128,512]{3,2,1,0:T(8,128)(2,1)S(1)}, u32[]{:S(2)}, u32[]{:S(2)}) %all-to-all-start.4) | async-done | bytes 1572896 | tf_op jit(solution)/shard_map/all_to_all | solution.py:181
  174.2 3.9 %collective-permute-done.5.refs_3_.refs_2_ = bf16[512,3584]{1,0:T(8,128)(2,1)} collective-permute-done((bf16[512,3584]{1,0:T(8,128)(2,1)}, bf16[512,3584]{1,0:T(8,128)(2,1)}, u32[]{:S(2)}, u32[]{:S(2)}) %collective-permute-start.5) | collective-permute-done | bytes 3670048 | tf_op jit(solution)/shard_map/ppermute | solution.py:263
  178.2 11.0 %shard_map.105 = (bf16[2,3,128,512]{3,2,1,0:T(8,128)(2,1)S(1)}, bf16[2,3,128,512]{3,2,1,0:T(8,128)(2,1)S(1)}) custom-call(s32[2]{0:T(128)S(1)} %pad_add_fusion.place_ref, bf16[512,3584]{1,0:T(8,128)(2,1)} %refs_0_.2, bf16[512,3584]{1,0:T(8,128)(2,1)} %collective-permute-done.refs_1_, bf16[512,3584]{1,0:T(8,128)(2,1)} %collective-permute-done.4.refs_2_, ...), custom_call_target="tpu_custom_call" | custom-call | tf_op jit(solution)/shard_map/pallas_call | solution.py:144
  190.5 9.2 %shard_map.106 = (bf16[2,1,128,1024]{3,2,1,0:T(8,128)(2,1)S(1)}, bf16[2,1,128,1024]{3,2,1,0:T(8,128)(2,1)S(1)}) custom-call(s32[2]{0:T(128)S(1)} %pad_add_fusion.place_ref, bf16[512,3584]{1,0:T(8,128)(2,1)} %collective-permute-done.10.refs_0_, bf16[512,3584]{1,0:T(8,128)(2,1)} %collective-permute-done.3.refs_3_.refs_1_, ...), custom_call_target="tpu_custom_call" | custom-call | tf_op jit(solution)/shard_map/pallas_call | solution.py:144
  201.8 4.5 %collective-permute-done.12.refs_4_ = bf16[4,16,4608]{2,1,0:T(8,128)(2,1)S(1)} collective-permute-done((bf16[4,16,4608]{2,1,0:T(8,128)(2,1)}, bf16[4,16,4608]{2,1,0:T(8,128)(2,1)S(1)}, u32[]{:S(2)}, u32[]{:S(2)}) %collective-permute-start.12) | collective-permute-done | bytes 589856 | tf_op jit(solution)/shard_map/ppermute | solution.py:283
  207.5 1.8 fusion.9
  214.6 4.1 %collective-permute-done.15 = bf16[1,128,1024]{2,1,0:T(8,128)(2,1)} collective-permute-done((bf16[1,128,1024]{2,1,0:T(8,128)(2,1)}, bf16[1,128,1024]{2,1,0:T(8,128)(2,1)}, u32[]{:S(2)}, u32[]{:S(2)}) %collective-permute-start.15) | collective-permute-done | bytes 262176 | tf_op jit(solution)/shard_map/ppermute | solution.py:176
  218.7 1.9 fusion.8
  221.8 3.2 %collective-permute-done.7 = bf16[3,128,512]{2,1,0:T(8,128)(2,1)S(1)} collective-permute-done((bf16[3,128,512]{2,1,0:T(8,128)(2,1)S(1)}, bf16[3,128,512]{2,1,0:T(8,128)(2,1)S(1)}, u32[]{:S(2)}, u32[]{:S(2)}) %collective-permute-start.7) | collective-permute-done | bytes 393248 | tf_op jit(solution)/shard_map/ppermute | solution.py:176
  231.0 7.5 %shard_map.107 = (f32[32,16,3584]{2,1,0:T(8,128)}, f32[32,16,1024]{2,1,0:T(8,128)}) custom-call(s32[24]{0:T(128)S(1)} %concatenate.35.slots_ref, bf16[4,16,4608]{2,1,0:T(8,128)(2,1)S(1)} %pad_maximum_fusion.refs_0_, bf16[4,16,4608]{2,1,0:T(8,128)(2,1)S(1)} %pad_maximum_fusion.1.refs_1_, bf16[4,16,4608]{2,1,0:T(8,128)(2,1)} %collective-permute-done.11.refs_2_, ...), custom_call_target="tpu_custom_call" | custom-call | bytes 18874368 | tf_op jit(solution)/shard_map/pallas_call | solution.py:49
  (99 shorter events, 35.2 us)
Async XLA Ops:
  0.6 11.6 %copy-start = (bf16[64,16,1024]{2,1,0:T(8,128)(2,1)S(1)}, bf16[64,16,1024]{2,1,0:T(8,128)(2,1)}, u32[]{:S(2)}) copy-start(bf16[64,16,1024]{2,1,0:T(8,128)(2,1)} %param.11) | copy-start | bytes 6291460
  0.7 11.3 %copy-start.13 = (s32[2048]{0:T(1024)S(1)}, s32[2048]{0:T(1024)}, u32[]{:S(2)}) copy-start(s32[2048]{0:T(1024)} %param.13) | copy-start | bytes 24580
  4.9 85.7 %collective-permute-start = (bf16[512,3584]{1,0:T(8,128)(2,1)}, bf16[512,3584]{1,0:T(8,128)(2,1)}, u32[]{:S(2)}, u32[]{:S(2)}) collective-permute-start(bf16[512,3584]{1,0:T(8,128)(2,1)} %refs_0_.2), channel_id=1, source_target_pairs={{0,4},{4,0},{8,12},{12,8},{1,5},{5,1},{9,13},{13,9},{2,6},{6,2},{1... | collective-permute-start | bytes 11010056 | tf_op jit(solution)/shard_map/ppermute | solution.py:218
  8.0 92.0 %collective-permute-start.4 = (bf16[512,3584]{1,0:T(8,128)(2,1)}, bf16[512,3584]{1,0:T(8,128)(2,1)}, u32[]{:S(2)}, u32[]{:S(2)}) collective-permute-start(bf16[512,3584]{1,0:T(8,128)(2,1)} %refs_0_.2), channel_id=1, source_target_pairs={{0,16},{16,0},{1,17},{17,1},{2,18},{18,2},{3,19},{19,3},{4,20},{20... | collective-permute-start | bytes 11010056 | tf_op jit(solution)/shard_map/ppermute | solution.py:219
  9.5 114.9 %collective-permute-start.3 = (bf16[512,3584]{1,0:T(8,128)(2,1)}, bf16[512,3584]{1,0:T(8,128)(2,1)}, u32[]{:S(2)}, u32[]{:S(2)}) collective-permute-start(bf16[512,3584]{1,0:T(8,128)(2,1)} %constant_dynamic-slice_fusion.4), channel_id=1, source_target_pairs={{4,8},{8,4},{5,9},{9,5},{6,10},{10,6},{7,11},{11,7},{20,24},{24,20... | collective-permute-start | bytes 11010056 | tf_op jit(solution)/shard_map/ppermute | solution.py:217
  13.5 10.9 %all-to-all-start = ((bf16[4,16,1024]{2,1,0:T(8,128)(2,1)}), bf16[4,16,1024]{2,1,0:T(8,128)(2,1)S(1)}, u32[]{:S(2)}, u32[]{:S(2)}) async-start(bf16[4,16,1024]{2,1,0:T(8,128)(2,1)} %gather_fusion.2), calls=%async_computation | async-start | bytes 262144 | tf_op jit(solution)/shard_map/all_to_all | solution.py:224
  20.5 4.0 %copy-start.6 = (bf16[128,4096]{1,0:T(8,128)(2,1)S(1)}, bf16[128,4096]{1,0:T(8,128)(2,1)}, u32[]{:S(2)}) copy-start(bf16[128,4096]{1,0:T(8,128)(2,1)} %param.8) | copy-start | bytes 3145732
  25.5 7.2 %all-to-all-start.1 = ((bf16[4,32,128]{2,1,0:T(8,128)(2,1)}), bf16[4,32,128]{2,1,0:T(8,128)(2,1)S(1)}, u32[]{:S(2)}, u32[]{:S(2)}) async-start(bf16[4,32,128]{2,1,0:T(8,128)(2,1)} %pad_maximum_fusion.6), calls=%async_computation.1 | async-start | bytes 65536 | tf_op jit(solution)/shard_map/all_to_all | solution.py:230
  34.3 7.9 %all-to-all-start.2 = ((bf16[16,4,1024]{2,0,1:T(8,128)(2,1)}), bf16[16,4,1024]{2,0,1:T(8,128)(2,1)S(1)}, u32[]{:S(2)}, u32[]{:S(2)}) async-start(bf16[16,4,1024]{2,0,1:T(8,128)(2,1)} %bitcast.86), calls=%async_computation.2 | async-start | bytes 262144 | tf_op jit(solution)/shard_map/all_to_all | solution.py:247
  42.2 48.4 %collective-permute-start.1 = (bf16[4,16,1152]{2,1,0:T(8,128)(2,1)S(1)}, bf16[4,16,1152]{2,1,0:T(8,128)(2,1)S(1)}, u32[]{:S(2)}, u32[]{:S(2)}) collective-permute-start(bf16[4,16,1152]{2,1,0:T(8,128)(2,1)S(1)} %pad_maximum_fusion.5), channel_id=1, source_target_pairs={{0,4},{4,0},{8,12},{12,8},{1,5},{5,1},{9,13},{13,9},{2,6},{6,2},{1... | collective-permute-start | bytes 442376 | tf_op jit(solution)/shard_map/ppermute | solution.py:253
  93.4 84.8 %collective-permute-start.5 = (bf16[512,3584]{1,0:T(8,128)(2,1)}, bf16[512,3584]{1,0:T(8,128)(2,1)}, u32[]{:S(2)}, u32[]{:S(2)}) collective-permute-start(bf16[512,3584]{1,0:T(8,128)(2,1)} %constant_dynamic-slice_fusion.4), channel_id=1, source_target_pairs={{0,8},{12,4},{1,9},{13,5},{2,10},{14,6},{3,11},{15,7},{16,24},{28,... | collective-permute-start | bytes 11010056 | tf_op jit(solution)/shard_map/ppermute | solution.py:263
  100.0 90.6 %collective-permute-start.10 = (bf16[512,3584]{1,0:T(8,128)(2,1)}, bf16[512,3584]{1,0:T(8,128)(2,1)}, u32[]{:S(2)}, u32[]{:S(2)}) collective-permute-start(bf16[512,3584]{1,0:T(8,128)(2,1)} %collective-permute-done.refs_1_), channel_id=1, source_target_pairs={{0,16},{16,0},{1,17},{17,1},{2,18},{18,2},{3,19},{19,3},{4,20},{20... | collective-permute-start | bytes 11010056 | tf_op jit(solution)/shard_map/ppermute | solution.py:264
  119.9 30.2 %all-to-all-start.3 = ((bf16[4,2,128,1024]{3,2,1,0:T(8,128)(2,1)}), bf16[4,2,128,1024]{3,2,1,0:T(8,128)(2,1)}, u32[]{:S(2)}, u32[]{:S(2)}) async-start(bf16[4,2,128,1024]{3,2,1,0:T(8,128)(2,1)} %shard_map.103), calls=%async_computation.3 | async-start | bytes 4194304 | tf_op jit(solution)/shard_map/all_to_all | solution.py:181
  150.2 23.6 %all-to-all-start.4 = ((bf16[4,3,128,512]{3,2,1,0:T(8,128)(2,1)}), bf16[4,3,128,512]{3,2,1,0:T(8,128)(2,1)S(1)}, u32[]{:S(2)}, u32[]{:S(2)}) async-start(bf16[4,3,128,512]{3,2,1,0:T(8,128)(2,1)} %shard_map.104), calls=%async_computation.4 | async-start | bytes 3145728 | tf_op jit(solution)/shard_map/all_to_all | solution.py:181
  153.7 35.5 %collective-permute-start.11 = (bf16[4,16,4608]{2,1,0:T(8,128)(2,1)S(1)}, bf16[4,16,4608]{2,1,0:T(8,128)(2,1)}, u32[]{:S(2)}, u32[]{:S(2)}) collective-permute-start(bf16[4,16,4608]{2,1,0:T(8,128)(2,1)S(1)} %pad_maximum_fusion.refs_0_), channel_id=1, source_target_pairs={{4,8},{8,4},{5,9},{9,5},{6,10},{10,6},{7,11},{11,7},{20,24},{24,20... | collective-permute-start | bytes 1769480 | tf_op jit(solution)/shard_map/ppermute | solution.py:274
  155.2 44.5 %collective-permute-start.13 = (bf16[4,16,4608]{2,1,0:T(8,128)(2,1)S(1)}, bf16[4,16,4608]{2,1,0:T(8,128)(2,1)}, u32[]{:S(2)}, u32[]{:S(2)}) collective-permute-start(bf16[4,16,4608]{2,1,0:T(8,128)(2,1)S(1)} %pad_maximum_fusion.1.refs_1_), channel_id=1, source_target_pairs={{4,8},{8,4},{5,9},{9,5},{6,10},{10,6},{7,11},{11,7},{20,24},{24,20... | collective-permute-start | bytes 1769480 | tf_op jit(solution)/shard_map/ppermute | solution.py:275
  159.5 31.0 %collective-permute-start.2 = (bf16[128,1024]{1,0:T(8,128)(2,1)}, bf16[128,1024]{1,0:T(8,128)(2,1)}, u32[]{:S(2)}, u32[]{:S(2)}) collective-permute-start(bf16[128,1024]{1,0:T(8,128)(2,1)} %slice_bitcast_fusion.2), channel_id=1, source_target_pairs={{0,4},{4,0},{8,12},{12,8},{1,5},{5,1},{9,13},{13,9},{2,6},{6,2},{1... | collective-permute-start | bytes 786440 | tf_op jit(solution)/shard_map/ppermute | solution.py:276
  174.2 52.0 %copy-start.7 = (bf16[3,128,512]{2,1,0:T(8,128)(2,1)}, bf16[3,128,512]{2,1,0:T(8,128)(2,1)S(1)}, u32[]{:S(2)}) copy-start(bf16[3,128,512]{2,1,0:T(8,128)(2,1)S(1)} %reduce_sum.47) | copy-start | bytes 1179652
  189.2 11.1 %copy-start.14 = (s32[64]{0:T(128)S(1)}, s32[64]{0:T(128)}, u32[]{:S(2)}) copy-start(s32[64]{0:T(128)} %param.15) | copy-start | bytes 772
  189.2 17.1 %collective-permute-start.12 = (bf16[4,16,4608]{2,1,0:T(8,128)(2,1)}, bf16[4,16,4608]{2,1,0:T(8,128)(2,1)S(1)}, u32[]{:S(2)}, u32[]{:S(2)}) collective-permute-start(bf16[4,16,4608]{2,1,0:T(8,128)(2,1)} %collective-permute-done.11.refs_2_), channel_id=1, source_target_pairs={{4,0},{8,12},{5,1},{9,13},{6,2},{10,14},{7,3},{11,15},{20,16},{24,... | collective-permute-start | bytes 1769480 | tf_op jit(solution)/shard_map/ppermute | solution.py:283
  199.8 6.6 %collective-permute-start.14 = (bf16[2,1,128,1024]{3,2,1,0:T(8,128)(2,1)S(1)}, bf16[2,1,128,1024]{3,2,1,0:T(8,128)(2,1)S(1)}, u32[]{:S(2)}, u32[]{:S(2)}) collective-permute-start(bf16[2,1,128,1024]{3,2,1,0:T(8,128)(2,1)S(1)} %get-tuple-element.37), channel_id=1, source_target_pairs={{0,1},{1,0},{2,3},{3,2},{4,5},{5,4},{6,7},{7,6},{8,9},{9,8},{10,11... | collective-permute-start | bytes 1572872 | tf_op jit(solution)/shard_map/ppermute | solution.py:170
  199.9 10.9 %collective-permute-start.6 = (bf16[2,3,128,512]{3,2,1,0:T(8,128)(2,1)S(1)}, bf16[2,3,128,512]{3,2,1,0:T(8,128)(2,1)S(1)}, u32[]{:S(2)}, u32[]{:S(2)}) collective-permute-start(bf16[2,3,128,512]{3,2,1,0:T(8,128)(2,1)S(1)} %get-tuple-element.28), channel_id=1, source_target_pairs={{0,1},{1,0},{2,3},{3,2},{4,5},{5,4},{6,7},{7,6},{8,9},{9,8},{10,11... | collective-permute-start | bytes 2359304 | tf_op jit(solution)/shard_map/ppermute | solution.py:170
  200.5 20.0 %collective-permute-start.16 = (bf16[4,16,4608]{2,1,0:T(8,128)(2,1)}, bf16[4,16,4608]{2,1,0:T(8,128)(2,1)}, u32[]{:S(2)}, u32[]{:S(2)}) collective-permute-start(bf16[4,16,4608]{2,1,0:T(8,128)(2,1)} %collective-permute-done.13.refs_3_), channel_id=1, source_target_pairs={{4,0},{8,12},{5,1},{9,13},{6,2},{10,14},{7,3},{11,15},{20,16},{24,... | collective-permute-start | bytes 1769480 | tf_op jit(solution)/shard_map/ppermute | solution.py:285
  206.3 5.8 %copy-start.3 = (bf16[4,16,4608]{2,1,0:T(8,128)(2,1)}, bf16[4,16,4608]{2,1,0:T(8,128)(2,1)S(1)}, u32[]{:S(2)}) copy-start(bf16[4,16,4608]{2,1,0:T(8,128)(2,1)S(1)} %collective-permute-done.12.refs_4_) | copy-start | bytes 1769476
  209.3 9.4 %collective-permute-start.15 = (bf16[1,128,1024]{2,1,0:T(8,128)(2,1)}, bf16[1,128,1024]{2,1,0:T(8,128)(2,1)}, u32[]{:S(2)}, u32[]{:S(2)}) collective-permute-start(bf16[1,128,1024]{2,1,0:T(8,128)(2,1)} %fusion.9), channel_id=1, source_target_pairs={{0,2},{2,0},{1,3},{3,1},{4,6},{6,4},{5,7},{7,5},{8,10},{10,8},{9,1... | collective-permute-start | bytes 786440 | tf_op jit(solution)/shard_map/ppermute | solution.py:176
  213.3 11.7 %collective-permute-start.7 = (bf16[3,128,512]{2,1,0:T(8,128)(2,1)S(1)}, bf16[3,128,512]{2,1,0:T(8,128)(2,1)S(1)}, u32[]{:S(2)}, u32[]{:S(2)}) collective-permute-start(bf16[3,128,512]{2,1,0:T(8,128)(2,1)S(1)} %fusion.7), channel_id=1, source_target_pairs={{0,2},{2,0},{1,3},{3,1},{4,6},{6,4},{5,7},{7,5},{8,10},{10,8},{9,1... | collective-permute-start | bytes 1179656 | tf_op jit(solution)/shard_map/ppermute | solution.py:176
  214.6 16.5 %copy-start.4 = (bf16[4,16,4608]{2,1,0:T(8,128)(2,1)S(1)}, bf16[4,16,4608]{2,1,0:T(8,128)(2,1)}, u32[]{:S(2)}) copy-start(bf16[4,16,4608]{2,1,0:T(8,128)(2,1)} %copy-done.3) | copy-start | bytes 1769476
  220.5 18.0 %collective-permute-start.17 = (bf16[128,1024]{1,0:T(8,128)(2,1)}, bf16[128,1024]{1,0:T(8,128)(2,1)}, u32[]{:S(2)}, u32[]{:S(2)}) collective-permute-start(bf16[128,1024]{1,0:T(8,128)(2,1)} %fusion.8), channel_id=1, source_target_pairs={{4,16},{8,28},{20,0},{24,12},{5,17},{9,29},{21,1},{25,13},{6,18},{... | collective-permute-start | bytes 786440 | tf_op jit(solution)/shard_map/ppermute | solution.py:292
  227.8 10.7 %copy-start.8 = (bf16[3,128,512]{2,1,0:T(8,128)(2,1)S(1)}, bf16[3,128,512]{2,1,0:T(8,128)(2,1)}, u32[]{:S(2)}) copy-start(bf16[3,128,512]{2,1,0:T(8,128)(2,1)} %copy-done.7) | copy-start | bytes 1179652
  227.8 10.7 %collective-permute-start.8 = (bf16[128,1024]{1,0:T(8,128)(2,1)}, bf16[128,1024]{1,0:T(8,128)(2,1)S(1)}, u32[]{:S(2)}, u32[]{:S(2)}) collective-permute-start(bf16[128,1024]{1,0:T(8,128)(2,1)} %get-tuple-element.51), channel_id=1, source_target_pairs={{4,0},{8,12},{5,1},{9,13},{6,2},{10,14},{7,3},{11,15},{20,16},{24,... | collective-permute-start | bytes 786440 | tf_op jit(solution)/shard_map/ppermute | solution.py:290
  229.3 9.3 %collective-permute-start.9 = (bf16[128,1024]{1,0:T(8,128)(2,1)}, bf16[128,1024]{1,0:T(8,128)(2,1)}, u32[]{:S(2)}, u32[]{:S(2)}) collective-permute-start(bf16[128,1024]{1,0:T(8,128)(2,1)} %get-tuple-element.52), channel_id=1, source_target_pairs={{0,16},{16,0},{1,17},{17,1},{2,18},{18,2},{3,19},{19,3},{4,20},{20... | collective-permute-start | bytes 786440 | tf_op jit(solution)/shard_map/ppermute | solution.py:291
  231.0 7.5 %copy-start.10 = (bf16[3,128,512]{2,1,0:T(8,128)(2,1)S(1)}, bf16[3,128,512]{2,1,0:T(8,128)(2,1)}, u32[]{:S(2)}) copy-start(bf16[3,128,512]{2,1,0:T(8,128)(2,1)} %copy-done.9) | copy-start | bytes 1179652
  (6 other events, 11.2 us)

commit v5 on v4

--- a/solution.py
+++ b/solution.py
@@ -69,6 +69,73 @@
     )(slots, *groups)
 
 
+def add_kernel(slots_ref, *refs):
+    *tile_refs, _, _, up_ref, down_ref, up_buffer, down_buffer, sems = refs
+    slot_count, _, ff_shard = up_ref.shape
+    for i, tiles_ref in enumerate(tile_refs):
+        copies = []
+        for k in range(tiles_ref.shape[0]):
+            slot = slots_ref[i * tiles_ref.shape[0] + k]
+            hit = (slot >= 0) & (slot < slot_count)
+            at = jnp.clip(slot, 0, slot_count - 1)
+            pairs = ((up_ref.at[at], up_buffer.at[k]), (down_ref.at[at], down_buffer.at[k]))
+            copies.append((hit, pairs, sems.at[k]))
+        for hit, pairs, pair_sems in copies:
+
+            @pl.when(hit)
+            def _(pairs=pairs, pair_sems=pair_sems):
+                for n, (place, buffer) in enumerate(pairs):
+                    pltpu.make_async_copy(place, buffer, pair_sems.at[n]).start()
+
+        for k, (hit, pairs, pair_sems) in enumerate(copies):
+
+            @pl.when(hit)
+            def _(k=k, pairs=pairs, pair_sems=pair_sems, tiles_ref=tiles_ref):
+                for n, (place, buffer) in enumerate(pairs):
+                    pltpu.make_async_copy(place, buffer, pair_sems.at[n]).wait()
+                up_buffer[k] += tiles_ref[k, :, :ff_shard].astype(jnp.float32)
+                down_buffer[k] += tiles_ref[k, :, ff_shard:].astype(jnp.float32)
+                for n, (place, buffer) in enumerate(pairs):
+                    pltpu.make_async_copy(buffer, place, pair_sems.at[n]).start()
+
+        for hit, pairs, pair_sems in copies:
+
+            @pl.when(hit)
+            def _(pairs=pairs, pair_sems=pair_sems):
+                for n, (place, buffer) in enumerate(pairs):
+                    pltpu.make_async_copy(buffer, place, pair_sems.at[n]).wait()
+
+
+def add_in_slots(groups, slots, grad_up, grad_down):
+    tile_count, rank, columns = groups[0].shape
+    ff_shard = grad_up.shape[2]
+    in_hbm = pl.BlockSpec(memory_space=pl.ANY)
+    whole = pl.BlockSpec((tile_count, rank, columns), lambda i, s: (0, 0, 0))
+    return pl.pallas_call(
+        add_kernel,
+        grid_spec=pltpu.PrefetchScalarGridSpec(
+            num_scalar_prefetch=1,
+            grid=(1,),
+            in_specs=[whole] * len(groups) + [in_hbm, in_hbm],
+            out_specs=[in_hbm, in_hbm],
+            scratch_shapes=[
+                pltpu.VMEM((tile_count, rank, ff_shard), jnp.float32),
+                pltpu.VMEM((tile_count, rank, columns - ff_shard), jnp.float32),
+                pltpu.SemaphoreType.DMA((tile_count, 2)),
+            ],
+        ),
+        out_shape=[
+            jax.ShapeDtypeStruct(grad_up.shape, grad_up.dtype),
+            jax.ShapeDtypeStruct(grad_down.shape, grad_down.dtype),
+        ],
+        input_output_aliases={len(groups) + 1: 0, len(groups) + 2: 1},
+        compiler_params=pltpu.CompilerParams(vmem_limit_bytes=20 * 1024 * 1024),
+        cost_estimate=pl.CostEstimate(
+            flops=0, bytes_accessed=4 * tile_count * rank * columns, transcendentals=0
+        ),
+    )(slots, *groups, grad_up, grad_down)
+
+
 def terms_kernel(group_count, out_count, place_ref, *refs):
     dy_refs, refs = refs[:group_count], refs[group_count:]
     *refs, dy_buffer, weight_buffer, total, dy_sems, weight_sems = refs
@@ -138,7 +205,7 @@
     rows_group, depth = groups[0].shape
     columns = sum(w.shape[0] for w in weights)
     rows = rows_group * len(groups)
-    step_depth = 512
+    step_depth = 896 if depth % 896 == 0 else depth
     out = jax.ShapeDtypeStruct((4 // out_count, len(groups), TILE, columns), jnp.bfloat16)
     in_hbm = pl.BlockSpec(memory_space=pl.ANY)
     return pl.pallas_call(
@@ -216,10 +283,10 @@
     crossing = lax.dynamic_slice_in_dim(frozen_weight, rep * half, half, 0)
     near = lax.ppermute(crossing, "dp", MIDDLE)
     partner_dy = lax.ppermute(after(grad_out, crossing), "dp", PARTNER)
-    other_dy = lax.ppermute(grad_out, "rep", OTHER_REP)
 
     dy_tiles = grad_out.reshape(tile_count, TILE, ff_shard)
-    down_sel = adapter_down[tenants]
+    down_sel = adapter_down[after(tenants, crossing)]
+    other_dy = lax.ppermute(after(grad_out, down_sel), "rep", OTHER_REP)
     up_sel = adapter_up[tenants]
     own_down = lax.all_to_all(down_sel, "tensor", split_axis=0, concat_axis=2, tiled=True)[0]
     middle = dot_last(own_down, tokens).astype(jnp.bfloat16)
@@ -260,8 +327,8 @@
         scale_of(partner_tenants), from_partner[:, :, :TILE], partner_dy
     )
     partner_grads = jnp.concatenate([partner_up, from_partner[:, :, TILE:]], axis=2)
-    far = lax.ppermute(after(crossing, partner_grads), "dp", OUTER_TO_MIDDLE)
-    partner_other_dy = lax.ppermute(after(partner_dy, other_dy), "rep", OTHER_REP)
+    far = lax.ppermute(after(crossing, partner_dy), "dp", OUTER_TO_MIDDLE)
+    partner_other_dy = lax.ppermute(partner_dy, "rep", OTHER_REP)
 
     events = (partner_dy, tile_grads, partner_grads)
     own_terms = product_terms([after(grad_out, *events), partner_dy], [frozen_weight], place, 1)
@@ -275,7 +342,16 @@
     far_grads = lax.ppermute(after(partner_grads, near_terms[0]), "dp", MIDDLE)
     partner_block = lax.ppermute(own_sum[1], "dp", PARTNER)
 
-    groups = [after(grad_out, own_sum, near_sum), partner_dy, other_dy]
+    tile_slots = owner_slots(owner_map, slot_count)[all_tenants].reshape(4, tile_count)
+    tile_slots = tile_slots - z * slot_count
+    grad_up, grad_down = place_in_slots(
+        [after(tile_grads, near_terms[0]), partner_grads],
+        jnp.concatenate([tile_slots[z], tile_slots[partner_index]]),
+        slot_count,
+        ff_shard,
+    )
+
+    groups = [after(grad_out, own_sum, near_sum, grad_up, grad_down), partner_dy, other_dy]
     far_terms = product_terms(groups, [far], place, 2)
     outer_terms = product_terms(
         [after(partner_other_dy, far_terms[0], near_grads, partner_block)], [near, far], place, 2
@@ -287,11 +363,9 @@
     far_sum = sum_of_chips(far_terms[1], far_got)
     outer_sum = sum_of_chips(after(outer_terms[1], near_grads_out), outer_got)[0]
     both_sum = jnp.concatenate([near_sum, far_sum], axis=2)
-    both_out = lax.ppermute(both_sum[1], "dp", OUTWARD)
+    both_out = lax.ppermute(after(both_sum[1], far_grads_out), "dp", OUTWARD)
     both_other = lax.ppermute(both_sum[2], "rep", OTHER_REP)
-    outer_other = lax.ppermute(
-        after(outer_sum, far_grads_out), ("rep", "dp"), OUTWARD_OTHER_REP
-    )
+    outer_other = lax.ppermute(outer_sum, ("rep", "dp"), OUTWARD_OTHER_REP)
 
     mine = jnp.where(inner, both_sum[0], both_out)
     other = jnp.where(inner, both_other, outer_other)
@@ -321,24 +395,17 @@
 
     near_index = jnp.where(z < 2, 2, 1)
     far_index = jnp.where(z < 2, 3, 0)
-    tile_slots = owner_slots(owner_map, slot_count)[all_tenants].reshape(4, tile_count)
-    tile_slots = tile_slots - z * slot_count
     nowhere = jnp.full((tile_count,), -1, jnp.int32)
     slots = jnp.concatenate(
         [
-            tile_slots[z],
-            tile_slots[partner_index],
             jnp.where(inner, tile_slots[near_index], nowhere),
+            jnp.where(inner, nowhere, tile_slots[near_index]),
             jnp.where(inner, tile_slots[far_index], nowhere),
-            jnp.where(inner, nowhere, tile_slots[near_index]),
             jnp.where(inner, nowhere, tile_slots[far_index]),
         ]
     )
-    grad_up, grad_down = place_in_slots(
-        [tile_grads, partner_grads, near_grads, far_grads, near_grads_out, far_grads_out],
-        slots,
-        slot_count,
-        ff_shard,
+    grad_up, grad_down = add_in_slots(
+        [near_grads, near_grads_out, far_grads, far_grads_out], slots, grad_up, grad_down
     )
     return input_grad, grad_down, grad_up
 

time: 245 us -> 235 us (0.959)
  local copies, waits for them, and re-layouts: 20.9 us -> 17.4 us
  waiting for transfers between devices: 96.4 us -> 93.2 us
  other arithmetic: 12.6 us -> 9.99 us
    ppermute x1, waiting for transfers between devices: 45.7 us -> 0.01 us  [line_of_four(): from_partner = lax.ppermute(to_partner, 'dp', PARTNER)]
    ppermute x1, waiting for transfers between devices: 0.01 us -> 42.8 us  [line_of_four(): partner_dy = lax.ppermute(after(grad_out, crossing), 'dp', PARTNER)]
    all_to_all x2, waiting for transfers between devices: 27.7 us -> 20.7 us  [sum_by_swap(): lax.all_to_all(terms[0], 'tensor', split_axis=0, concat_axis=0, tiled=True)]
    pallas_call x0 -> x1, Pallas kernels: none -> 3.67 us  [add_in_slots(): pl.pallas_call(add_kernel, grid_spec=pltpu.PrefetchScalarGridSpec(num_sca...]
    ppermute x1, waiting for transfers between devices: 0.01 us -> 3.12 us  [line_of_four(): far_grads_out = lax.ppermute(far_grads, 'dp', OUTWARD)]
    convert_element_type x2, local copies, waits for them, and re-layouts: 2.96 us -> 0.08 us  [sum_of_chips(): sent = after(pair[0].astype(jnp.bfloat16), *events)]
  transfers between devices with their start and end apart: 23 -> 23, of which waited for: 9 -> 13; matrix products, arithmetic and copies ran while one was open for 13% -> 11% of each run, Pallas kernels for 22% -> 22%
where the time goes in v5:
time: 235 us; the launch traced here: 234 us
  waiting for transfers between devices  93.2 us (40%)
  Pallas kernels  52.6 us (22%)
  starting transfers between devices  48.7 us (21%)
  local copies, waits for them, and re-layouts  17.4 us (7%)
  matrix products  11.2 us (5%)
  other arithmetic  9.99 us (4%)
    pallas_call x4, Pallas kernels, product_terms(): pl.pallas_call(functools.partial(terms_kernel, len(groups), out_count), g...  43.5 us
    ppermute x1, waiting for transfers between devices, line_of_four(): partner_dy = lax.ppermute(after(grad_out, crossing), 'dp', PARTNER)  42.8 us
    all_to_all x2, waiting for transfers between devices, sum_by_swap(): lax.all_to_all(terms[0], 'tensor', split_axis=0, concat_axis=0, tiled=True)  20.7 us
    ppermute x2, waiting for transfers between devices, sum_of_chips(): got = lax.ppermute(sent, 'tensor', [(0, 2), (2, 0), (1, 3), (3, 1)])  9.41 us
    all_to_all x2, starting transfers between devices, sum_by_swap(): lax.all_to_all(terms[0], 'tensor', split_axis=0, concat_axis=0, tiled=True)  8.04 us
    ppermute x1, starting transfers between devices, line_of_four(): far = lax.ppermute(after(crossing, partner_dy), 'dp', OUTER_TO_MIDDLE)  6.86 us
    ppermute x1, waiting for transfers between devices, line_of_four(): lax.ppermute(after(near_grads, far_terms[0]), 'dp', OUTWARD)  6.52 us
    pallas_call x1, Pallas kernels, place_in_slots(): pl.pallas_call(place_kernel, grid_spec=pltpu.PrefetchScalarGridSpec(num_s...  5.48 us
  transfers between devices with their start and end apart: 23, of which 13 were waited for; matrix products, arithmetic and copies ran while one was open for 11% of the time, Pallas kernels for 22%

profile of v5, /device:TPU:0, one launch (start us, length us, event | category | flops | bytes accessed | tf_op | source)
XLA Modules:
  0.0 234.3 jit_solution(10115121753840162473)
XLA Ops:
  0.7 4.3 %constant_dynamic-slice_fusion.5 = bf16[512,3584]{1,0:T(8,128)(2,1)} fusion(bf16[1024,3584]{1,0:T(8,128)(2,1)} %refs_2_.1, s32[]{:T(128)S(6)} %select_n.149), kind=kLoop, calls=%fused_computation.78 | loop fusion | bytes 7340036 | tf_op jit(solution)/shard_map/dynamic_slice | solution.py:283
  5.0 3.0 %collective-permute-start = (bf16[512,3584]{1,0:T(8,128)(2,1)}, bf16[512,3584]{1,0:T(8,128)(2,1)}, u32[]{:S(2)}, u32[]{:S(2)}) collective-permute-start(bf16[512,3584]{1,0:T(8,128)(2,1)} %refs_0_.2), channel_id=1, source_target_pairs={{0,4},{4,0},{8,12},{12,8},{1,5},{5,1},{9,13},{13,9},{2,6},{6,2},{1... | collective-permute-start | bytes 11010056 | tf_op jit(solution)/shard_map/ppermute | solution.py:285
  8.0 2.5 %collective-permute-start.3 = (bf16[512,3584]{1,0:T(8,128)(2,1)}, bf16[512,3584]{1,0:T(8,128)(2,1)}, u32[]{:S(2)}, u32[]{:S(2)}) collective-permute-start(bf16[512,3584]{1,0:T(8,128)(2,1)} %constant_dynamic-slice_fusion.5), channel_id=1, source_target_pairs={{4,8},{8,4},{5,9},{9,5},{6,10},{10,6},{7,11},{11,7},{20,24},{24,20... | collective-permute-start | bytes 11010056 | tf_op jit(solution)/shard_map/ppermute | solution.py:284
  12.0 3.3 %all-to-all-start = ((bf16[4,16,1024]{2,1,0:T(8,128)(2,1)}), bf16[4,16,1024]{2,1,0:T(8,128)(2,1)S(1)}, u32[]{:S(2)}, u32[]{:S(2)}) async-start(bf16[4,16,1024]{2,1,0:T(8,128)(2,1)} %gather_fusion.2), calls=%async_computation | async-start | bytes 262144 | tf_op jit(solution)/shard_map/all_to_all | solution.py:291
  17.0 3.7 %gather_fusion.1 = bf16[4,16,3584]{2,1,0:T(8,128)(2,1)S(1)} fusion(bf16[64,16,3584]{2,1,0:T(8,128)(2,1)} %param.12, s32[1024]{0:T(1024)S(1)} %get-tuple-element.75), kind=kCustom, calls=%fused_computation.1 | custom fusion | bytes 917520 | tf_op jit(solution)/shard_map/gather | solution.py:290
  21.9 3.2 %convolution_convert_fusion = bf16[4,16,128]{2,1,0:T(8,128)(2,1)S(1)} fusion(bf16[4,16,3584]{2,1,0:T(8,128)(2,1)S(1)} %gather_fusion.1, bf16[4,128,3584]{2,1,0:T(8,128)(2,1)} %bitcast.3), kind=kOutput, calls=%fused_computation.14 | convolution fusion | flops 58728448 | bytes 4145152 | tf_op jit(solution)/shard_map/krf,ktf->krt/dot_general | solution.py:293
  26.3 3.3 %all-to-all-start.1 = ((bf16[4,32,128]{2,1,0:T(8,128)(2,1)}), bf16[4,32,128]{2,1,0:T(8,128)(2,1)S(1)}, u32[]{:S(2)}, u32[]{:S(2)}) async-start(bf16[4,32,128]{2,1,0:T(8,128)(2,1)} %pad_maximum_fusion.6), calls=%async_computation.1 | async-start | bytes 65536 | tf_op jit(solution)/shard_map/all_to_all | solution.py:297
  30.3 3.2 %all-to-all-done.1 = bf16[4,32,128]{2,1,0:T(8,128)(2,1)S(1)} async-done(((bf16[4,32,128]{2,1,0:T(8,128)(2,1)}), bf16[4,32,128]{2,1,0:T(8,128)(2,1)S(1)}, u32[]{:S(2)}, u32[]{:S(2)}) %all-to-all-start.1) | async-done | bytes 32800 | tf_op jit(solution)/shard_map/all_to_all | solution.py:297
  35.1 3.3 %all-to-all-start.2 = ((bf16[16,4,1024]{2,0,1:T(8,128)(2,1)}), bf16[16,4,1024]{2,0,1:T(8,128)(2,1)S(1)}, u32[]{:S(2)}, u32[]{:S(2)}) async-start(bf16[16,4,1024]{2,0,1:T(8,128)(2,1)} %bitcast.86), calls=%async_computation.2 | async-start | bytes 262144 | tf_op jit(solution)/shard_map/all_to_all | solution.py:314
  38.4 2.6 %fusion = bf16[4,16,3584]{2,1,0:T(8,128)(2,1)S(1)} fusion(bf16[4,128,3584]{2,1,0:T(8,128)(2,1)} %bitcast.3, f32[4]{0:T(128)S(1)} %convert_divide_fusion.1, bf16[4,32,128]{2,1,0:T(8,128)(2,1)S(1)} %all-to-all-done.1), kind=kOutput, calls=%fused_computation.8 | convolution fusion | flops 59179008 | bytes 4145664 | tf_op jit(solution)/shard_map/krt,ktf->krf/dot_general | solution.py:306
  41.1 2.0 all-to-all-done.2
  43.0 2.7 %collective-permute-start.1 = (bf16[4,16,1152]{2,1,0:T(8,128)(2,1)S(1)}, bf16[4,16,1152]{2,1,0:T(8,128)(2,1)S(1)}, u32[]{:S(2)}, u32[]{:S(2)}) collective-permute-start(bf16[4,16,1152]{2,1,0:T(8,128)(2,1)S(1)} %pad_maximum_fusion.5), channel_id=1, source_target_pairs={{0,4},{4,0},{8,12},{12,8},{1,5},{5,1},{9,13},{13,9},{2,6},{6,2},{1... | collective-permute-start | bytes 442376 | tf_op jit(solution)/shard_map/ppermute | solution.py:320
  45.7 42.8 %collective-permute-done.refs_1_ = bf16[512,3584]{1,0:T(8,128)(2,1)} collective-permute-done((bf16[512,3584]{1,0:T(8,128)(2,1)}, bf16[512,3584]{1,0:T(8,128)(2,1)}, u32[]{:S(2)}, u32[]{:S(2)}) %collective-permute-start) | collective-permute-done | bytes 3670048 | tf_op jit(solution)/shard_map/ppermute | solution.py:285
  88.5 6.9 %collective-permute-start.5 = (bf16[512,3584]{1,0:T(8,128)(2,1)}, bf16[512,3584]{1,0:T(8,128)(2,1)}, u32[]{:S(2)}, u32[]{:S(2)}) collective-permute-start(bf16[512,3584]{1,0:T(8,128)(2,1)} %constant_dynamic-slice_fusion.5), channel_id=1, source_target_pairs={{0,8},{12,4},{1,9},{13,5},{2,10},{14,6},{3,11},{15,7},{16,24},{28,... | collective-permute-start | bytes 11010056 | tf_op jit(solution)/shard_map/ppermute | solution.py:330
  97.0 2.7 %fusion.1 = bf16[4,16,3584]{2,1,0:T(8,128)(2,1)S(1)} fusion(bf16[4,128,3584]{2,1,0:T(8,128)(2,1)} %bitcast.8, f32[4]{0:T(128)S(1)} %convert_divide_fusion, bf16[4,16,1152]{2,1,0:T(8,128)(2,1)S(1)} %collective-permute-done.1), kind=kOutput, calls=%fused_computation.9 | convolution fusion | flops 59179008 | bytes 4145664 | tf_op jit(solution)/shard_map/krt,ktf->krf/dot_general | solution.py:306
  99.8 3.1 %copy-done.2 = bf16[1024,3584]{1,0:T(8,128)(2,1)S(1)} copy-done((bf16[1024,3584]{1,0:T(8,128)(2,1)S(1)}, bf16[1024,3584]{1,0:T(8,128)(2,1)}, u32[]{:S(2)}) %copy-start.2) | copy-done | bytes 7340056
  102.8 13.3 %shard_map.103 = bf16[4,2,128,1024]{3,2,1,0:T(8,128)(2,1)} custom-call(s32[2]{0:T(128)S(1)} %pad_add_fusion.place_ref, bf16[512,3584]{1,0:T(8,128)(2,1)} %refs_0_.2, bf16[512,3584]{1,0:T(8,128)(2,1)} %collective-permute-done.refs_1_, bf16[1024,3584]{1,0:T(8,128)(2,1)S(1)} %copy-done.2), custom_call_target="tpu_custom_call" | custom-call | tf_op jit(solution)/shard_map/pallas_call | solution.py:211
  116.2 4.5 %all-to-all-start.3 = ((bf16[4,2,128,1024]{3,2,1,0:T(8,128)(2,1)}), bf16[4,2,128,1024]{3,2,1,0:T(8,128)(2,1)}, u32[]{:S(2)}, u32[]{:S(2)}) async-start(bf16[4,2,128,1024]{3,2,1,0:T(8,128)(2,1)} %shard_map.103), calls=%async_computation.3 | async-start | bytes 4194304 | tf_op jit(solution)/shard_map/all_to_all | solution.py:248
  120.7 11.6 %shard_map.104 = bf16[4,3,128,512]{3,2,1,0:T(8,128)(2,1)} custom-call(s32[2]{0:T(128)S(1)} %pad_add_fusion.place_ref, bf16[512,3584]{1,0:T(8,128)(2,1)} %refs_0_.2, bf16[512,3584]{1,0:T(8,128)(2,1)} %collective-permute-done.refs_1_, bf16[512,3584]{1,0:T(8,128)(2,1)} %collective-permute-done.4.refs_2_, bf16[512,3584]{1,0:T(8,128)(2,1)} %collective-permute-done.3.refs_3_.refs_1_), custom_call_target="tpu_custom_call" | custom-call | tf_op jit(solution)/shard_map/pallas_call | solution.py:211
  132.3 14.1 %all-to-all-done.3 = bf16[4,2,128,1024]{3,2,1,0:T(8,128)(2,1)} async-done(((bf16[4,2,128,1024]{3,2,1,0:T(8,128)(2,1)}), bf16[4,2,128,1024]{3,2,1,0:T(8,128)(2,1)}, u32[]{:S(2)}, u32[]{:S(2)}) %all-to-all-start.3) | async-done | bytes 2097184 | tf_op jit(solution)/shard_map/all_to_all | solution.py:248
  146.4 3.6 %all-to-all-start.4 = ((bf16[4,3,128,512]{3,2,1,0:T(8,128)(2,1)}), bf16[4,3,128,512]{3,2,1,0:T(8,128)(2,1)S(1)}, u32[]{:S(2)}, u32[]{:S(2)}) async-start(bf16[4,3,128,512]{3,2,1,0:T(8,128)(2,1)} %shard_map.104), calls=%async_computation.4 | async-start | bytes 3145728 | tf_op jit(solution)/shard_map/all_to_all | solution.py:248
  153.9 2.9 %reduce_sum.46 = bf16[2,128,1024]{2,1,0:T(8,128)(2,1)} reduce(bf16[4,2,128,1024]{3,2,1,0:T(8,128)(2,1)} %all-to-all-done.3, bf16[]{:T(256)} %constant.73.clone.1), dimensions={0}, to_apply=%region_1.2 | reduce | flops 786432 | bytes 2621442 | tf_op jit(solution)/shard_map/reduce_sum | solution.py:249
  158.0 5.5 %shard_map.105 = (f32[32,16,3584]{2,1,0:T(8,128)}, f32[32,16,1024]{2,1,0:T(8,128)}) custom-call(s32[8]{0:T(128)S(1)} %pad_add_fusion.1.slots_ref, bf16[4,16,4608]{2,1,0:T(8,128)(2,1)S(1)} %pad_maximum_fusion.refs_0_, bf16[4,16,4608]{2,1,0:T(8,128)(2,1)S(1)} %pad_maximum_fusion.1.refs_1_), custom_call_target="tpu_custom_call" | custom-call | bytes 18874368 | tf_op jit(solution)/shard_map/pallas_call | solution.py:49
  163.4 6.6 %all-to-all-done.4 = bf16[4,3,128,512]{3,2,1,0:T(8,128)(2,1)S(1)} async-done(((bf16[4,3,128,512]{3,2,1,0:T(8,128)(2,1)}), bf16[4,3,128,512]{3,2,1,0:T(8,128)(2,1)S(1)}, u32[]{:S(2)}, u32[]{:S(2)}) %all-to-all-start.4) | async-done | bytes 1572896 | tf_op jit(solution)/shard_map/all_to_all | solution.py:248
  171.1 2.1 collective-permute-done.5.refs_3_.refs_2_
  173.2 10.4 %shard_map.106 = (bf16[2,3,128,512]{3,2,1,0:T(8,128)(2,1)S(1)}, bf16[2,3,128,512]{3,2,1,0:T(8,128)(2,1)S(1)}) custom-call(s32[2]{0:T(128)S(1)} %pad_add_fusion.place_ref, bf16[512,3584]{1,0:T(8,128)(2,1)} %refs_0_.2, bf16[512,3584]{1,0:T(8,128)(2,1)} %collective-permute-done.refs_1_, bf16[512,3584]{1,0:T(8,128)(2,1)} %collective-permute-done.4.refs_2_, ...), custom_call_target="tpu_custom_call" | custom-call | tf_op jit(solution)/shard_map/pallas_call | solution.py:211
  185.1 8.2 %shard_map.107 = (bf16[2,1,128,1024]{3,2,1,0:T(8,128)(2,1)S(1)}, bf16[2,1,128,1024]{3,2,1,0:T(8,128)(2,1)S(1)}) custom-call(s32[2]{0:T(128)S(1)} %pad_add_fusion.place_ref, bf16[512,3584]{1,0:T(8,128)(2,1)} %collective-permute-done.12.refs_0_, bf16[512,3584]{1,0:T(8,128)(2,1)} %collective-permute-done.3.refs_3_.refs_1_, ...), custom_call_target="tpu_custom_call" | custom-call | tf_op jit(solution)/shard_map/pallas_call | solution.py:211
  193.9 6.5 %collective-permute-done.14.refs_1_ = bf16[4,16,4608]{2,1,0:T(8,128)(2,1)S(1)} collective-permute-done((bf16[4,16,4608]{2,1,0:T(8,128)(2,1)}, bf16[4,16,4608]{2,1,0:T(8,128)(2,1)S(1)}, u32[]{:S(2)}, u32[]{:S(2)}) %collective-permute-start.14) | collective-permute-done | bytes 589856 | tf_op jit(solution)/shard_map/ppermute | solution.py:359
  204.4 5.6 %collective-permute-done.16 = bf16[1,128,1024]{2,1,0:T(8,128)(2,1)S(1)} collective-permute-done((bf16[1,128,1024]{2,1,0:T(8,128)(2,1)S(1)}, bf16[1,128,1024]{2,1,0:T(8,128)(2,1)S(1)}, u32[]{:S(2)}, u32[]{:S(2)}) %collective-permute-start.16) | collective-permute-done | bytes 262176 | tf_op jit(solution)/shard_map/ppermute | solution.py:243
  212.0 3.8 %collective-permute-done.7 = bf16[3,128,512]{2,1,0:T(8,128)(2,1)S(1)} collective-permute-done((bf16[3,128,512]{2,1,0:T(8,128)(2,1)S(1)}, bf16[3,128,512]{2,1,0:T(8,128)(2,1)S(1)}, u32[]{:S(2)}, u32[]{:S(2)}) %collective-permute-start.7) | collective-permute-done | bytes 393248 | tf_op jit(solution)/shard_map/ppermute | solution.py:243
  218.3 3.1 %collective-permute-done.9.refs_3_ = bf16[4,16,4608]{2,1,0:T(8,128)(2,1)S(1)} collective-permute-done((bf16[4,16,4608]{2,1,0:T(8,128)(2,1)}, bf16[4,16,4608]{2,1,0:T(8,128)(2,1)S(1)}, u32[]{:S(2)}, u32[]{:S(2)}) %collective-permute-start.9) | collective-permute-done | bytes 589856 | tf_op jit(solution)/shard_map/ppermute | solution.py:361
  222.8 3.7 %shard_map.108 = (f32[32,16,3584]{2,1,0:T(8,128)}, f32[32,16,1024]{2,1,0:T(8,128)}) custom-call(s32[16]{0:T(128)S(1)} %pad_add_fusion.2.slots_ref, bf16[4,16,4608]{2,1,0:T(8,128)(2,1)} %collective-permute-done.13.refs_0_, bf16[4,16,4608]{2,1,0:T(8,128)(2,1)S(1)} %collective-permute-done.14.refs_1_, ...), custom_call_target="tpu_custom_call", output_to_operand_aliasing={{0}: (5, {}), {1}: (6, {})} | custom-call | bytes 1179648 | tf_op jit(solution)/shard_map/pallas_call | solution.py:114
  (95 shorter events, 35.1 us)
Async XLA Ops:
  0.6 10.2 %copy-start = (bf16[64,16,1024]{2,1,0:T(8,128)(2,1)S(1)}, bf16[64,16,1024]{2,1,0:T(8,128)(2,1)}, u32[]{:S(2)}) copy-start(bf16[64,16,1024]{2,1,0:T(8,128)(2,1)} %param.11) | copy-start | bytes 6291460
  0.7 9.9 %copy-start.9 = (s32[2048]{0:T(1024)S(1)}, s32[2048]{0:T(1024)}, u32[]{:S(2)}) copy-start(s32[2048]{0:T(1024)} %param.13) | copy-start | bytes 24580
  0.7 20.0 %copy-start.3 = (s32[64]{0:T(128)S(1)}, s32[64]{0:T(128)}, u32[]{:S(2)}) copy-start(s32[64]{0:T(128)} %param.14) | copy-start | bytes 772
  5.0 83.5 %collective-permute-start = (bf16[512,3584]{1,0:T(8,128)(2,1)}, bf16[512,3584]{1,0:T(8,128)(2,1)}, u32[]{:S(2)}, u32[]{:S(2)}) collective-permute-start(bf16[512,3584]{1,0:T(8,128)(2,1)} %refs_0_.2), channel_id=1, source_target_pairs={{0,4},{4,0},{8,12},{12,8},{1,5},{5,1},{9,13},{13,9},{2,6},{6,2},{1... | collective-permute-start | bytes 11010056 | tf_op jit(solution)/shard_map/ppermute | solution.py:285
  8.0 112.6 %collective-permute-start.3 = (bf16[512,3584]{1,0:T(8,128)(2,1)}, bf16[512,3584]{1,0:T(8,128)(2,1)}, u32[]{:S(2)}, u32[]{:S(2)}) collective-permute-start(bf16[512,3584]{1,0:T(8,128)(2,1)} %constant_dynamic-slice_fusion.5), channel_id=1, source_target_pairs={{4,8},{8,4},{5,9},{9,5},{6,10},{10,6},{7,11},{11,7},{20,24},{24,20... | collective-permute-start | bytes 11010056 | tf_op jit(solution)/shard_map/ppermute | solution.py:284
  12.0 13.1 %all-to-all-start = ((bf16[4,16,1024]{2,1,0:T(8,128)(2,1)}), bf16[4,16,1024]{2,1,0:T(8,128)(2,1)S(1)}, u32[]{:S(2)}, u32[]{:S(2)}) async-start(bf16[4,16,1024]{2,1,0:T(8,128)(2,1)} %gather_fusion.2), calls=%async_computation | async-start | bytes 262144 | tf_op jit(solution)/shard_map/all_to_all | solution.py:291
  15.4 105.3 %collective-permute-start.4 = (bf16[512,3584]{1,0:T(8,128)(2,1)}, bf16[512,3584]{1,0:T(8,128)(2,1)}, u32[]{:S(2)}, u32[]{:S(2)}) collective-permute-start(bf16[512,3584]{1,0:T(8,128)(2,1)} %refs_0_.2), channel_id=1, source_target_pairs={{0,16},{16,0},{1,17},{17,1},{2,18},{18,2},{3,19},{19,3},{4,20},{20... | collective-permute-start | bytes 11010056 | tf_op jit(solution)/shard_map/ppermute | solution.py:289
  21.9 3.4 %copy-start.4 = (bf16[128,4096]{1,0:T(8,128)(2,1)S(1)}, bf16[128,4096]{1,0:T(8,128)(2,1)}, u32[]{:S(2)}) copy-start(bf16[128,4096]{1,0:T(8,128)(2,1)} %param.8) | copy-start | bytes 3145732
  26.3 7.2 %all-to-all-start.1 = ((bf16[4,32,128]{2,1,0:T(8,128)(2,1)}), bf16[4,32,128]{2,1,0:T(8,128)(2,1)S(1)}, u32[]{:S(2)}, u32[]{:S(2)}) async-start(bf16[4,32,128]{2,1,0:T(8,128)(2,1)} %pad_maximum_fusion.6), calls=%async_computation.1 | async-start | bytes 65536 | tf_op jit(solution)/shard_map/all_to_all | solution.py:297
  35.1 7.9 %all-to-all-start.2 = ((bf16[16,4,1024]{2,0,1:T(8,128)(2,1)}), bf16[16,4,1024]{2,0,1:T(8,128)(2,1)S(1)}, u32[]{:S(2)}, u32[]{:S(2)}) async-start(bf16[16,4,1024]{2,0,1:T(8,128)(2,1)} %bitcast.86), calls=%async_computation.2 | async-start | bytes 262144 | tf_op jit(solution)/shard_map/all_to_all | solution.py:314
  43.0 52.4 %collective-permute-start.1 = (bf16[4,16,1152]{2,1,0:T(8,128)(2,1)S(1)}, bf16[4,16,1152]{2,1,0:T(8,128)(2,1)S(1)}, u32[]{:S(2)}, u32[]{:S(2)}) collective-permute-start(bf16[4,16,1152]{2,1,0:T(8,128)(2,1)S(1)} %pad_maximum_fusion.5), channel_id=1, source_target_pairs={{0,4},{4,0},{8,12},{12,8},{1,5},{5,1},{9,13},{13,9},{2,6},{6,2},{1... | collective-permute-start | bytes 442376 | tf_op jit(solution)/shard_map/ppermute | solution.py:320
  88.5 84.7 %collective-permute-start.5 = (bf16[512,3584]{1,0:T(8,128)(2,1)}, bf16[512,3584]{1,0:T(8,128)(2,1)}, u32[]{:S(2)}, u32[]{:S(2)}) collective-permute-start(bf16[512,3584]{1,0:T(8,128)(2,1)} %constant_dynamic-slice_fusion.5), channel_id=1, source_target_pairs={{0,8},{12,4},{1,9},{13,5},{2,10},{14,6},{3,11},{15,7},{16,24},{28,... | collective-permute-start | bytes 11010056 | tf_op jit(solution)/shard_map/ppermute | solution.py:330
  95.4 89.7 %collective-permute-start.12 = (bf16[512,3584]{1,0:T(8,128)(2,1)}, bf16[512,3584]{1,0:T(8,128)(2,1)}, u32[]{:S(2)}, u32[]{:S(2)}) collective-permute-start(bf16[512,3584]{1,0:T(8,128)(2,1)} %collective-permute-done.refs_1_), channel_id=1, source_target_pairs={{0,16},{16,0},{1,17},{17,1},{2,18},{18,2},{3,19},{19,3},{4,20},{20... | collective-permute-start | bytes 11010056 | tf_op jit(solution)/shard_map/ppermute | solution.py:331
  116.2 30.2 %all-to-all-start.3 = ((bf16[4,2,128,1024]{3,2,1,0:T(8,128)(2,1)}), bf16[4,2,128,1024]{3,2,1,0:T(8,128)(2,1)}, u32[]{:S(2)}, u32[]{:S(2)}) async-start(bf16[4,2,128,1024]{3,2,1,0:T(8,128)(2,1)} %shard_map.103), calls=%async_computation.3 | async-start | bytes 4194304 | tf_op jit(solution)/shard_map/all_to_all | solution.py:248
  132.3 17.7 %copy-start.10 = (s32[64]{0:T(128)S(1)}, s32[64]{0:T(128)}, u32[]{:S(2)}) copy-start(s32[64]{0:T(128)} %param.15) | copy-start | bytes 772
  146.4 23.6 %all-to-all-start.4 = ((bf16[4,3,128,512]{3,2,1,0:T(8,128)(2,1)}), bf16[4,3,128,512]{3,2,1,0:T(8,128)(2,1)S(1)}, u32[]{:S(2)}, u32[]{:S(2)}) async-start(bf16[4,3,128,512]{3,2,1,0:T(8,128)(2,1)} %shard_map.104), calls=%async_computation.4 | async-start | bytes 3145728 | tf_op jit(solution)/shard_map/all_to_all | solution.py:248
  150.9 32.8 %collective-permute-start.13 = (bf16[4,16,4608]{2,1,0:T(8,128)(2,1)S(1)}, bf16[4,16,4608]{2,1,0:T(8,128)(2,1)}, u32[]{:S(2)}, u32[]{:S(2)}) collective-permute-start(bf16[4,16,4608]{2,1,0:T(8,128)(2,1)S(1)} %pad_maximum_fusion.refs_0_), channel_id=1, source_target_pairs={{4,8},{8,4},{5,9},{9,5},{6,10},{10,6},{7,11},{11,7},{20,24},{24,20... | collective-permute-start | bytes 1769480 | tf_op jit(solution)/shard_map/ppermute | solution.py:341
  152.3 41.0 %collective-permute-start.8 = (bf16[4,16,4608]{2,1,0:T(8,128)(2,1)S(1)}, bf16[4,16,4608]{2,1,0:T(8,128)(2,1)}, u32[]{:S(2)}, u32[]{:S(2)}) collective-permute-start(bf16[4,16,4608]{2,1,0:T(8,128)(2,1)S(1)} %pad_maximum_fusion.1.refs_1_), channel_id=1, source_target_pairs={{4,8},{8,4},{5,9},{9,5},{6,10},{10,6},{7,11},{11,7},{20,24},{24,20... | collective-permute-start | bytes 1769480 | tf_op jit(solution)/shard_map/ppermute | solution.py:342
  157.8 27.4 %collective-permute-start.2 = (bf16[128,1024]{1,0:T(8,128)(2,1)S(1)}, bf16[128,1024]{1,0:T(8,128)(2,1)}, u32[]{:S(2)}, u32[]{:S(2)}) collective-permute-start(bf16[128,1024]{1,0:T(8,128)(2,1)S(1)} %slice_bitcast_fusion.2), channel_id=1, source_target_pairs={{0,4},{4,0},{8,12},{12,8},{1,5},{5,1},{9,13},{13,9},{2,6},{6,2},{1... | collective-permute-start | bytes 786440 | tf_op jit(solution)/shard_map/ppermute | solution.py:343
  183.6 16.8 %collective-permute-start.14 = (bf16[4,16,4608]{2,1,0:T(8,128)(2,1)}, bf16[4,16,4608]{2,1,0:T(8,128)(2,1)S(1)}, u32[]{:S(2)}, u32[]{:S(2)}) collective-permute-start(bf16[4,16,4608]{2,1,0:T(8,128)(2,1)} %collective-permute-done.13.refs_0_), channel_id=1, source_target_pairs={{4,0},{8,12},{5,1},{9,13},{6,2},{10,14},{7,3},{11,15},{20,16},{24,... | collective-permute-start | bytes 1769480 | tf_op jit(solution)/shard_map/ppermute | solution.py:359
  193.3 7.1 %collective-permute-start.15 = (bf16[2,1,128,1024]{3,2,1,0:T(8,128)(2,1)S(1)}, bf16[2,1,128,1024]{3,2,1,0:T(8,128)(2,1)S(1)}, u32[]{:S(2)}, u32[]{:S(2)}) collective-permute-start(bf16[2,1,128,1024]{3,2,1,0:T(8,128)(2,1)S(1)} %get-tuple-element.44), channel_id=1, source_target_pairs={{0,1},{1,0},{2,3},{3,2},{4,5},{5,4},{6,7},{7,6},{8,9},{9,8},{10,11... | collective-permute-start | bytes 1572872 | tf_op jit(solution)/shard_map/ppermute | solution.py:237
  193.4 8.8 %collective-permute-start.6 = (bf16[2,3,128,512]{3,2,1,0:T(8,128)(2,1)S(1)}, bf16[2,3,128,512]{3,2,1,0:T(8,128)(2,1)S(1)}, u32[]{:S(2)}, u32[]{:S(2)}) collective-permute-start(bf16[2,3,128,512]{3,2,1,0:T(8,128)(2,1)S(1)} %get-tuple-element.36), channel_id=1, source_target_pairs={{0,1},{1,0},{2,3},{3,2},{4,5},{5,4},{6,7},{7,6},{8,9},{9,8},{10,11... | collective-permute-start | bytes 2359304 | tf_op jit(solution)/shard_map/ppermute | solution.py:237
  200.6 9.3 %collective-permute-start.16 = (bf16[1,128,1024]{2,1,0:T(8,128)(2,1)S(1)}, bf16[1,128,1024]{2,1,0:T(8,128)(2,1)S(1)}, u32[]{:S(2)}, u32[]{:S(2)}) collective-permute-start(bf16[1,128,1024]{2,1,0:T(8,128)(2,1)S(1)} %fusion.9), channel_id=1, source_target_pairs={{0,2},{2,0},{1,3},{3,1},{4,6},{6,4},{5,7},{7,5},{8,10},{10,8},{9,1... | collective-permute-start | bytes 786440 | tf_op jit(solution)/shard_map/ppermute | solution.py:243
  202.4 13.6 %copy-start.5 = (bf16[3,128,512]{2,1,0:T(8,128)(2,1)S(1)}, bf16[3,128,512]{2,1,0:T(8,128)(2,1)}, u32[]{:S(2)}) copy-start(bf16[3,128,512]{2,1,0:T(8,128)(2,1)} %reduce_sum.47) | copy-start | bytes 1179652
  202.5 13.4 %collective-permute-start.7 = (bf16[3,128,512]{2,1,0:T(8,128)(2,1)S(1)}, bf16[3,128,512]{2,1,0:T(8,128)(2,1)S(1)}, u32[]{:S(2)}, u32[]{:S(2)}) collective-permute-start(bf16[3,128,512]{2,1,0:T(8,128)(2,1)S(1)} %fusion.7), channel_id=1, source_target_pairs={{0,2},{2,0},{1,3},{3,1},{4,6},{6,4},{5,7},{7,5},{8,10},{10,8},{9,1... | collective-permute-start | bytes 1179656 | tf_op jit(solution)/shard_map/ppermute | solution.py:243
  203.1 18.4 %collective-permute-start.9 = (bf16[4,16,4608]{2,1,0:T(8,128)(2,1)}, bf16[4,16,4608]{2,1,0:T(8,128)(2,1)S(1)}, u32[]{:S(2)}, u32[]{:S(2)}) collective-permute-start(bf16[4,16,4608]{2,1,0:T(8,128)(2,1)} %collective-permute-done.8.refs_2_), channel_id=1, source_target_pairs={{4,0},{8,12},{5,1},{9,13},{6,2},{10,14},{7,3},{11,15},{20,16},{24,... | collective-permute-start | bytes 1769480 | tf_op jit(solution)/shard_map/ppermute | solution.py:361
  210.7 17.2 %collective-permute-start.17 = (bf16[128,1024]{1,0:T(8,128)(2,1)}, bf16[128,1024]{1,0:T(8,128)(2,1)}, u32[]{:S(2)}, u32[]{:S(2)}) collective-permute-start(bf16[128,1024]{1,0:T(8,128)(2,1)} %fusion.8), channel_id=1, source_target_pairs={{4,16},{8,28},{20,0},{24,12},{5,17},{9,29},{21,1},{25,13},{6,18},{... | collective-permute-start | bytes 786440 | tf_op jit(solution)/shard_map/ppermute | solution.py:368
  216.0 6.8 %copy-start.6 = (bf16[3,128,512]{2,1,0:T(8,128)(2,1)}, bf16[3,128,512]{2,1,0:T(8,128)(2,1)S(1)}, u32[]{:S(2)}) copy-start(bf16[3,128,512]{2,1,0:T(8,128)(2,1)S(1)} %fusion.4) | copy-start | bytes 1179652
  216.8 11.2 %collective-permute-start.11 = (bf16[128,1024]{1,0:T(8,128)(2,1)}, bf16[128,1024]{1,0:T(8,128)(2,1)}, u32[]{:S(2)}, u32[]{:S(2)}) collective-permute-start(bf16[128,1024]{1,0:T(8,128)(2,1)} %get-tuple-element.59), channel_id=1, source_target_pairs={{0,16},{16,0},{1,17},{17,1},{2,18},{18,2},{3,19},{19,3},{4,20},{20... | collective-permute-start | bytes 786440 | tf_op jit(solution)/shard_map/ppermute | solution.py:367
  221.4 8.4 %collective-permute-start.10 = (bf16[128,1024]{1,0:T(8,128)(2,1)S(1)}, bf16[128,1024]{1,0:T(8,128)(2,1)}, u32[]{:S(2)}, u32[]{:S(2)}) collective-permute-start(bf16[128,1024]{1,0:T(8,128)(2,1)S(1)} %get-tuple-element.38), channel_id=1, source_target_pairs={{4,0},{8,12},{5,1},{9,13},{6,2},{10,14},{7,3},{11,15},{20,16},{24,... | collective-permute-start | bytes 786440 | tf_op jit(solution)/shard_map/ppermute | solution.py:366
  222.8 7.0 %copy-start.7 = (bf16[3,128,512]{2,1,0:T(8,128)(2,1)S(1)}, bf16[3,128,512]{2,1,0:T(8,128)(2,1)}, u32[]{:S(2)}) copy-start(bf16[3,128,512]{2,1,0:T(8,128)(2,1)} %copy-done.6) | copy-start | bytes 1179652
  226.5 4.6 %copy-start.8 = (bf16[2,128,1024]{2,1,0:T(8,128)(2,1)S(1)}, bf16[2,128,1024]{2,1,0:T(8,128)(2,1)}, u32[]{:S(2)}) copy-start(bf16[2,128,1024]{2,1,0:T(8,128)(2,1)} %reduce_sum.46) | copy-start | bytes 1572868
  (2 other events, 5.0 us)

commit v6 on v5

--- a/solution.py
+++ b/solution.py
@@ -227,6 +227,55 @@
         compiler_params=pltpu.CompilerParams(vmem_limit_bytes=20 * 1024 * 1024),
         cost_estimate=pl.CostEstimate(flops=0, bytes_accessed=0, transcendentals=0),
     )(place, *groups, *weights)
+
+
+def assemble_kernel(flags_ref, *refs):
+    own_ref, partner_ref, here_ref, out_ref, swapped_ref, diagonal_ref = refs[:6]
+    backed_ref, down_ref, input_grad_ref, lora = refs[6:]
+    z, rep = flags_ref[0], flags_ref[1]
+    width = own_ref.shape[1]
+    half = width // 2
+    lora[...] = adapter_scale * lax.dot_general(
+        backed_ref[...],
+        down_ref[...],
+        (((0,), (0,)), ((), ())),
+        preferred_element_type=jnp.float32,
+    )
+    inner = (z == 1) | (z == 2)
+    near_block = jnp.where(z < 2, 2, 1)
+    far_block = jnp.where(z < 2, 3, 0)
+
+    def put(start, values):
+        columns = pl.ds(pl.multiple_of(start, half), values.shape[1])
+        input_grad_ref[:, columns] = (values.astype(jnp.float32) + lora[:, columns]).astype(
+            input_grad_ref.dtype
+        )
+
+    put(z * width, own_ref[...])
+    put((z + 1 - 2 * lax.rem(z, 2)) * width, partner_ref[...])
+    for block, columns in ((near_block, slice(0, half)), (far_block, slice(half, width))):
+        mine = jnp.where(inner, here_ref[:, columns], out_ref[:, columns])
+        put(block * width + rep * half, mine)
+        other = jnp.where(inner, swapped_ref[:, columns], diagonal_ref[:, columns])
+        put(block * width + (1 - rep) * half, other)
+
+
+def assemble(z, rep, blocks, backed, own_down):
+    whole = [pl.BlockSpec(x.shape, lambda i, f: (0, 0)) for x in (*blocks, backed, own_down)]
+    shape = (blocks[0].shape[0], own_down.shape[1])
+    return pl.pallas_call(
+        assemble_kernel,
+        grid_spec=pltpu.PrefetchScalarGridSpec(
+            num_scalar_prefetch=1,
+            grid=(1,),
+            in_specs=whole,
+            out_specs=pl.BlockSpec(shape, lambda i, f: (0, 0)),
+            scratch_shapes=[pltpu.VMEM(shape, jnp.float32)],
+        ),
+        out_shape=jax.ShapeDtypeStruct(shape, jnp.bfloat16),
+        compiler_params=pltpu.CompilerParams(vmem_limit_bytes=20 * 1024 * 1024),
+        cost_estimate=pl.CostEstimate(flops=0, bytes_accessed=0, transcendentals=0),
+    )(jnp.stack([z, rep]).astype(jnp.int32), *blocks, backed, own_down)
 
 
 def after(value, *events):
@@ -339,7 +388,7 @@
     near_sum = sum_by_swap(near_terms)
 
     near_grads = lax.ppermute(after(tile_grads, near_terms[0]), "dp", MIDDLE)
-    far_grads = lax.ppermute(after(partner_grads, near_terms[0]), "dp", MIDDLE)
+    far_grads = lax.ppermute(after(partner_grads, own_sum), "dp", MIDDLE)
     partner_block = lax.ppermute(own_sum[1], "dp", PARTNER)
 
     tile_slots = owner_slots(owner_map, slot_count)[all_tenants].reshape(4, tile_count)
@@ -363,35 +412,14 @@
     far_sum = sum_of_chips(far_terms[1], far_got)
     outer_sum = sum_of_chips(after(outer_terms[1], near_grads_out), outer_got)[0]
     both_sum = jnp.concatenate([near_sum, far_sum], axis=2)
-    both_out = lax.ppermute(after(both_sum[1], far_grads_out), "dp", OUTWARD)
+    both_out = lax.ppermute(both_sum[1], "dp", OUTWARD)
     both_other = lax.ppermute(both_sum[2], "rep", OTHER_REP)
-    outer_other = lax.ppermute(outer_sum, ("rep", "dp"), OUTWARD_OTHER_REP)
-
-    mine = jnp.where(inner, both_sum[0], both_out)
-    other = jnp.where(inner, both_other, outer_other)
-    low = jnp.where(rep == 0, mine, other)
-    high = jnp.where(rep == 0, other, mine)
-    near_block = jnp.concatenate([low[:, :half], high[:, :half]], axis=1)
-    far_block = jnp.concatenate([low[:, half:], high[:, half:]], axis=1)
-    own_block = own_sum[0]
-
-    lora = adapter_scale * lax.dot_general(
-        backed, own_down, (((0,), (0,)), ((), ())), preferred_element_type=jnp.float32
-    )
-    even = z % 2 == 0
-    first = jnp.where(even, own_block, partner_block)
-    second = jnp.where(even, partner_block, own_block)
-    left = z < 2
-    frozen = jnp.concatenate(
-        [
-            jnp.where(left, first, far_block),
-            jnp.where(left, second, near_block),
-            jnp.where(left, near_block, first),
-            jnp.where(left, far_block, second),
-        ],
-        axis=1,
-    )
-    input_grad = (frozen.astype(jnp.float32) + lora).astype(jnp.bfloat16)
+    outer_other = lax.ppermute(
+        after(outer_sum, far_grads_out), ("rep", "dp"), OUTWARD_OTHER_REP
+    )
+
+    blocks = [own_sum[0], partner_block, both_sum[0], both_out, both_other, outer_other]
+    input_grad = assemble(z, rep, blocks, backed, own_down)
 
     near_index = jnp.where(z < 2, 2, 1)
     far_index = jnp.where(z < 2, 3, 0)

time: 235 us -> 233 us (level)
  other arithmetic: 9.99 us -> 5.97 us
    ppermute x3, waiting for transfers between devices: 3.19 us -> 6.92 us  [the longest x1 4.2 us: line_of_four(): both_out = lax.ppermute(both_sum[1], 'dp', OUTWARD)]
    select_n x2 -> x0, other arithmetic: 2.42 us -> none  [the longest x1 1.21 us: line_of_four(): jnp.where(left, first, far_block)]
  transfers between devices with their start and end apart: 23 -> 23, of which waited for: 13 -> 12; matrix products, arithmetic and copies ran while one was open for 11% -> 11% of each run, Pallas kernels for 22% -> 23%
where the time goes in v6:
time: 233 us; the launch traced here: 232 us
  waiting for transfers between devices  94.4 us (41%)
  Pallas kernels  54.8 us (24%)
  starting transfers between devices  49.6 us (21%)
  local copies, waits for them, and re-layouts  16.6 us (7%)
  matrix products  9.66 us (4%)
  other arithmetic  5.97 us (3%)
    pallas_call x4, Pallas kernels, product_terms(): pl.pallas_call(functools.partial(terms_kernel, len(groups), out_count), g...  43.3 us
    ppermute x1, waiting for transfers between devices, line_of_four(): partner_dy = lax.ppermute(after(grad_out, crossing), 'dp', PARTNER)  42.9 us
    all_to_all x2, waiting for transfers between devices, sum_by_swap(): lax.all_to_all(terms[0], 'tensor', split_axis=0, concat_axis=0, tiled=True)  22.1 us
    all_to_all x2, starting transfers between devices, sum_by_swap(): lax.all_to_all(terms[0], 'tensor', split_axis=0, concat_axis=0, tiled=True)  8.79 us
    ppermute x2, waiting for transfers between devices, sum_of_chips(): got = lax.ppermute(sent, 'tensor', [(0, 2), (2, 0), (1, 3), (3, 1)])  7.85 us
    ppermute x1, starting transfers between devices, line_of_four(): far = lax.ppermute(after(crossing, partner_dy), 'dp', OUTER_TO_MIDDLE)  6.89 us
    pallas_call x1, Pallas kernels, place_in_slots(): pl.pallas_call(place_kernel, grid_spec=pltpu.PrefetchScalarGridSpec(num_s...  5.48 us
    dot_general x2, matrix products, up_gradients(): jnp.einsum('krt,ktf->krf', middle, dy, preferred_element_type=jnp.float32)  5.3 us
  transfers between devices with their start and end apart: 23, of which 12 were waited for; matrix products, arithmetic and copies ran while one was open for 11% of the time, Pallas kernels for 23%

profile of v6, /device:TPU:0, one launch (start us, length us, event | category | flops | bytes accessed | tf_op | source)
XLA Modules:
  0.0 232.1 jit_solution(5932891784645523459)
XLA Ops:
  0.7 4.3 %constant_dynamic-slice_fusion.5 = bf16[512,3584]{1,0:T(8,128)(2,1)} fusion(bf16[1024,3584]{1,0:T(8,128)(2,1)} %refs_2_.1, s32[]{:T(128)S(6)} %select_n.94), kind=kLoop, calls=%fused_computation.64 | loop fusion | bytes 7340036 | tf_op jit(solution)/shard_map/dynamic_slice | solution.py:332
  5.0 3.0 %collective-permute-start = (bf16[512,3584]{1,0:T(8,128)(2,1)}, bf16[512,3584]{1,0:T(8,128)(2,1)}, u32[]{:S(2)}, u32[]{:S(2)}) collective-permute-start(bf16[512,3584]{1,0:T(8,128)(2,1)} %refs_0_.2), channel_id=1, source_target_pairs={{0,4},{4,0},{8,12},{12,8},{1,5},{5,1},{9,13},{13,9},{2,6},{6,2},{1... | collective-permute-start | bytes 11010056 | tf_op jit(solution)/shard_map/ppermute | solution.py:334
  8.0 2.5 %collective-permute-start.3 = (bf16[512,3584]{1,0:T(8,128)(2,1)}, bf16[512,3584]{1,0:T(8,128)(2,1)}, u32[]{:S(2)}, u32[]{:S(2)}) collective-permute-start(bf16[512,3584]{1,0:T(8,128)(2,1)} %constant_dynamic-slice_fusion.5), channel_id=1, source_target_pairs={{4,8},{8,4},{5,9},{9,5},{6,10},{10,6},{7,11},{11,7},{20,24},{24,20... | collective-permute-start | bytes 11010056 | tf_op jit(solution)/shard_map/ppermute | solution.py:333
  12.0 3.3 %all-to-all-start = ((bf16[4,16,1024]{2,1,0:T(8,128)(2,1)}), bf16[4,16,1024]{2,1,0:T(8,128)(2,1)S(1)}, u32[]{:S(2)}, u32[]{:S(2)}) async-start(bf16[4,16,1024]{2,1,0:T(8,128)(2,1)} %gather_fusion.2), calls=%async_computation | async-start | bytes 262144 | tf_op jit(solution)/shard_map/all_to_all | solution.py:340
  17.0 3.7 %gather_fusion.1 = bf16[4,16,3584]{2,1,0:T(8,128)(2,1)S(1)} fusion(bf16[64,16,3584]{2,1,0:T(8,128)(2,1)} %param.12, s32[1024]{0:T(1024)S(1)} %get-tuple-element.66), kind=kCustom, calls=%fused_computation.1 | custom fusion | bytes 917520 | tf_op jit(solution)/shard_map/gather | solution.py:339
  21.9 3.1 %convolution_convert_fusion = bf16[4,16,128]{2,1,0:T(8,128)(2,1)S(1)} fusion(bf16[4,16,3584]{2,1,0:T(8,128)(2,1)S(1)} %gather_fusion.1, bf16[4,128,3584]{2,1,0:T(8,128)(2,1)} %bitcast.5), kind=kOutput, calls=%fused_computation.12 | convolution fusion | flops 58728448 | bytes 4145152 | tf_op jit(solution)/shard_map/krf,ktf->krt/dot_general | solution.py:342
  26.2 3.3 %all-to-all-start.1 = ((bf16[4,32,128]{2,1,0:T(8,128)(2,1)}), bf16[4,32,128]{2,1,0:T(8,128)(2,1)S(1)}, u32[]{:S(2)}, u32[]{:S(2)}) async-start(bf16[4,32,128]{2,1,0:T(8,128)(2,1)} %pad_maximum_fusion.4), calls=%async_computation.1 | async-start | bytes 65536 | tf_op jit(solution)/shard_map/all_to_all | solution.py:346
  30.2 3.2 %all-to-all-done.1 = bf16[4,32,128]{2,1,0:T(8,128)(2,1)S(1)} async-done(((bf16[4,32,128]{2,1,0:T(8,128)(2,1)}), bf16[4,32,128]{2,1,0:T(8,128)(2,1)S(1)}, u32[]{:S(2)}, u32[]{:S(2)}) %all-to-all-start.1) | async-done | bytes 32800 | tf_op jit(solution)/shard_map/all_to_all | solution.py:346
  35.0 3.3 %all-to-all-start.2 = ((bf16[16,4,1024]{2,0,1:T(8,128)(2,1)}), bf16[16,4,1024]{2,0,1:T(8,128)(2,1)S(1)}, u32[]{:S(2)}, u32[]{:S(2)}) async-start(bf16[16,4,1024]{2,0,1:T(8,128)(2,1)} %bitcast.68), calls=%async_computation.2 | async-start | bytes 262144 | tf_op jit(solution)/shard_map/all_to_all | solution.py:363
  38.3 2.6 %fusion = bf16[4,16,3584]{2,1,0:T(8,128)(2,1)S(1)} fusion(bf16[4,128,3584]{2,1,0:T(8,128)(2,1)} %bitcast.5, f32[4]{0:T(128)S(1)} %convert_divide_fusion.1, bf16[4,32,128]{2,1,0:T(8,128)(2,1)S(1)} %all-to-all-done.1), kind=kOutput, calls=%fused_computation.7 | convolution fusion | flops 59179008 | bytes 4145664 | tf_op jit(solution)/shard_map/krt,ktf->krf/dot_general | solution.py:355
  43.0 2.7 %collective-permute-start.1 = (bf16[4,16,1152]{2,1,0:T(8,128)(2,1)S(1)}, bf16[4,16,1152]{2,1,0:T(8,128)(2,1)S(1)}, u32[]{:S(2)}, u32[]{:S(2)}) collective-permute-start(bf16[4,16,1152]{2,1,0:T(8,128)(2,1)S(1)} %pad_maximum_fusion.3), channel_id=1, source_target_pairs={{0,4},{4,0},{8,12},{12,8},{1,5},{5,1},{9,13},{13,9},{2,6},{6,2},{1... | collective-permute-start | bytes 442376 | tf_op jit(solution)/shard_map/ppermute | solution.py:369
  45.6 42.9 %collective-permute-done.refs_1_ = bf16[512,3584]{1,0:T(8,128)(2,1)} collective-permute-done((bf16[512,3584]{1,0:T(8,128)(2,1)}, bf16[512,3584]{1,0:T(8,128)(2,1)}, u32[]{:S(2)}, u32[]{:S(2)}) %collective-permute-start) | collective-permute-done | bytes 3670048 | tf_op jit(solution)/shard_map/ppermute | solution.py:334
  88.5 6.9 %collective-permute-start.5 = (bf16[512,3584]{1,0:T(8,128)(2,1)}, bf16[512,3584]{1,0:T(8,128)(2,1)}, u32[]{:S(2)}, u32[]{:S(2)}) collective-permute-start(bf16[512,3584]{1,0:T(8,128)(2,1)} %constant_dynamic-slice_fusion.5), channel_id=1, source_target_pairs={{0,8},{12,4},{1,9},{13,5},{2,10},{14,6},{3,11},{15,7},{16,24},{28,... | collective-permute-start | bytes 11010056 | tf_op jit(solution)/shard_map/ppermute | solution.py:379
  97.1 2.7 %fusion.1 = bf16[4,16,3584]{2,1,0:T(8,128)(2,1)S(1)} fusion(bf16[4,128,3584]{2,1,0:T(8,128)(2,1)} %bitcast.10, f32[4]{0:T(128)S(1)} %convert_divide_fusion, bf16[4,16,1152]{2,1,0:T(8,128)(2,1)S(1)} %collective-permute-done.1), kind=kOutput, calls=%fused_computation.8 | convolution fusion | flops 59179008 | bytes 4145664 | tf_op jit(solution)/shard_map/krt,ktf->krf/dot_general | solution.py:355
  99.8 3.1 %copy-done.2 = bf16[1024,3584]{1,0:T(8,128)(2,1)S(1)} copy-done((bf16[1024,3584]{1,0:T(8,128)(2,1)S(1)}, bf16[1024,3584]{1,0:T(8,128)(2,1)}, u32[]{:S(2)}) %copy-start.2) | copy-done | bytes 7340056
  102.9 13.3 %shard_map.103 = bf16[4,2,128,1024]{3,2,1,0:T(8,128)(2,1)} custom-call(s32[2]{0:T(128)S(1)} %pad_add_fusion.1.place_ref, bf16[512,3584]{1,0:T(8,128)(2,1)} %refs_0_.2, bf16[512,3584]{1,0:T(8,128)(2,1)} %collective-permute-done.refs_1_, bf16[1024,3584]{1,0:T(8,128)(2,1)S(1)} %copy-done.2), custom_call_target="tpu_custom_call" | custom-call | tf_op jit(solution)/shard_map/pallas_call | solution.py:211
  116.2 4.5 %all-to-all-start.3 = ((bf16[4,2,128,1024]{3,2,1,0:T(8,128)(2,1)}), bf16[4,2,128,1024]{3,2,1,0:T(8,128)(2,1)}, u32[]{:S(2)}, u32[]{:S(2)}) async-start(bf16[4,2,128,1024]{3,2,1,0:T(8,128)(2,1)} %shard_map.103), calls=%async_computation.3 | async-start | bytes 4194304 | tf_op jit(solution)/shard_map/all_to_all | solution.py:297
  120.7 11.5 %shard_map.104 = bf16[4,3,128,512]{3,2,1,0:T(8,128)(2,1)} custom-call(s32[2]{0:T(128)S(1)} %pad_add_fusion.1.place_ref, bf16[512,3584]{1,0:T(8,128)(2,1)} %refs_0_.2, bf16[512,3584]{1,0:T(8,128)(2,1)} %collective-permute-done.refs_1_, bf16[512,3584]{1,0:T(8,128)(2,1)} %collective-permute-done.4.refs_2_, bf16[512,3584]{1,0:T(8,128)(2,1)} %collective-permute-done.3.refs_3_.refs_1_), custom_call_target="tpu_custom_call" | custom-call | tf_op jit(solution)/shard_map/pallas_call | solution.py:211
  132.2 14.2 %all-to-all-done.3 = bf16[4,2,128,1024]{3,2,1,0:T(8,128)(2,1)} async-done(((bf16[4,2,128,1024]{3,2,1,0:T(8,128)(2,1)}), bf16[4,2,128,1024]{3,2,1,0:T(8,128)(2,1)}, u32[]{:S(2)}, u32[]{:S(2)}) %all-to-all-start.3) | async-done | bytes 2097184 | tf_op jit(solution)/shard_map/all_to_all | solution.py:297
  146.4 4.3 %all-to-all-start.4 = ((bf16[4,3,128,512]{3,2,1,0:T(8,128)(2,1)}), bf16[4,3,128,512]{3,2,1,0:T(8,128)(2,1)}, u32[]{:S(2)}, u32[]{:S(2)}) async-start(bf16[4,3,128,512]{3,2,1,0:T(8,128)(2,1)} %shard_map.104), calls=%async_computation.4 | async-start | bytes 3145728 | tf_op jit(solution)/shard_map/all_to_all | solution.py:297
  153.2 2.0 reduce_sum.46
  157.6 5.5 %shard_map.105 = (f32[32,16,3584]{2,1,0:T(8,128)}, f32[32,16,1024]{2,1,0:T(8,128)}) custom-call(s32[8]{0:T(128)S(1)} %pad_add_fusion.2.slots_ref, bf16[4,16,4608]{2,1,0:T(8,128)(2,1)S(1)} %pad_maximum_fusion.refs_0_, bf16[4,16,4608]{2,1,0:T(8,128)(2,1)S(1)} %pad_maximum_fusion.1.refs_1_), custom_call_target="tpu_custom_call" | custom-call | bytes 18874368 | tf_op jit(solution)/shard_map/pallas_call | solution.py:49
  163.1 7.8 %all-to-all-done.4 = bf16[4,3,128,512]{3,2,1,0:T(8,128)(2,1)} async-done(((bf16[4,3,128,512]{3,2,1,0:T(8,128)(2,1)}), bf16[4,3,128,512]{3,2,1,0:T(8,128)(2,1)}, u32[]{:S(2)}, u32[]{:S(2)}) %all-to-all-start.4) | async-done | bytes 1572896 | tf_op jit(solution)/shard_map/all_to_all | solution.py:297
  173.2 10.4 %shard_map.106 = (bf16[2,3,128,512]{3,2,1,0:T(8,128)(2,1)S(1)}, bf16[2,3,128,512]{3,2,1,0:T(8,128)(2,1)S(1)}) custom-call(s32[2]{0:T(128)S(1)} %pad_add_fusion.1.place_ref, bf16[512,3584]{1,0:T(8,128)(2,1)} %refs_0_.2, bf16[512,3584]{1,0:T(8,128)(2,1)} %collective-permute-done.refs_1_, bf16[512,3584]{1,0:T(8,128)(2,1)} %collective-permute-done.4.refs_2_, ...), custom_call_target="tpu_custom_call" | custom-call | tf_op jit(solution)/shard_map/pallas_call | solution.py:211
  185.1 8.1 %shard_map.107 = (bf16[2,1,128,1024]{3,2,1,0:T(8,128)(2,1)S(1)}, bf16[2,1,128,1024]{3,2,1,0:T(8,128)(2,1)S(1)}) custom-call(s32[2]{0:T(128)S(1)} %pad_add_fusion.1.place_ref, bf16[512,3584]{1,0:T(8,128)(2,1)} %collective-permute-done.10.refs_0_, bf16[512,3584]{1,0:T(8,128)(2,1)} %collective-permute-done.3.refs_3_.refs_1_, ...), custom_call_target="tpu_custom_call" | custom-call | tf_op jit(solution)/shard_map/pallas_call | solution.py:211
  195.2 5.2 %collective-permute-done.12.refs_1_ = bf16[4,16,4608]{2,1,0:T(8,128)(2,1)S(1)} collective-permute-done((bf16[4,16,4608]{2,1,0:T(8,128)(2,1)}, bf16[4,16,4608]{2,1,0:T(8,128)(2,1)S(1)}, u32[]{:S(2)}, u32[]{:S(2)}) %collective-permute-start.12) | collective-permute-done | bytes 589856 | tf_op jit(solution)/shard_map/ppermute | solution.py:408
  203.1 6.8 %collective-permute-done.15 = bf16[1,128,1024]{2,1,0:T(8,128)(2,1)S(1)} collective-permute-done((bf16[1,128,1024]{2,1,0:T(8,128)(2,1)S(1)}, bf16[1,128,1024]{2,1,0:T(8,128)(2,1)S(1)}, u32[]{:S(2)}, u32[]{:S(2)}) %collective-permute-start.15) | collective-permute-done | bytes 262176 | tf_op jit(solution)/shard_map/ppermute | solution.py:292
  210.0 3.5 %collective-permute-done.16.refs_3_ = bf16[4,16,4608]{2,1,0:T(8,128)(2,1)S(1)} collective-permute-done((bf16[4,16,4608]{2,1,0:T(8,128)(2,1)}, bf16[4,16,4608]{2,1,0:T(8,128)(2,1)S(1)}, u32[]{:S(2)}, u32[]{:S(2)}) %collective-permute-start.16) | collective-permute-done | bytes 589856 | tf_op jit(solution)/shard_map/ppermute | solution.py:410
  219.1 3.8 %shard_map.109 = (f32[32,16,3584]{2,1,0:T(8,128)}, f32[32,16,1024]{2,1,0:T(8,128)}) custom-call(s32[16]{0:T(128)S(1)} %pad_add_fusion.3.slots_ref, bf16[4,16,4608]{2,1,0:T(8,128)(2,1)} %collective-permute-done.11.refs_0_, bf16[4,16,4608]{2,1,0:T(8,128)(2,1)S(1)} %collective-permute-done.12.refs_1_, ...), custom_call_target="tpu_custom_call", output_to_operand_aliasing={{0}: (5, {}), {1}: (6, {})} | custom-call | bytes 1179648 | tf_op jit(solution)/shard_map/pallas_call | solution.py:114
  222.9 2.7 %collective-permute-done.17.refs_5_ = bf16[128,1024]{1,0:T(8,128)(2,1)S(1)} collective-permute-done((bf16[128,1024]{1,0:T(8,128)(2,1)S(1)}, bf16[128,1024]{1,0:T(8,128)(2,1)S(1)}, u32[]{:S(2)}, u32[]{:S(2)}) %collective-permute-start.17) | collective-permute-done | bytes 262176 | tf_op jit(solution)/shard_map/ppermute | solution.py:417
  225.6 4.2 %collective-permute-done.8.refs_3_ = bf16[128,1024]{1,0:T(8,128)(2,1)S(1)} collective-permute-done((bf16[128,1024]{1,0:T(8,128)(2,1)S(1)}, bf16[128,1024]{1,0:T(8,128)(2,1)S(1)}, u32[]{:S(2)}, u32[]{:S(2)}) %collective-permute-start.8) | collective-permute-done | bytes 262176 | tf_op jit(solution)/shard_map/ppermute | solution.py:415
  229.8 2.2 shard_map.108
  (90 shorter events, 30.1 us)
Async XLA Ops:
  0.6 10.2 %copy-start = (bf16[64,16,1024]{2,1,0:T(8,128)(2,1)S(1)}, bf16[64,16,1024]{2,1,0:T(8,128)(2,1)}, u32[]{:S(2)}) copy-start(bf16[64,16,1024]{2,1,0:T(8,128)(2,1)} %param.11) | copy-start | bytes 6291460
  0.7 9.9 %copy-start.8 = (s32[2048]{0:T(1024)S(1)}, s32[2048]{0:T(1024)}, u32[]{:S(2)}) copy-start(s32[2048]{0:T(1024)} %param.13) | copy-start | bytes 24580
  0.7 20.0 %copy-start.6 = (s32[64]{0:T(128)S(1)}, s32[64]{0:T(128)}, u32[]{:S(2)}) copy-start(s32[64]{0:T(128)} %param.14) | copy-start | bytes 772
  5.0 20.2 %copy-start.7 = (bf16[128,4096]{1,0:T(8,128)(2,1)S(1)}, bf16[128,4096]{1,0:T(8,128)(2,1)}, u32[]{:S(2)}) copy-start(bf16[128,4096]{1,0:T(8,128)(2,1)} %param.8) | copy-start | bytes 3145732
  5.0 83.5 %collective-permute-start = (bf16[512,3584]{1,0:T(8,128)(2,1)}, bf16[512,3584]{1,0:T(8,128)(2,1)}, u32[]{:S(2)}, u32[]{:S(2)}) collective-permute-start(bf16[512,3584]{1,0:T(8,128)(2,1)} %refs_0_.2), channel_id=1, source_target_pairs={{0,4},{4,0},{8,12},{12,8},{1,5},{5,1},{9,13},{13,9},{2,6},{6,2},{1... | collective-permute-start | bytes 11010056 | tf_op jit(solution)/shard_map/ppermute | solution.py:334
  8.0 112.6 %collective-permute-start.3 = (bf16[512,3584]{1,0:T(8,128)(2,1)}, bf16[512,3584]{1,0:T(8,128)(2,1)}, u32[]{:S(2)}, u32[]{:S(2)}) collective-permute-start(bf16[512,3584]{1,0:T(8,128)(2,1)} %constant_dynamic-slice_fusion.5), channel_id=1, source_target_pairs={{4,8},{8,4},{5,9},{9,5},{6,10},{10,6},{7,11},{11,7},{20,24},{24,20... | collective-permute-start | bytes 11010056 | tf_op jit(solution)/shard_map/ppermute | solution.py:333
  12.0 13.0 %all-to-all-start = ((bf16[4,16,1024]{2,1,0:T(8,128)(2,1)}), bf16[4,16,1024]{2,1,0:T(8,128)(2,1)S(1)}, u32[]{:S(2)}, u32[]{:S(2)}) async-start(bf16[4,16,1024]{2,1,0:T(8,128)(2,1)} %gather_fusion.2), calls=%async_computation | async-start | bytes 262144 | tf_op jit(solution)/shard_map/all_to_all | solution.py:340
  15.4 105.3 %collective-permute-start.4 = (bf16[512,3584]{1,0:T(8,128)(2,1)}, bf16[512,3584]{1,0:T(8,128)(2,1)}, u32[]{:S(2)}, u32[]{:S(2)}) collective-permute-start(bf16[512,3584]{1,0:T(8,128)(2,1)} %refs_0_.2), channel_id=1, source_target_pairs={{0,16},{16,0},{1,17},{17,1},{2,18},{18,2},{3,19},{19,3},{4,20},{20... | collective-permute-start | bytes 11010056 | tf_op jit(solution)/shard_map/ppermute | solution.py:338
  26.2 7.2 %all-to-all-start.1 = ((bf16[4,32,128]{2,1,0:T(8,128)(2,1)}), bf16[4,32,128]{2,1,0:T(8,128)(2,1)S(1)}, u32[]{:S(2)}, u32[]{:S(2)}) async-start(bf16[4,32,128]{2,1,0:T(8,128)(2,1)} %pad_maximum_fusion.4), calls=%async_computation.1 | async-start | bytes 65536 | tf_op jit(solution)/shard_map/all_to_all | solution.py:346
  35.0 7.9 %all-to-all-start.2 = ((bf16[16,4,1024]{2,0,1:T(8,128)(2,1)}), bf16[16,4,1024]{2,0,1:T(8,128)(2,1)S(1)}, u32[]{:S(2)}, u32[]{:S(2)}) async-start(bf16[16,4,1024]{2,0,1:T(8,128)(2,1)} %bitcast.68), calls=%async_computation.2 | async-start | bytes 262144 | tf_op jit(solution)/shard_map/all_to_all | solution.py:363
  43.0 52.5 %collective-permute-start.1 = (bf16[4,16,1152]{2,1,0:T(8,128)(2,1)S(1)}, bf16[4,16,1152]{2,1,0:T(8,128)(2,1)S(1)}, u32[]{:S(2)}, u32[]{:S(2)}) collective-permute-start(bf16[4,16,1152]{2,1,0:T(8,128)(2,1)S(1)} %pad_maximum_fusion.3), channel_id=1, source_target_pairs={{0,4},{4,0},{8,12},{12,8},{1,5},{5,1},{9,13},{13,9},{2,6},{6,2},{1... | collective-permute-start | bytes 442376 | tf_op jit(solution)/shard_map/ppermute | solution.py:369
  88.5 84.7 %collective-permute-start.5 = (bf16[512,3584]{1,0:T(8,128)(2,1)}, bf16[512,3584]{1,0:T(8,128)(2,1)}, u32[]{:S(2)}, u32[]{:S(2)}) collective-permute-start(bf16[512,3584]{1,0:T(8,128)(2,1)} %constant_dynamic-slice_fusion.5), channel_id=1, source_target_pairs={{0,8},{12,4},{1,9},{13,5},{2,10},{14,6},{3,11},{15,7},{16,24},{28,... | collective-permute-start | bytes 11010056 | tf_op jit(solution)/shard_map/ppermute | solution.py:379
  95.5 89.7 %collective-permute-start.10 = (bf16[512,3584]{1,0:T(8,128)(2,1)}, bf16[512,3584]{1,0:T(8,128)(2,1)}, u32[]{:S(2)}, u32[]{:S(2)}) collective-permute-start(bf16[512,3584]{1,0:T(8,128)(2,1)} %collective-permute-done.refs_1_), channel_id=1, source_target_pairs={{0,16},{16,0},{1,17},{17,1},{2,18},{18,2},{3,19},{19,3},{4,20},{20... | collective-permute-start | bytes 11010056 | tf_op jit(solution)/shard_map/ppermute | solution.py:380
  116.2 30.2 %all-to-all-start.3 = ((bf16[4,2,128,1024]{3,2,1,0:T(8,128)(2,1)}), bf16[4,2,128,1024]{3,2,1,0:T(8,128)(2,1)}, u32[]{:S(2)}, u32[]{:S(2)}) async-start(bf16[4,2,128,1024]{3,2,1,0:T(8,128)(2,1)} %shard_map.103), calls=%async_computation.3 | async-start | bytes 4194304 | tf_op jit(solution)/shard_map/all_to_all | solution.py:297
  120.7 30.1 %copy-start.9 = (s32[64]{0:T(128)S(1)}, s32[64]{0:T(128)}, u32[]{:S(2)}) copy-start(s32[64]{0:T(128)} %param.15) | copy-start | bytes 772
  146.4 24.5 %all-to-all-start.4 = ((bf16[4,3,128,512]{3,2,1,0:T(8,128)(2,1)}), bf16[4,3,128,512]{3,2,1,0:T(8,128)(2,1)}, u32[]{:S(2)}, u32[]{:S(2)}) async-start(bf16[4,3,128,512]{3,2,1,0:T(8,128)(2,1)} %shard_map.104), calls=%async_computation.4 | async-start | bytes 3145728 | tf_op jit(solution)/shard_map/all_to_all | solution.py:297
  151.6 32.0 %collective-permute-start.11 = (bf16[4,16,4608]{2,1,0:T(8,128)(2,1)S(1)}, bf16[4,16,4608]{2,1,0:T(8,128)(2,1)}, u32[]{:S(2)}, u32[]{:S(2)}) collective-permute-start(bf16[4,16,4608]{2,1,0:T(8,128)(2,1)S(1)} %pad_maximum_fusion.refs_0_), channel_id=1, source_target_pairs={{4,8},{8,4},{5,9},{9,5},{6,10},{10,6},{7,11},{11,7},{20,24},{24,20... | collective-permute-start | bytes 1769480 | tf_op jit(solution)/shard_map/ppermute | solution.py:390
  155.2 38.1 %collective-permute-start.13 = (bf16[4,16,4608]{2,1,0:T(8,128)(2,1)S(1)}, bf16[4,16,4608]{2,1,0:T(8,128)(2,1)}, u32[]{:S(2)}, u32[]{:S(2)}) collective-permute-start(bf16[4,16,4608]{2,1,0:T(8,128)(2,1)S(1)} %pad_maximum_fusion.1.refs_1_), channel_id=1, source_target_pairs={{4,8},{8,4},{5,9},{9,5},{6,10},{10,6},{7,11},{11,7},{20,24},{24,20... | collective-permute-start | bytes 1769480 | tf_op jit(solution)/shard_map/ppermute | solution.py:391
  157.5 27.6 %collective-permute-start.2 = (bf16[128,1024]{1,0:T(8,128)(2,1)S(1)}, bf16[128,1024]{1,0:T(8,128)(2,1)S(1)}, u32[]{:S(2)}, u32[]{:S(2)}) collective-permute-start(bf16[128,1024]{1,0:T(8,128)(2,1)S(1)} %get-tuple-element.53), channel_id=1, source_target_pairs={{0,4},{4,0},{8,12},{12,8},{1,5},{5,1},{9,13},{13,9},{2,6},{6,2},{1... | collective-permute-start | bytes 786440 | tf_op jit(solution)/shard_map/ppermute | solution.py:392
  183.6 16.8 %collective-permute-start.12 = (bf16[4,16,4608]{2,1,0:T(8,128)(2,1)}, bf16[4,16,4608]{2,1,0:T(8,128)(2,1)S(1)}, u32[]{:S(2)}, u32[]{:S(2)}) collective-permute-start(bf16[4,16,4608]{2,1,0:T(8,128)(2,1)} %collective-permute-done.11.refs_0_), channel_id=1, source_target_pairs={{4,0},{8,12},{5,1},{9,13},{6,2},{10,14},{7,3},{11,15},{20,16},{24,... | collective-permute-start | bytes 1769480 | tf_op jit(solution)/shard_map/ppermute | solution.py:408
  185.1 8.2 %copy-start.4 = (bf16[128,1024]{1,0:T(8,128)(2,1)}, bf16[128,1024]{1,0:T(8,128)(2,1)S(1)}, u32[]{:S(2)}) copy-start(bf16[128,1024]{1,0:T(8,128)(2,1)S(1)} %collective-permute-done.2.refs_1_) | copy-start | bytes 786436
  193.3 7.1 %collective-permute-start.14 = (bf16[2,1,128,1024]{3,2,1,0:T(8,128)(2,1)S(1)}, bf16[2,1,128,1024]{3,2,1,0:T(8,128)(2,1)S(1)}, u32[]{:S(2)}, u32[]{:S(2)}) collective-permute-start(bf16[2,1,128,1024]{3,2,1,0:T(8,128)(2,1)S(1)} %get-tuple-element.43), channel_id=1, source_target_pairs={{0,1},{1,0},{2,3},{3,2},{4,5},{5,4},{6,7},{7,6},{8,9},{9,8},{10,11... | collective-permute-start | bytes 1572872 | tf_op jit(solution)/shard_map/ppermute | solution.py:286
  193.4 8.8 %collective-permute-start.6 = (bf16[2,3,128,512]{3,2,1,0:T(8,128)(2,1)S(1)}, bf16[2,3,128,512]{3,2,1,0:T(8,128)(2,1)S(1)}, u32[]{:S(2)}, u32[]{:S(2)}) collective-permute-start(bf16[2,3,128,512]{3,2,1,0:T(8,128)(2,1)S(1)} %get-tuple-element.36), channel_id=1, source_target_pairs={{0,1},{1,0},{2,3},{3,2},{4,5},{5,4},{6,7},{7,6},{8,9},{9,8},{10,11... | collective-permute-start | bytes 2359304 | tf_op jit(solution)/shard_map/ppermute | solution.py:286
  193.9 19.7 %collective-permute-start.16 = (bf16[4,16,4608]{2,1,0:T(8,128)(2,1)}, bf16[4,16,4608]{2,1,0:T(8,128)(2,1)S(1)}, u32[]{:S(2)}, u32[]{:S(2)}) collective-permute-start(bf16[4,16,4608]{2,1,0:T(8,128)(2,1)} %collective-permute-done.13.refs_2_), channel_id=1, source_target_pairs={{4,0},{8,12},{5,1},{9,13},{6,2},{10,14},{7,3},{11,15},{20,16},{24,... | collective-permute-start | bytes 1769480 | tf_op jit(solution)/shard_map/ppermute | solution.py:410
  200.6 9.3 %collective-permute-start.15 = (bf16[1,128,1024]{2,1,0:T(8,128)(2,1)S(1)}, bf16[1,128,1024]{2,1,0:T(8,128)(2,1)S(1)}, u32[]{:S(2)}, u32[]{:S(2)}) collective-permute-start(bf16[1,128,1024]{2,1,0:T(8,128)(2,1)S(1)} %fusion.9), channel_id=1, source_target_pairs={{0,2},{2,0},{1,3},{3,1},{4,6},{6,4},{5,7},{7,5},{8,10},{10,8},{9,1... | collective-permute-start | bytes 786440 | tf_op jit(solution)/shard_map/ppermute | solution.py:292
  202.5 13.4 %collective-permute-start.7 = (bf16[3,128,512]{2,1,0:T(8,128)(2,1)S(1)}, bf16[3,128,512]{2,1,0:T(8,128)(2,1)S(1)}, u32[]{:S(2)}, u32[]{:S(2)}) collective-permute-start(bf16[3,128,512]{2,1,0:T(8,128)(2,1)S(1)} %fusion.7), channel_id=1, source_target_pairs={{0,2},{2,0},{1,3},{3,1},{4,6},{6,4},{5,7},{7,5},{8,10},{10,8},{9,1... | collective-permute-start | bytes 1179656 | tf_op jit(solution)/shard_map/ppermute | solution.py:292
  213.6 12.1 %collective-permute-start.17 = (bf16[128,1024]{1,0:T(8,128)(2,1)S(1)}, bf16[128,1024]{1,0:T(8,128)(2,1)S(1)}, u32[]{:S(2)}, u32[]{:S(2)}) collective-permute-start(bf16[128,1024]{1,0:T(8,128)(2,1)S(1)} %fusion.8), channel_id=1, source_target_pairs={{4,16},{8,28},{20,0},{24,12},{5,17},{9,29},{21,1},{25,13},{6,18},{... | collective-permute-start | bytes 786440 | tf_op jit(solution)/shard_map/ppermute | solution.py:417
  216.1 13.7 %collective-permute-start.8 = (bf16[128,1024]{1,0:T(8,128)(2,1)S(1)}, bf16[128,1024]{1,0:T(8,128)(2,1)S(1)}, u32[]{:S(2)}, u32[]{:S(2)}) collective-permute-start(bf16[128,1024]{1,0:T(8,128)(2,1)S(1)} %get-tuple-element.52), channel_id=1, source_target_pairs={{4,0},{8,12},{5,1},{9,13},{6,2},{10,14},{7,3},{11,15},{20,16},{24,... | collective-permute-start | bytes 786440 | tf_op jit(solution)/shard_map/ppermute | solution.py:415
  217.4 12.4 %collective-permute-start.9 = (bf16[128,1024]{1,0:T(8,128)(2,1)S(1)}, bf16[128,1024]{1,0:T(8,128)(2,1)S(1)}, u32[]{:S(2)}, u32[]{:S(2)}) collective-permute-start(bf16[128,1024]{1,0:T(8,128)(2,1)S(1)} %get-tuple-element.50), channel_id=1, source_target_pairs={{0,16},{16,0},{1,17},{17,1},{2,18},{18,2},{3,19},{19,3},{4,20},{20... | collective-permute-start | bytes 786440 | tf_op jit(solution)/shard_map/ppermute | solution.py:416
  219.1 10.7 %copy-start.3 = (bf16[128,1024]{1,0:T(8,128)(2,1)S(1)}, bf16[128,1024]{1,0:T(8,128)(2,1)}, u32[]{:S(2)}) copy-start(bf16[128,1024]{1,0:T(8,128)(2,1)} %get-tuple-element.54.refs_0_) | copy-start | bytes 786436
  219.1 10.7 %copy-start.5 = (bf16[128,1024]{1,0:T(8,128)(2,1)S(1)}, bf16[128,1024]{1,0:T(8,128)(2,1)}, u32[]{:S(2)}) copy-start(bf16[128,1024]{1,0:T(8,128)(2,1)} %copy-done.4) | copy-start | bytes 786436
  219.1 13.0 %copy-start.1 = (bf16[64,16,1024]{2,1,0:T(8,128)(2,1)S(1)}, bf16[64,16,1024]{2,1,0:T(8,128)(2,1)}, u32[]{:S(2)}) copy-start(bf16[64,16,1024]{2,1,0:T(8,128)(2,1)} %param.11) | copy-start | bytes 6291460
  (1 other events, 3.1 us)

commit v7 on v6

--- a/solution.py
+++ b/solution.py
@@ -329,12 +329,20 @@
     tenants = lax.dynamic_slice_in_dim(all_tenants, z * tile_count, tile_count)
     half = frozen_weight.shape[0] // 2
 
-    crossing = lax.dynamic_slice_in_dim(frozen_weight, rep * half, half, 0)
-    near = lax.ppermute(crossing, "dp", MIDDLE)
-    partner_dy = lax.ppermute(after(grad_out, crossing), "dp", PARTNER)
+    def rows_of_half(start, count, *events):
+        first = rep * half + start
+        if events:
+            first = after(first, *events)
+        return lax.dynamic_slice_in_dim(frozen_weight, first, count, 0)
+
+    quarter = half // 2
+    early_rows = rows_of_half(0, quarter)
+    late_rows = rows_of_half(quarter, quarter, early_rows)
+    near = [lax.ppermute(early_rows, "dp", MIDDLE), lax.ppermute(late_rows, "dp", MIDDLE)]
+    partner_dy = lax.ppermute(grad_out, "dp", PARTNER)
 
     dy_tiles = grad_out.reshape(tile_count, TILE, ff_shard)
-    down_sel = adapter_down[after(tenants, crossing)]
+    down_sel = adapter_down[after(tenants, late_rows)]
     other_dy = lax.ppermute(after(grad_out, down_sel), "rep", OTHER_REP)
     up_sel = adapter_up[tenants]
     own_down = lax.all_to_all(down_sel, "tensor", split_axis=0, concat_axis=2, tiled=True)[0]
@@ -376,15 +384,16 @@
         scale_of(partner_tenants), from_partner[:, :, :TILE], partner_dy
     )
     partner_grads = jnp.concatenate([partner_up, from_partner[:, :, TILE:]], axis=2)
-    far = lax.ppermute(after(crossing, partner_dy), "dp", OUTER_TO_MIDDLE)
+    far_rows = rows_of_half(0, half, late_rows, down_sel)
+    far = lax.ppermute(after(far_rows, from_partner, partner_dy), "dp", OUTER_TO_MIDDLE)
     partner_other_dy = lax.ppermute(partner_dy, "rep", OTHER_REP)
 
     events = (partner_dy, tile_grads, partner_grads)
     own_terms = product_terms([after(grad_out, *events), partner_dy], [frozen_weight], place, 1)
     own_sum = sum_by_swap(own_terms)
 
-    groups = [after(grad_out, near, own_terms[0]), partner_dy, other_dy]
-    near_terms = product_terms(groups, [near], place, 1)
+    groups = [after(grad_out, *near, own_terms[0]), partner_dy, other_dy]
+    near_terms = product_terms(groups, near, place, 1)
     near_sum = sum_by_swap(near_terms)
 
     near_grads = lax.ppermute(after(tile_grads, near_terms[0]), "dp", MIDDLE)
@@ -403,7 +412,7 @@
     groups = [after(grad_out, own_sum, near_sum, grad_up, grad_down), partner_dy, other_dy]
     far_terms = product_terms(groups, [far], place, 2)
     outer_terms = product_terms(
-        [after(partner_other_dy, far_terms[0], near_grads, partner_block)], [near, far], place, 2
+        [after(partner_other_dy, far_terms[0], near_grads, partner_block)], near + [far], place, 2
     )
     near_grads_out = lax.ppermute(after(near_grads, far_terms[0]), "dp", OUTWARD)
     outer_got = from_other_core(after(outer_terms[0], far_grads))

time: 233 us -> 233 us (level)
  waiting for transfers between devices: 94.4 us -> 81.5 us
  local copies, waits for them, and re-layouts: 16.6 us -> 29.5 us
    ppermute x3 -> x4, waiting for transfers between devices: 43.5 us -> 0.01 us  [the longest x1 0.01 us: line_of_four(): partner_dy = lax.ppermute(grad_out, 'dp', PARTNER)]
    ppermute x1, waiting for transfers between devices: 0.01 us -> 29.5 us  [line_of_four(): from_partner = lax.ppermute(to_partner, 'dp', PARTNER)]
    dynamic_slice x1 -> x3, local copies, waits for them, and re-layouts: 4.34 us -> 10.9 us  [rows_of_half(): return lax.dynamic_slice_in_dim(frozen_weight, first, count, 0)]
    unnamed x21 -> x31, local copies, waits for them, and re-layouts: 3.17 us -> 9.44 us
    all_to_all x1, waiting for transfers between devices: 1.96 us -> 4.52 us  [line_of_four(): lax.all_to_all(own_tile_down, 'tensor', split_axis=1, concat_axis=0, tile...]
    ppermute x3 -> x4, starting transfers between devices: 12.4 us -> 13.6 us  [the longest x1 6.58 us: line_of_four(): lax.ppermute(after(far_rows, from_partner, partner_dy), 'dp', OUTER_TO_MI...]
  transfers between devices with their start and end apart: 23 -> 24, of which waited for: 12 -> 12; matrix products, arithmetic and copies ran while one was open for 11% -> 16% of each run, Pallas kernels for 23% -> 22%
where the time goes in v7:
time: 233 us; the launch traced here: 231 us
  waiting for transfers between devices  81.5 us (35%)
  Pallas kernels  53.1 us (23%)
  starting transfers between devices  49.6 us (21%)
  local copies, waits for them, and re-layouts  29.5 us (13%)
  matrix products  9.8 us (4%)
  other arithmetic  6.73 us (3%)
    pallas_call x4, Pallas kernels, product_terms(): pl.pallas_call(functools.partial(terms_kernel, len(groups), out_count), g...  41.6 us
    ppermute x1, waiting for transfers between devices, line_of_four(): from_partner = lax.ppermute(to_partner, 'dp', PARTNER)  29.5 us
    all_to_all x2, waiting for transfers between devices, sum_by_swap(): lax.all_to_all(terms[0], 'tensor', split_axis=0, concat_axis=0, tiled=True)  20.3 us
    dynamic_slice x3, local copies, waits for them, and re-layouts, rows_of_half(): return lax.dynamic_slice_in_dim(frozen_weight, first, count, 0)  10.9 us
    unnamed x31, local copies, waits for them, and re-layouts  9.44 us
    all_to_all x2, starting transfers between devices, sum_by_swap(): lax.all_to_all(terms[0], 'tensor', split_axis=0, concat_axis=0, tiled=True)  8.79 us
    ppermute x2, waiting for transfers between devices, sum_of_chips(): got = lax.ppermute(sent, 'tensor', [(0, 2), (2, 0), (1, 3), (3, 1)])  8.57 us
    ppermute x1, starting transfers between devices, line_of_four(): lax.ppermute(after(far_rows, from_partner, partner_dy), 'dp', OUTER_TO_MI...  6.58 us
  transfers between devices with their start and end apart: 24, of which 12 were waited for; matrix products, arithmetic and copies ran while one was open for 16% of the time, Pallas kernels for 22%

profile of v7, /device:TPU:0, one launch (start us, length us, event | category | flops | bytes accessed | tf_op | source)
XLA Modules:
  0.0 231.5 jit_solution(2999771583419898753)
XLA Ops:
  0.6 3.1 %collective-permute-start = (bf16[512,3584]{1,0:T(8,128)(2,1)}, bf16[512,3584]{1,0:T(8,128)(2,1)}, u32[]{:S(2)}, u32[]{:S(2)}) collective-permute-start(bf16[512,3584]{1,0:T(8,128)(2,1)} %refs_0_.2), channel_id=1, source_target_pairs={{0,4},{4,0},{8,12},{12,8},{1,5},{5,1},{9,13},{13,9},{2,6},{6,2},{1... | collective-permute-start | bytes 11010056 | tf_op jit(solution)/shard_map/ppermute | solution.py:342
  3.7 2.8 %constant_dynamic-slice_fusion.7 = bf16[256,3584]{1,0:T(8,128)(2,1)} fusion(bf16[1024,3584]{1,0:T(8,128)(2,1)} %refs_2_.1, s32[]{:T(128)S(6)} %select_n.102), kind=kLoop, calls=%fused_computation.64 | loop fusion | bytes 3670020 | tf_op jit(solution)/shard_map/dynamic_slice | solution.py:336
  8.6 3.3 %constant_dynamic-slice_fusion.6 = bf16[256,3584]{1,0:T(8,128)(2,1)} fusion(bf16[1024,3584]{1,0:T(8,128)(2,1)} %refs_2_.1, s32[]{:T(128)S(6)} %select_n.103), kind=kLoop, calls=%fused_computation.63 | loop fusion | bytes 3670020 | tf_op jit(solution)/shard_map/dynamic_slice | solution.py:336
  15.3 3.3 %all-to-all-start = ((bf16[4,16,1024]{2,1,0:T(8,128)(2,1)}), bf16[4,16,1024]{2,1,0:T(8,128)(2,1)S(1)}, u32[]{:S(2)}, u32[]{:S(2)}) async-start(bf16[4,16,1024]{2,1,0:T(8,128)(2,1)} %gather_fusion.2), calls=%async_computation | async-start | bytes 262144 | tf_op jit(solution)/shard_map/all_to_all | solution.py:348
  20.2 3.7 %gather_fusion.1 = bf16[4,16,3584]{2,1,0:T(8,128)(2,1)S(1)} fusion(bf16[64,16,3584]{2,1,0:T(8,128)(2,1)} %param.12, s32[1024]{0:T(1024)S(1)} %get-tuple-element.68), kind=kCustom, calls=%fused_computation.1 | custom fusion | bytes 917520 | tf_op jit(solution)/shard_map/gather | solution.py:347
  24.5 3.1 %convolution_convert_fusion = bf16[4,16,128]{2,1,0:T(8,128)(2,1)S(1)} fusion(bf16[4,16,3584]{2,1,0:T(8,128)(2,1)S(1)} %gather_fusion.1, bf16[4,128,3584]{2,1,0:T(8,128)(2,1)} %bitcast.69), kind=kOutput, calls=%fused_computation.12 | convolution fusion | flops 58728448 | bytes 4145152 | tf_op jit(solution)/shard_map/krf,ktf->krt/dot_general | solution.py:350
  27.6 4.8 %constant_dynamic-slice_fusion.2 = bf16[512,3584]{1,0:T(8,128)(2,1)} fusion(bf16[1024,3584]{1,0:T(8,128)(2,1)} %refs_2_.1, s32[]{:T(128)S(6)} %select_n.112), kind=kLoop, calls=%fused_computation.59 | loop fusion | bytes 7340036 | tf_op jit(solution)/shard_map/dynamic_slice | solution.py:336
  34.3 3.3 %all-to-all-start.1 = ((bf16[4,32,128]{2,1,0:T(8,128)(2,1)}), bf16[4,32,128]{2,1,0:T(8,128)(2,1)S(1)}, u32[]{:S(2)}, u32[]{:S(2)}) async-start(bf16[4,32,128]{2,1,0:T(8,128)(2,1)} %pad_maximum_fusion.4), calls=%async_computation.1 | async-start | bytes 65536 | tf_op jit(solution)/shard_map/all_to_all | solution.py:354
  38.3 3.2 %all-to-all-done.1 = bf16[4,32,128]{2,1,0:T(8,128)(2,1)S(1)} async-done(((bf16[4,32,128]{2,1,0:T(8,128)(2,1)}), bf16[4,32,128]{2,1,0:T(8,128)(2,1)S(1)}, u32[]{:S(2)}, u32[]{:S(2)}) %all-to-all-start.1) | async-done | bytes 32800 | tf_op jit(solution)/shard_map/all_to_all | solution.py:354
  43.1 3.3 %all-to-all-start.2 = ((bf16[16,4,1024]{2,0,1:T(8,128)(2,1)}), bf16[16,4,1024]{2,0,1:T(8,128)(2,1)S(1)}, u32[]{:S(2)}, u32[]{:S(2)}) async-start(bf16[16,4,1024]{2,0,1:T(8,128)(2,1)} %bitcast.68), calls=%async_computation.2 | async-start | bytes 262144 | tf_op jit(solution)/shard_map/all_to_all | solution.py:371
  46.5 4.5 %all-to-all-done.2 = bf16[16,4,1024]{2,0,1:T(8,128)(2,1)S(1)} async-done(((bf16[16,4,1024]{2,0,1:T(8,128)(2,1)}), bf16[16,4,1024]{2,0,1:T(8,128)(2,1)S(1)}, u32[]{:S(2)}, u32[]{:S(2)}) %all-to-all-start.2) | async-done | bytes 131104 | tf_op jit(solution)/shard_map/all_to_all | solution.py:371
  51.0 3.3 %collective-permute-start.1 = (bf16[4,16,1152]{2,1,0:T(8,128)(2,1)S(1)}, bf16[4,16,1152]{2,1,0:T(8,128)(2,1)S(1)}, u32[]{:S(2)}, u32[]{:S(2)}) collective-permute-start(bf16[4,16,1152]{2,1,0:T(8,128)(2,1)S(1)} %pad_maximum_fusion.3), channel_id=1, source_target_pairs={{0,4},{4,0},{8,12},{12,8},{1,5},{5,1},{9,13},{13,9},{2,6},{6,2},{1... | collective-permute-start | bytes 442376 | tf_op jit(solution)/shard_map/ppermute | solution.py:377
  54.3 2.6 %fusion = bf16[4,16,3584]{2,1,0:T(8,128)(2,1)S(1)} fusion(bf16[4,128,3584]{2,1,0:T(8,128)(2,1)} %bitcast.70, f32[4]{0:T(128)S(1)} %convert_divide_fusion.1, bf16[4,32,128]{2,1,0:T(8,128)(2,1)S(1)} %all-to-all-done.1), kind=kOutput, calls=%fused_computation.7 | convolution fusion | flops 59179008 | bytes 4145664 | tf_op jit(solution)/shard_map/krt,ktf->krf/dot_general | solution.py:363
  56.9 29.5 %collective-permute-done.1 = bf16[4,16,1152]{2,1,0:T(8,128)(2,1)S(1)} collective-permute-done((bf16[4,16,1152]{2,1,0:T(8,128)(2,1)S(1)}, bf16[4,16,1152]{2,1,0:T(8,128)(2,1)S(1)}, u32[]{:S(2)}, u32[]{:S(2)}) %collective-permute-start.1) | collective-permute-done | bytes 147488 | tf_op jit(solution)/shard_map/ppermute | solution.py:377
  86.4 6.6 %collective-permute-start.6 = (bf16[512,3584]{1,0:T(8,128)(2,1)}, bf16[512,3584]{1,0:T(8,128)(2,1)}, u32[]{:S(2)}, u32[]{:S(2)}) collective-permute-start(bf16[512,3584]{1,0:T(8,128)(2,1)} %constant_dynamic-slice_fusion.2), channel_id=1, source_target_pairs={{0,8},{12,4},{1,9},{13,5},{2,10},{14,6},{3,11},{15,7},{16,24},{28,... | collective-permute-start | bytes 11010056 | tf_op jit(solution)/shard_map/ppermute | solution.py:388
  94.7 2.8 %fusion.1 = bf16[4,16,3584]{2,1,0:T(8,128)(2,1)S(1)} fusion(bf16[4,128,3584]{2,1,0:T(8,128)(2,1)} %bitcast.10, f32[4]{0:T(128)S(1)} %convert_divide_fusion, bf16[4,16,1152]{2,1,0:T(8,128)(2,1)S(1)} %collective-permute-done.1), kind=kOutput, calls=%fused_computation.8 | convolution fusion | flops 59179008 | bytes 4145664 | tf_op jit(solution)/shard_map/krt,ktf->krf/dot_general | solution.py:363
  97.8 3.1 %copy-done.5 = bf16[1024,3584]{1,0:T(8,128)(2,1)S(1)} copy-done((bf16[1024,3584]{1,0:T(8,128)(2,1)S(1)}, bf16[1024,3584]{1,0:T(8,128)(2,1)}, u32[]{:S(2)}) %copy-start.5) | copy-done | bytes 7340056
  100.9 13.3 %shard_map.103 = bf16[4,2,128,1024]{3,2,1,0:T(8,128)(2,1)} custom-call(s32[2]{0:T(128)S(1)} %pad_add_fusion.1.place_ref, bf16[512,3584]{1,0:T(8,128)(2,1)S(1)} %copy-done.2, bf16[512,3584]{1,0:T(8,128)(2,1)} %collective-permute-done.refs_1_, bf16[1024,3584]{1,0:T(8,128)(2,1)S(1)} %copy-done.5), custom_call_target="tpu_custom_call" | custom-call | tf_op jit(solution)/shard_map/pallas_call | solution.py:211
  114.2 4.5 %all-to-all-start.3 = ((bf16[4,2,128,1024]{3,2,1,0:T(8,128)(2,1)}), bf16[4,2,128,1024]{3,2,1,0:T(8,128)(2,1)}, u32[]{:S(2)}, u32[]{:S(2)}) async-start(bf16[4,2,128,1024]{3,2,1,0:T(8,128)(2,1)} %shard_map.103), calls=%async_computation.3 | async-start | bytes 4194304 | tf_op jit(solution)/shard_map/all_to_all | solution.py:297
  120.7 10.0 %shard_map.104 = bf16[4,3,128,512]{3,2,1,0:T(8,128)(2,1)S(1)} custom-call(s32[2]{0:T(128)S(1)} %pad_add_fusion.1.place_ref, bf16[512,3584]{1,0:T(8,128)(2,1)S(1)} %copy-done.3, bf16[512,3584]{1,0:T(8,128)(2,1)} %collective-permute-done.refs_1_, bf16[512,3584]{1,0:T(8,128)(2,1)} %collective-permute-done.5.refs_2_, ...), custom_call_target="tpu_custom_call" | custom-call | tf_op jit(solution)/shard_map/pallas_call | solution.py:211
  131.9 12.5 %all-to-all-done.3 = bf16[4,2,128,1024]{3,2,1,0:T(8,128)(2,1)} async-done(((bf16[4,2,128,1024]{3,2,1,0:T(8,128)(2,1)}), bf16[4,2,128,1024]{3,2,1,0:T(8,128)(2,1)}, u32[]{:S(2)}, u32[]{:S(2)}) %all-to-all-start.3) | async-done | bytes 2097184 | tf_op jit(solution)/shard_map/all_to_all | solution.py:297
  144.4 4.3 %all-to-all-start.4 = ((bf16[4,3,128,512]{3,2,1,0:T(8,128)(2,1)}), bf16[4,3,128,512]{3,2,1,0:T(8,128)(2,1)}, u32[]{:S(2)}, u32[]{:S(2)}) async-start(bf16[4,3,128,512]{3,2,1,0:T(8,128)(2,1)} %copy-done.6), calls=%async_computation.4 | async-start | bytes 3145728 | tf_op jit(solution)/shard_map/all_to_all | solution.py:297
  155.6 5.5 %shard_map.105 = (f32[32,16,3584]{2,1,0:T(8,128)}, f32[32,16,1024]{2,1,0:T(8,128)}) custom-call(s32[8]{0:T(128)S(1)} %pad_add_fusion.2.slots_ref, bf16[4,16,4608]{2,1,0:T(8,128)(2,1)S(1)} %pad_maximum_fusion.refs_0_, bf16[4,16,4608]{2,1,0:T(8,128)(2,1)S(1)} %pad_maximum_fusion.1.refs_1_), custom_call_target="tpu_custom_call" | custom-call | bytes 18874368 | tf_op jit(solution)/shard_map/pallas_call | solution.py:49
  161.0 7.9 %all-to-all-done.4 = bf16[4,3,128,512]{3,2,1,0:T(8,128)(2,1)} async-done(((bf16[4,3,128,512]{3,2,1,0:T(8,128)(2,1)}), bf16[4,3,128,512]{3,2,1,0:T(8,128)(2,1)}, u32[]{:S(2)}, u32[]{:S(2)}) %all-to-all-start.4) | async-done | bytes 1572896 | tf_op jit(solution)/shard_map/all_to_all | solution.py:297
  168.9 2.5 %reduce_sum.47 = bf16[3,128,512]{2,1,0:T(8,128)(2,1)} reduce(bf16[4,3,128,512]{3,2,1,0:T(8,128)(2,1)} %all-to-all-done.4, bf16[]{:T(256)} %constant.72.clone.1), dimensions={0}, to_apply=%region_2.3 | reduce | flops 589824 | bytes 1966082 | tf_op jit(solution)/shard_map/reduce_sum | solution.py:298
  173.4 10.1 %shard_map.106 = (bf16[2,3,128,512]{3,2,1,0:T(8,128)(2,1)S(1)}, bf16[2,3,128,512]{3,2,1,0:T(8,128)(2,1)S(1)}) custom-call(s32[2]{0:T(128)S(1)} %pad_add_fusion.1.place_ref, bf16[512,3584]{1,0:T(8,128)(2,1)S(1)} %copy-done.4, bf16[512,3584]{1,0:T(8,128)(2,1)} %collective-permute-done.refs_1_, bf16[512,3584]{1,0:T(8,128)(2,1)} %collective-permute-done.5.refs_2_, ...), custom_call_target="tpu_custom_call" | custom-call | tf_op jit(solution)/shard_map/pallas_call | solution.py:211
  185.6 8.1 %shard_map.107 = (bf16[2,1,128,1024]{3,2,1,0:T(8,128)(2,1)S(1)}, bf16[2,1,128,1024]{3,2,1,0:T(8,128)(2,1)S(1)}) custom-call(s32[2]{0:T(128)S(1)} %pad_add_fusion.1.place_ref, bf16[512,3584]{1,0:T(8,128)(2,1)} %collective-permute-done.11.refs_0_, bf16[256,3584]{1,0:T(8,128)(2,1)} %collective-permute-done.3.refs_3_.refs_1_, ...), custom_call_target="tpu_custom_call" | custom-call | tf_op jit(solution)/shard_map/pallas_call | solution.py:211
  195.7 5.6 %collective-permute-done.13.refs_1_ = bf16[4,16,4608]{2,1,0:T(8,128)(2,1)S(1)} collective-permute-done((bf16[4,16,4608]{2,1,0:T(8,128)(2,1)}, bf16[4,16,4608]{2,1,0:T(8,128)(2,1)S(1)}, u32[]{:S(2)}, u32[]{:S(2)}) %collective-permute-start.13) | collective-permute-done | bytes 589856 | tf_op jit(solution)/shard_map/ppermute | solution.py:417
  204.0 6.9 %collective-permute-done.16 = bf16[1,128,1024]{2,1,0:T(8,128)(2,1)S(1)} collective-permute-done((bf16[1,128,1024]{2,1,0:T(8,128)(2,1)S(1)}, bf16[1,128,1024]{2,1,0:T(8,128)(2,1)S(1)}, u32[]{:S(2)}, u32[]{:S(2)}) %collective-permute-start.16) | collective-permute-done | bytes 262176 | tf_op jit(solution)/shard_map/ppermute | solution.py:292
  218.0 3.8 %shard_map.109 = (f32[32,16,3584]{2,1,0:T(8,128)}, f32[32,16,1024]{2,1,0:T(8,128)}) custom-call(s32[16]{0:T(128)S(1)} %pad_add_fusion.3.slots_ref, bf16[4,16,4608]{2,1,0:T(8,128)(2,1)} %collective-permute-done.12.refs_0_, bf16[4,16,4608]{2,1,0:T(8,128)(2,1)S(1)} %collective-permute-done.13.refs_1_, ...), custom_call_target="tpu_custom_call", output_to_operand_aliasing={{0}: (5, {}), {1}: (6, {})} | custom-call | bytes 1179648 | tf_op jit(solution)/shard_map/pallas_call | solution.py:114
  221.8 3.5 %collective-permute-done.18.refs_5_ = bf16[128,1024]{1,0:T(8,128)(2,1)S(1)} collective-permute-done((bf16[128,1024]{1,0:T(8,128)(2,1)S(1)}, bf16[128,1024]{1,0:T(8,128)(2,1)S(1)}, u32[]{:S(2)}, u32[]{:S(2)}) %collective-permute-start.18) | collective-permute-done | bytes 262176 | tf_op jit(solution)/shard_map/ppermute | solution.py:426
  225.3 3.4 %collective-permute-done.9.refs_3_ = bf16[128,1024]{1,0:T(8,128)(2,1)S(1)} collective-permute-done((bf16[128,1024]{1,0:T(8,128)(2,1)S(1)}, bf16[128,1024]{1,0:T(8,128)(2,1)S(1)}, u32[]{:S(2)}, u32[]{:S(2)}) %collective-permute-start.9) | collective-permute-done | bytes 262176 | tf_op jit(solution)/shard_map/ppermute | solution.py:424
  (104 shorter events, 42.3 us)
Async XLA Ops:
  0.6 13.5 %copy-start = (bf16[64,16,1024]{2,1,0:T(8,128)(2,1)S(1)}, bf16[64,16,1024]{2,1,0:T(8,128)(2,1)}, u32[]{:S(2)}) copy-start(bf16[64,16,1024]{2,1,0:T(8,128)(2,1)} %param.11) | copy-start | bytes 6291460
  0.6 85.8 %collective-permute-start = (bf16[512,3584]{1,0:T(8,128)(2,1)}, bf16[512,3584]{1,0:T(8,128)(2,1)}, u32[]{:S(2)}, u32[]{:S(2)}) collective-permute-start(bf16[512,3584]{1,0:T(8,128)(2,1)} %refs_0_.2), channel_id=1, source_target_pairs={{0,4},{4,0},{8,12},{12,8},{1,5},{5,1},{9,13},{13,9},{2,6},{6,2},{1... | collective-permute-start | bytes 11010056 | tf_op jit(solution)/shard_map/ppermute | solution.py:342
  6.6 7.2 %copy-start.13 = (s32[2048]{0:T(1024)S(1)}, s32[2048]{0:T(1024)}, u32[]{:S(2)}) copy-start(s32[2048]{0:T(1024)} %param.13) | copy-start | bytes 24580
  6.6 112.1 %collective-permute-start.3 = (bf16[256,3584]{1,0:T(8,128)(2,1)}, bf16[256,3584]{1,0:T(8,128)(2,1)}, u32[]{:S(2)}, u32[]{:S(2)}) collective-permute-start(bf16[256,3584]{1,0:T(8,128)(2,1)} %constant_dynamic-slice_fusion.7), channel_id=1, source_target_pairs={{4,8},{8,4},{5,9},{9,5},{6,10},{10,6},{7,11},{11,7},{20,24},{24,20... | collective-permute-start | bytes 5505032 | tf_op jit(solution)/shard_map/ppermute | solution.py:341
  8.6 15.3 %copy-start.10 = (s32[64]{0:T(128)S(1)}, s32[64]{0:T(128)}, u32[]{:S(2)}) copy-start(s32[64]{0:T(128)} %param.14) | copy-start | bytes 772
  11.9 106.7 %collective-permute-start.4 = (bf16[256,3584]{1,0:T(8,128)(2,1)}, bf16[256,3584]{1,0:T(8,128)(2,1)}, u32[]{:S(2)}, u32[]{:S(2)}) collective-permute-start(bf16[256,3584]{1,0:T(8,128)(2,1)} %constant_dynamic-slice_fusion.6), channel_id=1, source_target_pairs={{4,8},{8,4},{5,9},{9,5},{6,10},{10,6},{7,11},{11,7},{20,24},{24,20... | collective-permute-start | bytes 5505032 | tf_op jit(solution)/shard_map/ppermute | solution.py:341
  15.3 17.8 %all-to-all-start = ((bf16[4,16,1024]{2,1,0:T(8,128)(2,1)}), bf16[4,16,1024]{2,1,0:T(8,128)(2,1)S(1)}, u32[]{:S(2)}, u32[]{:S(2)}) async-start(bf16[4,16,1024]{2,1,0:T(8,128)(2,1)} %gather_fusion.2), calls=%async_computation | async-start | bytes 262144 | tf_op jit(solution)/shard_map/all_to_all | solution.py:348
  18.7 100.0 %collective-permute-start.5 = (bf16[512,3584]{1,0:T(8,128)(2,1)}, bf16[512,3584]{1,0:T(8,128)(2,1)}, u32[]{:S(2)}, u32[]{:S(2)}) collective-permute-start(bf16[512,3584]{1,0:T(8,128)(2,1)} %refs_0_.2), channel_id=1, source_target_pairs={{0,16},{16,0},{1,17},{17,1},{2,18},{18,2},{3,19},{19,3},{4,20},{20... | collective-permute-start | bytes 11010056 | tf_op jit(solution)/shard_map/ppermute | solution.py:346
  34.3 7.2 %all-to-all-start.1 = ((bf16[4,32,128]{2,1,0:T(8,128)(2,1)}), bf16[4,32,128]{2,1,0:T(8,128)(2,1)S(1)}, u32[]{:S(2)}, u32[]{:S(2)}) async-start(bf16[4,32,128]{2,1,0:T(8,128)(2,1)} %pad_maximum_fusion.4), calls=%async_computation.1 | async-start | bytes 65536 | tf_op jit(solution)/shard_map/all_to_all | solution.py:354
  43.1 7.9 %all-to-all-start.2 = ((bf16[16,4,1024]{2,0,1:T(8,128)(2,1)}), bf16[16,4,1024]{2,0,1:T(8,128)(2,1)S(1)}, u32[]{:S(2)}, u32[]{:S(2)}) async-start(bf16[16,4,1024]{2,0,1:T(8,128)(2,1)} %bitcast.68), calls=%async_computation.2 | async-start | bytes 262144 | tf_op jit(solution)/shard_map/all_to_all | solution.py:371
  51.0 35.4 %collective-permute-start.1 = (bf16[4,16,1152]{2,1,0:T(8,128)(2,1)S(1)}, bf16[4,16,1152]{2,1,0:T(8,128)(2,1)S(1)}, u32[]{:S(2)}, u32[]{:S(2)}) collective-permute-start(bf16[4,16,1152]{2,1,0:T(8,128)(2,1)S(1)} %pad_maximum_fusion.3), channel_id=1, source_target_pairs={{0,4},{4,0},{8,12},{12,8},{1,5},{5,1},{9,13},{13,9},{2,6},{6,2},{1... | collective-permute-start | bytes 442376 | tf_op jit(solution)/shard_map/ppermute | solution.py:377
  86.4 85.0 %collective-permute-start.6 = (bf16[512,3584]{1,0:T(8,128)(2,1)}, bf16[512,3584]{1,0:T(8,128)(2,1)}, u32[]{:S(2)}, u32[]{:S(2)}) collective-permute-start(bf16[512,3584]{1,0:T(8,128)(2,1)} %constant_dynamic-slice_fusion.2), channel_id=1, source_target_pairs={{0,8},{12,4},{1,9},{13,5},{2,10},{14,6},{3,11},{15,7},{16,24},{28,... | collective-permute-start | bytes 11010056 | tf_op jit(solution)/shard_map/ppermute | solution.py:388
  93.1 92.6 %collective-permute-start.11 = (bf16[512,3584]{1,0:T(8,128)(2,1)}, bf16[512,3584]{1,0:T(8,128)(2,1)}, u32[]{:S(2)}, u32[]{:S(2)}) collective-permute-start(bf16[512,3584]{1,0:T(8,128)(2,1)} %collective-permute-done.refs_1_), channel_id=1, source_target_pairs={{0,16},{16,0},{1,17},{17,1},{2,18},{18,2},{3,19},{19,3},{4,20},{20... | collective-permute-start | bytes 11010056 | tf_op jit(solution)/shard_map/ppermute | solution.py:389
  114.2 30.2 %all-to-all-start.3 = ((bf16[4,2,128,1024]{3,2,1,0:T(8,128)(2,1)}), bf16[4,2,128,1024]{3,2,1,0:T(8,128)(2,1)}, u32[]{:S(2)}, u32[]{:S(2)}) async-start(bf16[4,2,128,1024]{3,2,1,0:T(8,128)(2,1)} %shard_map.103), calls=%async_computation.3 | async-start | bytes 4194304 | tf_op jit(solution)/shard_map/all_to_all | solution.py:297
  131.9 16.8 %copy-start.14 = (s32[64]{0:T(128)S(1)}, s32[64]{0:T(128)}, u32[]{:S(2)}) copy-start(s32[64]{0:T(128)} %param.15) | copy-start | bytes 772
  144.4 24.5 %all-to-all-start.4 = ((bf16[4,3,128,512]{3,2,1,0:T(8,128)(2,1)}), bf16[4,3,128,512]{3,2,1,0:T(8,128)(2,1)}, u32[]{:S(2)}, u32[]{:S(2)}) async-start(bf16[4,3,128,512]{3,2,1,0:T(8,128)(2,1)} %copy-done.6), calls=%async_computation.4 | async-start | bytes 3145728 | tf_op jit(solution)/shard_map/all_to_all | solution.py:297
  149.6 34.0 %collective-permute-start.12 = (bf16[4,16,4608]{2,1,0:T(8,128)(2,1)S(1)}, bf16[4,16,4608]{2,1,0:T(8,128)(2,1)}, u32[]{:S(2)}, u32[]{:S(2)}) collective-permute-start(bf16[4,16,4608]{2,1,0:T(8,128)(2,1)S(1)} %pad_maximum_fusion.refs_0_), channel_id=1, source_target_pairs={{4,8},{8,4},{5,9},{9,5},{6,10},{10,6},{7,11},{11,7},{20,24},{24,20... | collective-permute-start | bytes 1769480 | tf_op jit(solution)/shard_map/ppermute | solution.py:399
  153.1 40.7 %collective-permute-start.14 = (bf16[4,16,4608]{2,1,0:T(8,128)(2,1)S(1)}, bf16[4,16,4608]{2,1,0:T(8,128)(2,1)}, u32[]{:S(2)}, u32[]{:S(2)}) collective-permute-start(bf16[4,16,4608]{2,1,0:T(8,128)(2,1)S(1)} %pad_maximum_fusion.1.refs_1_), channel_id=1, source_target_pairs={{4,8},{8,4},{5,9},{9,5},{6,10},{10,6},{7,11},{11,7},{20,24},{24,20... | collective-permute-start | bytes 1769480 | tf_op jit(solution)/shard_map/ppermute | solution.py:400
  155.5 29.4 %collective-permute-start.2 = (bf16[128,1024]{1,0:T(8,128)(2,1)S(1)}, bf16[128,1024]{1,0:T(8,128)(2,1)S(1)}, u32[]{:S(2)}, u32[]{:S(2)}) collective-permute-start(bf16[128,1024]{1,0:T(8,128)(2,1)S(1)} %get-tuple-element.55), channel_id=1, source_target_pairs={{0,4},{4,0},{8,12},{12,8},{1,5},{5,1},{9,13},{13,9},{2,6},{6,2},{1... | collective-permute-start | bytes 786440 | tf_op jit(solution)/shard_map/ppermute | solution.py:401
  183.6 17.7 %collective-permute-start.13 = (bf16[4,16,4608]{2,1,0:T(8,128)(2,1)}, bf16[4,16,4608]{2,1,0:T(8,128)(2,1)S(1)}, u32[]{:S(2)}, u32[]{:S(2)}) collective-permute-start(bf16[4,16,4608]{2,1,0:T(8,128)(2,1)} %collective-permute-done.12.refs_0_), channel_id=1, source_target_pairs={{4,0},{8,12},{5,1},{9,13},{6,2},{10,14},{7,3},{11,15},{20,16},{24,... | collective-permute-start | bytes 1769480 | tf_op jit(solution)/shard_map/ppermute | solution.py:417
  193.8 7.5 %collective-permute-start.15 = (bf16[2,1,128,1024]{3,2,1,0:T(8,128)(2,1)S(1)}, bf16[2,1,128,1024]{3,2,1,0:T(8,128)(2,1)S(1)}, u32[]{:S(2)}, u32[]{:S(2)}) collective-permute-start(bf16[2,1,128,1024]{3,2,1,0:T(8,128)(2,1)S(1)} %get-tuple-element.45), channel_id=1, source_target_pairs={{0,1},{1,0},{2,3},{3,2},{4,5},{5,4},{6,7},{7,6},{8,9},{9,8},{10,11... | collective-permute-start | bytes 1572872 | tf_op jit(solution)/shard_map/ppermute | solution.py:286
  193.9 7.7 %collective-permute-start.7 = (bf16[2,3,128,512]{3,2,1,0:T(8,128)(2,1)S(1)}, bf16[2,3,128,512]{3,2,1,0:T(8,128)(2,1)S(1)}, u32[]{:S(2)}, u32[]{:S(2)}) collective-permute-start(bf16[2,3,128,512]{3,2,1,0:T(8,128)(2,1)S(1)} %get-tuple-element.38), channel_id=1, source_target_pairs={{0,1},{1,0},{2,3},{3,2},{4,5},{5,4},{6,7},{7,6},{8,9},{9,8},{10,11... | collective-permute-start | bytes 2359304 | tf_op jit(solution)/shard_map/ppermute | solution.py:286
  194.4 18.8 %collective-permute-start.17 = (bf16[4,16,4608]{2,1,0:T(8,128)(2,1)}, bf16[4,16,4608]{2,1,0:T(8,128)(2,1)S(1)}, u32[]{:S(2)}, u32[]{:S(2)}) collective-permute-start(bf16[4,16,4608]{2,1,0:T(8,128)(2,1)} %collective-permute-done.14.refs_2_), channel_id=1, source_target_pairs={{4,0},{8,12},{5,1},{9,13},{6,2},{10,14},{7,3},{11,15},{20,16},{24,... | collective-permute-start | bytes 1769480 | tf_op jit(solution)/shard_map/ppermute | solution.py:419
  201.5 9.3 %collective-permute-start.16 = (bf16[1,128,1024]{2,1,0:T(8,128)(2,1)S(1)}, bf16[1,128,1024]{2,1,0:T(8,128)(2,1)S(1)}, u32[]{:S(2)}, u32[]{:S(2)}) collective-permute-start(bf16[1,128,1024]{2,1,0:T(8,128)(2,1)S(1)} %fusion.9), channel_id=1, source_target_pairs={{0,2},{2,0},{1,3},{3,1},{4,6},{6,4},{5,7},{7,5},{8,10},{10,8},{9,1... | collective-permute-start | bytes 786440 | tf_op jit(solution)/shard_map/ppermute | solution.py:292
  201.8 14.5 %copy-start.12 = (bf16[3,128,512]{2,1,0:T(8,128)(2,1)S(1)}, bf16[3,128,512]{2,1,0:T(8,128)(2,1)}, u32[]{:S(2)}) copy-start(bf16[3,128,512]{2,1,0:T(8,128)(2,1)} %reduce_sum.47) | copy-start | bytes 1179652
  201.9 14.3 %collective-permute-start.8 = (bf16[3,128,512]{2,1,0:T(8,128)(2,1)S(1)}, bf16[3,128,512]{2,1,0:T(8,128)(2,1)S(1)}, u32[]{:S(2)}, u32[]{:S(2)}) collective-permute-start(bf16[3,128,512]{2,1,0:T(8,128)(2,1)S(1)} %fusion.7), channel_id=1, source_target_pairs={{0,2},{2,0},{1,3},{3,1},{4,6},{6,4},{5,7},{7,5},{8,10},{10,8},{9,1... | collective-permute-start | bytes 1179656 | tf_op jit(solution)/shard_map/ppermute | solution.py:292
  213.2 12.1 %collective-permute-start.18 = (bf16[128,1024]{1,0:T(8,128)(2,1)S(1)}, bf16[128,1024]{1,0:T(8,128)(2,1)S(1)}, u32[]{:S(2)}, u32[]{:S(2)}) collective-permute-start(bf16[128,1024]{1,0:T(8,128)(2,1)S(1)} %fusion.8), channel_id=1, source_target_pairs={{4,16},{8,28},{20,0},{24,12},{5,17},{9,29},{21,1},{25,13},{6,18},{... | collective-permute-start | bytes 786440 | tf_op jit(solution)/shard_map/ppermute | solution.py:426
  216.5 12.2 %collective-permute-start.9 = (bf16[128,1024]{1,0:T(8,128)(2,1)S(1)}, bf16[128,1024]{1,0:T(8,128)(2,1)S(1)}, u32[]{:S(2)}, u32[]{:S(2)}) collective-permute-start(bf16[128,1024]{1,0:T(8,128)(2,1)S(1)} %get-tuple-element.54), channel_id=1, source_target_pairs={{4,0},{8,12},{5,1},{9,13},{6,2},{10,14},{7,3},{11,15},{20,16},{24,... | collective-permute-start | bytes 786440 | tf_op jit(solution)/shard_map/ppermute | solution.py:424
  217.8 11.4 %collective-permute-start.10 = (bf16[128,1024]{1,0:T(8,128)(2,1)S(1)}, bf16[128,1024]{1,0:T(8,128)(2,1)S(1)}, u32[]{:S(2)}, u32[]{:S(2)}) collective-permute-start(bf16[128,1024]{1,0:T(8,128)(2,1)S(1)} %get-tuple-element.52), channel_id=1, source_target_pairs={{0,16},{16,0},{1,17},{17,1},{2,18},{18,2},{3,19},{19,3},{4,20},{20... | collective-permute-start | bytes 786440 | tf_op jit(solution)/shard_map/ppermute | solution.py:425
  218.0 11.2 %copy-start.7 = (bf16[128,1024]{1,0:T(8,128)(2,1)S(1)}, bf16[128,1024]{1,0:T(8,128)(2,1)}, u32[]{:S(2)}) copy-start(bf16[128,1024]{1,0:T(8,128)(2,1)} %get-tuple-element.56.refs_0_) | copy-start | bytes 786436
  218.0 11.2 %copy-start.9 = (bf16[128,1024]{1,0:T(8,128)(2,1)S(1)}, bf16[128,1024]{1,0:T(8,128)(2,1)}, u32[]{:S(2)}) copy-start(bf16[128,1024]{1,0:T(8,128)(2,1)} %copy-done.8) | copy-start | bytes 786436
  218.0 13.5 %copy-start.1 = (bf16[64,16,1024]{2,1,0:T(8,128)(2,1)S(1)}, bf16[64,16,1024]{2,1,0:T(8,128)(2,1)}, u32[]{:S(2)}) copy-start(bf16[64,16,1024]{2,1,0:T(8,128)(2,1)} %param.11) | copy-start | bytes 6291460
  (7 other events, 17.8 us)
